TPU v7x, 512 devices: a whole 4x8x8 slice. The times are simulated.
512 devices in a mesh: group: 64 (over z, x, core), tp: 8 (over y).
Axes of the slice: x: 4, y: 8, z: 8, core: 2. Of those that a mesh axis runs over, the one named last changes fastest.
Arguments:
- saved: bfloat16 [128, 128, 5120], P('group'), may hold values from -400 to 400
- block_per_slot: int32 [128], P('group'), may hold values from 0 to 127, each once
- lengths: int32 [4], replicated, may hold values from 1 to 4096, 8192 in all
- norm_gain: bfloat16 [5120], replicated, may hold values from 0.099609375 to 1.8984375
- kv_weight: bfloat16 [5120, 2, 5120], P('group', None, 'tp'), may hold values from -0.078125 to 0.078125
- out_weight: bfloat16 [5120, 5120], P('tp', 'group'), may hold values from -0.078125 to 0.078125
- queries: bfloat16 [64, 5120], P('group', 'tp'), may hold values from -400 to 400
- new_kv: bfloat16 [64, 2, 5120], P('group', None, 'tp'), may hold values from -6 to 6
- row_conv: int32 [64], P('group'), may hold values from 0 to 3
Outputs:
- kv_cache: bfloat16 [128, 128, 2, 5120], P('group', None, None, 'tp')
- decoded: bfloat16 [64, 5120], P('tp', 'group')
Inputs may be any that keep to these rules, and one draw needn't show every extreme that they name: `block_per_slot`: every block number 0 to 128 - 1 (conversation c, block b as c * 32 + b) is held by exactly one slot. The lengths sum to 8192; the longest is 4096.
All inputs are finite; a program needn't handle non-finite values.
Results may differ from a plain program's by a relative error of at most 0.019.
Values may be sent and summed in bfloat16 or wider, within the bound.
No kernel may reach another device: no remote copies, remote signals or barrier semaphores. Data moves between devices by JAX's collectives and lax.ppermute only.
A program may use at most 128 MiB of HBM per device.

v0:
```python
import math

import jax
import jax.numpy as jnp
from jax import lax
from jax.sharding import PartitionSpec as P

HEAD_DIM = 128


EPSILON = 1e-05
NEG_FILL = -1e30


def joined(shard, axis, combine):
    everything = jax.tree.map(lambda part: lax.all_gather(part, axis), shard)
    leading = jax.tree.map(lambda part: part[0], everything)

    def hop(k, so_far):
        return combine(so_far, jax.tree.map(lambda part: part[k], everything))

    return lax.fori_loop(1, lax.axis_size(axis), hop, leading)


def rotate(key_heads, positions):
    half_dim = key_heads.shape[-1] // 2
    freq_index = jnp.arange(half_dim, dtype=jnp.float32)
    inverse = jnp.exp(freq_index * (-2.0 * math.log(10000.0) / key_heads.shape[-1]))
    angles = positions.astype(jnp.float32)[..., None] * inverse
    cosine = jnp.cos(angles)[..., None, :]
    sine_part = jnp.sin(angles)[..., None, :]
    first_half = key_heads[..., :half_dim]
    second = key_heads[..., half_dim:]
    return jnp.concatenate(
        [first_half * cosine - second * sine_part, second * cosine + first_half * sine_part],
        axis=-1,
    )


def finish(projected, positions, row_live, kv_width):
    lead_shape = projected.shape[:-1]
    key_heads = projected[..., :kv_width].reshape(lead_shape + (kv_width // HEAD_DIM, HEAD_DIM))
    rotated = rotate(key_heads, positions).reshape(lead_shape + (kv_width,))
    values = projected[..., kv_width:]
    stacked = jnp.stack([rotated, values], axis=-2)
    return jnp.where(row_live[..., None, None], stacked, 0.0).astype(jnp.bfloat16)


def normalize(saved_rows, norm_gain):
    as_float = saved_rows.astype(jnp.float32)
    inv_rms = lax.rsqrt(jnp.mean(as_float * as_float, axis=-1, keepdims=True) + EPSILON)
    return (as_float * inv_rms * norm_gain.astype(jnp.float32)).astype(jnp.bfloat16)


def lookup(lookup_table, indices):
    matches = indices[..., None] == jnp.arange(lookup_table.shape[0], dtype=jnp.int32)
    return jnp.sum(jnp.where(matches, lookup_table, 0), axis=-1)


def combine(first_part, second_part):
    first_top, first_sum, first_mix = first_part
    second_top, second_sum, second_mix = second_part
    merged_top = jnp.maximum(first_top, second_top)
    factor_first = jnp.exp(first_top - merged_top)
    factor_second = jnp.exp(second_top - merged_top)
    head_count = merged_top.shape[-1]
    lead_shape = first_mix.shape[:-1]
    merged_mix = first_mix.reshape(lead_shape + (head_count, -1)) * factor_first[..., None]
    merged_mix = (
        merged_mix + second_mix.reshape(lead_shape + (head_count, -1)) * factor_second[..., None]
    )
    return (
        merged_top,
        first_sum * factor_first + second_sum * factor_second,
        merged_mix.reshape(first_mix.shape),
    )


def per_device(
    saved, block_per_slot, lengths, norm_gain, kv_weight, out_weight, queries, new_kv, row_conv
):
    slot_dev, block_rows, model_width = saved.shape
    groups = lax.axis_size("group")
    conv_count = lengths.shape[0]
    blocks_conv = slot_dev * groups // conv_count
    local_width = kv_weight.shape[2]
    heads_here = local_width // HEAD_DIM
    me_group = lax.axis_index("group")
    row_range = jnp.arange(block_rows, dtype=jnp.int32)
    stack_len = slot_dev * block_rows
    conv_here = block_per_slot // blocks_conv
    start_here = block_per_slot % blocks_conv * block_rows
    length_here = lookup(lengths, conv_here)
    flat_normed = normalize(saved, norm_gain).reshape(stack_len, model_width)
    piece_rows = lax.all_gather(kv_weight, "group", axis=0, tiled=True)
    piece_len = piece_rows.shape[0]
    piece_flat = piece_rows.reshape(piece_len, piece_rows.shape[1] * piece_rows.shape[2])
    projected = jnp.dot(flat_normed, piece_flat, preferred_element_type=jnp.float32)
    projected = projected.reshape(slot_dev, block_rows, 2 * local_width)
    positions = start_here[:, None] + row_range[None, :]
    row_live = positions < length_here[:, None]
    kv_cache = finish(projected, positions, row_live, local_width)
    rows_here = queries.shape[0]
    all_queries, all_convs = (
        lax.all_gather(queries, "group", axis=0, tiled=True),
        lax.all_gather(row_conv, "group", axis=0, tiled=True),
    )
    rows_total = all_queries.shape[0]
    inv_sqrt = 1.0 / math.sqrt(HEAD_DIM)
    query_heads = all_queries.reshape(rows_total, heads_here, HEAD_DIM)
    cache_keys = kv_cache[:, :, 0].reshape(stack_len, heads_here, HEAD_DIM)
    cache_values = kv_cache[:, :, 1].reshape(stack_len, heads_here, HEAD_DIM)
    key_conv = jnp.repeat(conv_here, block_rows)
    key_live = (start_here[:, None] + row_range[None, :] < length_here[:, None]).reshape(-1)
    scores = (
        jnp.einsum("rhd,khd->rhk", query_heads, cache_keys, preferred_element_type=jnp.float32)
        * inv_sqrt
    )
    allowed = ((all_convs[:, None] == key_conv[None, :]) & key_live[None, :])[:, None, :]
    own_key = new_kv[:, 0].reshape(rows_here, heads_here, HEAD_DIM).astype(jnp.float32)
    own_value = new_kv[:, 1].reshape(rows_here, heads_here, HEAD_DIM).astype(jnp.float32)
    own_score = (
        jnp.sum(
            queries.reshape(rows_here, heads_here, HEAD_DIM).astype(jnp.float32) * own_key, axis=-1
        )
        * inv_sqrt
    )
    first_row = me_group * rows_here
    own_full = lax.dynamic_update_slice_in_dim(
        jnp.full((rows_total, heads_here), NEG_FILL, jnp.float32), own_score, first_row, 0
    )
    own_values_full = lax.dynamic_update_slice_in_dim(
        jnp.zeros((rows_total, heads_here, HEAD_DIM), jnp.float32), own_value, first_row, 0
    )
    row_index = jnp.arange(rows_total, dtype=jnp.int32)
    own_rows = (row_index >= first_row) & (row_index < first_row + rows_here)
    row_top = jnp.maximum(jnp.max(jnp.where(allowed, scores, NEG_FILL), axis=-1), own_full)
    attn_weight = jnp.where(allowed, jnp.exp(scores - row_top[..., None]), 0.0).astype(jnp.bfloat16)
    own_weight = jnp.where(own_rows[:, None], jnp.exp(own_full - row_top), 0.0).astype(jnp.bfloat16)
    own_weight = lax.optimization_barrier(own_weight).astype(jnp.float32)
    weight_sum = (
        jnp.sum(lax.optimization_barrier(attn_weight).astype(jnp.float32), axis=-1) + own_weight
    )
    weighted = jnp.einsum(
        "rhk,khd->rhd", attn_weight, cache_values, preferred_element_type=jnp.float32
    )
    weighted = (weighted + own_weight[..., None] * own_values_full).reshape(rows_total, local_width)
    best_top, row_sum, summed = joined((row_top, weight_sum, weighted), "group", combine)
    attended = (
        (summed.reshape(rows_total, heads_here, HEAD_DIM) / row_sum[..., None])
        .reshape(rows_total, local_width)
        .astype(jnp.bfloat16)
    )
    decoded = lax.psum_scatter(
        jnp.dot(attended, out_weight, preferred_element_type=jnp.float32).astype(jnp.bfloat16),
        "tp",
        scatter_dimension=0,
        tiled=True,
    )
    return (kv_cache, decoded)


def solution(mesh):
    placed = (
        P("group", None, None),
        P("group"),
        P(),
        P(),
        P("group", None, "tp"),
        P("tp", "group"),
        P("group", "tp"),
        P("group", None, "tp"),
        P("group"),
    )
    return jax.shard_map(
        per_device,
        mesh=mesh,
        in_specs=placed,
        out_specs=(P("group", None, None, "tp"), P("tp", "group")),
        check_vma=False,
    )
```

profile of v0, /device:TPU:1, one launch (start us, length us, event | category | flops | bytes accessed | tf_op | source)
XLA Modules:
  0.0 374.0 jit_solution(3668397435075359717)
XLA Ops:
  11.0 1.3 dynamic-slice
  12.2 51.3 %all-gather.2 = bf16[64,1,640]{2,1,0:T(2,128)(2,1)S(1)} all-gather(bf16[1,1,640]{2,1,0:T(2,128)(2,1)} %bitcast.104), channel_id=1, replica_groups=mesh['group'=64,'tp'=8] {'group'}, dimensions={0}, use_global_device_ids=true | all-gather | bytes 83200 | tf_op jit(solution)/shard_map/all_gather | solution.py:105
  65.7 14.0 %all-reduce = s32[64]{0:T(128)S(1)} all-reduce(s32[64]{0:T(128)S(1)} %dynamic-update-slice), channel_id=1, replica_groups=mesh['group'=64,'tp'=8] {'group'}, use_global_device_ids=true, to_apply=%add | all-reduce | flops 64 | bytes 512
  81.5 2.4 fusion.3
  84.3 30.2 %all-gather.8.cloned.1.call-done = bf16[5120,2,640]{2,1,0:T(2,128)(2,1)} async-done(((bf16[80,2,640]{2,1,0:T(2,128)(2,1)}), bf16[5120,2,640]{2,1,0:T(2,128)(2,1)}) %all-gather.8.cloned.1.call-update) | async-done | bytes 13107216 | tf_op jit(solution)/shard_map/all_gather | solution.py:95
  114.4 28.7 %reshape.280 = bf16[5120,1280,1]{1,0,2:T(8,128)(2,1)} reshape(bf16[5120,2,640]{2,1,0:T(2,128)(2,1)} %all-gather.8.cloned.1.call-done) | data formatting | bytes 26214400 | tf_op jit(solution)/shard_map/reshape | solution.py:97
  143.1 6.8 %fusion.6 = f32[2,128,1280]{2,1,0:T(8,128)S(1)} fusion(bf16[5120,1280,1]{1,0,2:T(8,128)(2,1)} %reshape.280, bf16[2,128,5120]{2,1,0:T(8,128)(2,1)S(1)} %copy-done.1, f32[5120]{0:T(1024)S(1)} %convert_element_type.86, f32[2,128]{1,0:T(2,128)S(1)} %add_rsqrt_fusion), kind=kOutput, calls=%fused_computation.16 | convolution fusion | flops 3360686080 | bytes 17060864 | tf_op jit(solution)/shard_map/dot_general | solution.py:98
  153.2 1.3 dynamic-slice.1
  155.1 1.5 copy.56
  156.6 42.6 %all-gather.3 = f32[64,64,5]{1,2,0:T(8,128)S(1)} all-gather(f32[1,64,5]{1,2,0:T(8,128)S(1)} %bitcast.103), channel_id=2, replica_groups=mesh['group'=64,'tp'=8] {'group'}, dimensions={0}, use_global_device_ids=true | all-gather | bytes 83200 | tf_op jit(solution)/shard_map/all_gather | solution.py:16
  199.5 42.7 %all-gather.4 = f32[64,64,5]{1,2,0:T(8,128)S(1)} all-gather(f32[1,64,5]{1,2,0:T(8,128)S(1)} %add_bitcast_fusion), channel_id=3, replica_groups=mesh['group'=64,'tp'=8] {'group'}, dimensions={0}, use_global_device_ids=true | all-gather | bytes 83200 | tf_op jit(solution)/shard_map/all_gather | solution.py:16
  243.5 99.9 %while.19 = (s32[]{:T(128)}, f32[64,5]{1,0:T(8,128)S(1)}, f32[64,5]{1,0:T(8,128)S(1)}, f32[64,640]{1,0:T(8,128)S(1)}, f32[64,64,5]{1,2,0:T(8,128)S(1)}, /*index=...) while((s32[]{:T(128)}, f32[64,5]{1,0:T(8,128)S(1)}, ...), condition=%wide.region_6.7_spmd, body=%wide.region_5.6_spmd.sunk | while | flops 124805 | bytes 1170071 | solution.py:22
  244.0 1.1 fusion.34
  245.6 1.1 fusion.34
  247.2 1.1 fusion.34
  248.8 1.1 fusion.34
  250.4 1.1 fusion.34
  251.9 1.1 fusion.34
  253.5 1.1 fusion.34
  255.1 1.1 fusion.34
  256.7 1.1 fusion.34
  258.3 1.1 fusion.34
  259.9 1.1 fusion.34
  343.7 22.9 %all-reduce.1 = bf16[64,80]{1,0:T(8,128)(2,1)S(1)} all-reduce(bf16[64,80]{1,0:T(8,128)(2,1)S(1)} %convolution_convert_fusion), channel_id=4, replica_groups=mesh['group'=64,'tp'=8] {'tp'}, use_global_device_ids=true, to_apply=%region_7.8.clone | all-reduce | flops 5120 | bytes 20480
  (491 shorter events, 98.3 us)
Async XLA Ops:
  7.2 336.3 %copy-start = (bf16[640,80]{0,1:T(8,128)(2,1)S(1)}, bf16[640,80]{0,1:T(8,128)(2,1)}, u32[]{:S(2)}) copy-start(bf16[640,80]{0,1:T(8,128)(2,1)} %param.16) | copy-start | bytes 307204
  7.2 107.3 %all-gather.8.cloned.1.call-start = ((), (), s32[]{:S(2)}) async-start(), calls=%async_computation | async-start | bytes 13312000 | tf_op jit(solution)/shard_map/all_gather | solution.py:95
  7.9 234.6 %all-gather.10.cloned.1.call-start = ((), (), s32[]{:S(2)}) async-start(), calls=%async_computation.1 | async-start | bytes 10649600 | tf_op jit(solution)/shard_map/all_gather | solution.py:16
  84.3 58.9 %copy-start.1 = (bf16[2,128,5120]{2,1,0:T(8,128)(2,1)S(1)}, bf16[2,128,5120]{2,1,0:T(8,128)(2,1)}, u32[]{:S(2)}) copy-start(bf16[2,128,5120]{2,1,0:T(8,128)(2,1)} %param.11) | copy-start | bytes 7864324
Sparse Core Ops, SparseCore 0:
  11.3 103.0 all-gather.7
  153.3 89.1 all-gather.9
where the time goes:
time: 381 us; the launch traced here: 374 us
  blocking collectives  173 us (45%)
  other arithmetic  77.1 us (20%)
  local copies, waits for them, and re-layouts  66.1 us (17%)
  waiting for transfers between devices  31.2 us (8%)
  between operations  15.6 us (4%)
  matrix products  7.5 us (2%)
    all_gather x2, blocking collectives, joined(): everything = jax.tree.map(lambda part: lax.all_gather(part, axis), shard)  85.3 us
    add x63, other arithmetic, combine(): merged_mix + second_mix.reshape(lead_shape + (head_count, -1)) * factor_s...  66.2 us
    all_gather x1, blocking collectives, per_device(): lax.all_gather(queries, 'group', axis=0, tiled=True)  51.3 us
    unnamed x2, blocking collectives  36.8 us
    all_gather x1, waiting for transfers between devices, per_device(): piece_rows = lax.all_gather(kv_weight, 'group', axis=0, tiled=True)  30.2 us
    reshape x1, local copies, waits for them, and re-layouts, per_device(): piece_rows.reshape(piece_len, piece_rows.shape[1] * piece_rows.shape[2])  28.7 us
    dynamic_slice x189, local copies, waits for them, and re-layouts, hop(): return combine(so_far, jax.tree.map(lambda part: part[k], everything))  12.6 us
    mul x63, local copies, waits for them, and re-layouts, combine(): first_mix.reshape(lead_shape + (head_count, -1)) * factor_first[..., None]  7.99 us
  transfers between devices with their start and end apart: 2, of which 2 were waited for; matrix products, arithmetic and copies ran while one was open for 4% of the time, Pallas kernels for 0%

commit v1 on v0

v1 whole, which is shorter than its diff:
```python
import functools
import math

import jax
import jax.numpy as jnp
from jax import lax
from jax.experimental import pallas as pl
from jax.experimental.pallas import tpu as pltpu
from jax.sharding import Mesh
from jax.sharding import PartitionSpec as P

HEAD_DIM = 128
EPSILON = 1e-05
NEG_FILL = -1e30
GROUP = ("z", "x", "core")
MIB = 1 << 20
Z_CHIPS, X_CHIPS = 8, 4
Z_RING, X_RING = (0, -1, 1, -2, 2, -3, 3, 4), (0, -1, 1, 2)
TOP_PARTS, SUM_PARTS = 3, 2


def normalize(saved_rows, norm_gain):
    as_float = saved_rows.astype(jnp.float32)
    inv_rms = lax.rsqrt(jnp.mean(as_float * as_float, axis=-1, keepdims=True) + EPSILON)
    return (as_float * inv_rms * norm_gain.astype(jnp.float32)).astype(jnp.bfloat16)


def lookup(lookup_table, indices):
    matches = indices[..., None] == jnp.arange(lookup_table.shape[0], dtype=jnp.int32)
    return jnp.sum(jnp.where(matches, lookup_table, 0), axis=-1)


def swap_cores(value):
    return lax.ppermute(value, "core", [(0, 1), (1, 0)])


def chip_of(place_ref, dz, dx):
    sign = 1 - 2 * place_ref[2]
    z = lax.rem(place_ref[0] + sign * dz + Z_CHIPS, Z_CHIPS)
    x = lax.rem(place_ref[1] + sign * dx + X_CHIPS, X_CHIPS)
    return z * X_CHIPS + x


def project_kernel(split, place_ref, own_ref, other_ref, cos_ref, sin_ref, *refs):
    a_refs, b_refs = refs[: len(X_RING)], refs[len(X_RING) : len(X_RING) + len(Z_RING)]
    own_out, other_out, query_out, weight = refs[len(X_RING) + len(Z_RING) :]
    core = place_ref[2]
    rows, depth = own_ref.shape
    width = weight.shape[1]
    half = depth // (2 * Z_CHIPS * X_CHIPS)
    extra = a_refs[0].shape[0] // len(Z_RING) - 2 * half

    def place(piece, at, chip, columns):
        for part, whose in ((0, core), (1, 1 - core)):
            to = pl.multiple_of((2 * chip + whose) * half, 16)
            weight[pl.ds(to, half), columns] = piece[pl.ds(at + part * half, half), :]

    for i, dx in enumerate(X_RING):
        for j, dz in enumerate(Z_RING):
            chip = chip_of(place_ref, dz, dx)
            at = j * (2 * half + extra)
            place(a_refs[i], at, chip, pl.ds(0, split))
            tiles = a_refs[i][pl.ds(at + 2 * half, extra), :].astype(jnp.float32)
            query_out[chip, pl.ds(pl.multiple_of(core * 8, 8), 8), :] = tiles[:8]
            query_out[chip, pl.ds(pl.multiple_of(8 - core * 8, 8), 8), :] = tiles[8:16]
            place(b_refs[j], i * 2 * half, chip, pl.ds(split, width - split))

    chunk = 1024 if depth % 1024 == 0 else depth
    for part, (rows_ref, out) in enumerate(((own_ref, own_out), (other_ref, other_out))):
        span = pl.ds(part * rows, rows)
        total = jnp.zeros((rows, width), jnp.float32)
        for k in range(depth // chunk):
            lanes = pl.ds(k * chunk, chunk)
            total += jnp.dot(
                rows_ref[:, lanes], weight[lanes, :], preferred_element_type=jnp.float32
            )
        cosine, sine = cos_ref[span, :], sin_ref[span, :]
        for head in range(width // HEAD_DIM):
            value = total[:, head * HEAD_DIM : (head + 1) * HEAD_DIM]
            turned = value * cosine + pltpu.roll(value, HEAD_DIM // 2, 1) * sine
            out[:, pl.ds(head * HEAD_DIM, HEAD_DIM)] = turned.astype(out.dtype)


def project(place, own, other, cosine, sine, a_blocks, b_blocks):
    rows, depth = own.shape
    split = a_blocks[0].shape[1]
    width = split + b_blocks[0].shape[1]
    out = jax.ShapeDtypeStruct((rows, width), jnp.bfloat16)
    tiles = jax.ShapeDtypeStruct((Z_CHIPS * X_CHIPS, 16, split), jnp.float32)
    vmem = pl.BlockSpec(memory_space=pltpu.VMEM)
    operands = (own, other, cosine, sine, *a_blocks, *b_blocks)
    return pl.pallas_call(
        functools.partial(project_kernel, split),
        in_specs=[pl.BlockSpec(memory_space=pltpu.SMEM)] + [vmem] * len(operands),
        out_specs=[vmem] * 3,
        out_shape=[out, out, tiles],
        scratch_shapes=[pltpu.VMEM((depth, width), jnp.bfloat16)],
        compiler_params=pltpu.CompilerParams(vmem_limit_bytes=40 * MIB),
        cost_estimate=pl.CostEstimate(
            flops=4 * rows * depth * width,
            bytes_accessed=4 * rows * depth + 2 * depth * width,
            transcendentals=0,
        ),
    )(place, *operands)


def attend_kernel(place_ref, mine_ref, theirs_ref, query_ref, keys_ref, out_ref, tiles):
    has_keys = place_ref[2] == 0
    chips = query_ref.shape[0]
    heads = mine_ref.shape[1] // HEAD_DIM
    key_conv = keys_ref[0:1, :]

    def rows_of(part):
        lanes = pl.ds(part % 2 * HEAD_DIM, HEAD_DIM)
        return jnp.concatenate([query_ref[:, core * 8 + part // 2, lanes] for core in (0, 1)])

    allowed = rows_of(heads)[:, 0:1] == key_conv
    lane = lax.broadcasted_iota(jnp.int32, (2 * chips, HEAD_DIM), 1)
    stats = jnp.zeros(lane.shape, jnp.float32)

    def put(row, value):
        for core in (0, 1):
            tiles[:, core, row, :] = value[core * chips : (core + 1) * chips]

    for head in range(heads):
        lanes = pl.ds(head * HEAD_DIM, HEAD_DIM)
        mine, theirs = mine_ref[:, lanes], theirs_ref[:, lanes]
        keys = jnp.where(has_keys, mine, theirs)
        values = jnp.where(has_keys, theirs, mine)
        scores = lax.dot_general(
            rows_of(head).astype(jnp.bfloat16),
            keys,
            (((1,), (1,)), ((), ())),
            preferred_element_type=jnp.float32,
        )
        scores = jnp.where(allowed, scores * (1.0 / math.sqrt(HEAD_DIM)), NEG_FILL)
        top = jnp.max(scores, axis=-1, keepdims=True)
        weight = jnp.where(allowed, jnp.exp(scores - top), 0.0).astype(jnp.bfloat16)
        total = jnp.sum(weight.astype(jnp.float32), axis=-1, keepdims=True)
        put(head, jnp.dot(weight, values, preferred_element_type=jnp.float32))
        at = head
        for value, parts in ((top, TOP_PARTS), (total, SUM_PARTS)):
            for _ in range(parts):
                rounded = value.astype(jnp.bfloat16).astype(jnp.float32)
                stats = jnp.where(lane == at, rounded, stats)
                value = value - rounded
                at += 8
    put(heads, stats)
    for row in range(heads + 1, 8):
        put(row, jnp.zeros_like(stats))
    out_ref[...] = tiles[...].astype(jnp.bfloat16)


def attend(place, mine, theirs, queries, key_conv):
    shape = (queries.shape[0], 2, 8, HEAD_DIM)
    vmem = pl.BlockSpec(memory_space=pltpu.VMEM)
    return pl.pallas_call(
        attend_kernel,
        in_specs=[pl.BlockSpec(memory_space=pltpu.SMEM)] + [vmem] * 4,
        out_specs=vmem,
        out_shape=jax.ShapeDtypeStruct(shape, jnp.bfloat16),
        scratch_shapes=[pltpu.VMEM(shape, jnp.float32)],
        compiler_params=pltpu.CompilerParams(vmem_limit_bytes=16 * MIB),
    )(place, mine, theirs, queries, key_conv)


def merge_kernel(heads, parts_ref, query_ref, new_ref, out_ref, parts, tile):
    parts[...] = parts_ref[...].astype(jnp.float32)
    stats = parts[:, heads, :]
    tile[...] = jnp.zeros_like(tile)
    for head in range(heads):
        lanes = pl.ds(head * HEAD_DIM, HEAD_DIM)
        query = query_ref[:, lanes].astype(jnp.float32)
        own_key = new_ref[0:1, lanes].astype(jnp.float32)
        own_value = new_ref[1:2, lanes].astype(jnp.float32)
        own = jnp.sum(query * own_key, axis=-1, keepdims=True) * (1.0 / math.sqrt(HEAD_DIM))
        stat = [stats[:, head + 8 * k : head + 8 * k + 1] for k in range(TOP_PARTS + SUM_PARTS)]
        top, total = sum(stat[1:TOP_PARTS], stat[0]), sum(stat[TOP_PARTS + 1 :], stat[TOP_PARTS])
        best = jnp.maximum(jnp.max(top, axis=0, keepdims=True), own)
        factor = jnp.exp(top - best)
        own_weight = jnp.exp(own - best).astype(jnp.bfloat16).astype(jnp.float32)
        total = jnp.sum(total * factor, axis=0, keepdims=True) + own_weight
        mixed = jnp.sum(parts[:, head, :] * factor, axis=0, keepdims=True)
        tile[head : head + 1, :] = (mixed + own_weight * own_value) / total
    out_ref[...] = jnp.broadcast_to(tile[...].astype(jnp.bfloat16), out_ref.shape)


def merge(parts, query, new_pair):
    vmem = pl.BlockSpec(memory_space=pltpu.VMEM)
    return pl.pallas_call(
        functools.partial(merge_kernel, query.shape[1] // HEAD_DIM),
        in_specs=[vmem] * 3,
        out_specs=vmem,
        out_shape=jax.ShapeDtypeStruct(parts.shape, jnp.bfloat16),
        scratch_shapes=[
            pltpu.VMEM(parts.shape, jnp.float32),
            pltpu.VMEM(parts.shape[1:], jnp.float32),
        ],
        compiler_params=pltpu.CompilerParams(vmem_limit_bytes=16 * MIB),
    )(parts, query, new_pair)


def send(value, dz, dx):
    pairs = []
    for z in range(Z_CHIPS):
        for x in range(X_CHIPS):
            for core, sign in ((0, 1), (1, -1)):
                to = ((z + sign * dz) % Z_CHIPS * X_CHIPS + (x + sign * dx) % X_CHIPS) * 2 + core
                pairs.append(((z * X_CHIPS + x) * 2 + core, to))
    return lax.ppermute(value, GROUP, pairs)


def ring(value, chips, dz, dx):
    behind, ahead, found = value, value, [value]
    for _ in range(chips // 2 - 1):
        behind, ahead = send(behind, dz, dx), send(ahead, -dz, -dx)
        found += [behind, ahead]
    return found + [send(behind, dz, dx)]


def exchange(value, axis):
    return lax.all_to_all(value, axis, 0, 0, tiled=True)


def per_device(
    saved, block_per_slot, lengths, norm_gain, kv_weight, out_weight, queries, new_kv, row_conv
):
    slot_dev, block_rows, model_width = saved.shape
    groups = lax.axis_size(GROUP)
    blocks_conv = slot_dev * groups // lengths.shape[0]
    local_width = kv_weight.shape[2]
    heads = local_width // HEAD_DIM
    core = lax.axis_index("core")
    first_core = core == 0

    split = 2 * HEAD_DIM
    keep = jnp.where(first_core, kv_weight[:, 0], kv_weight[:, 1])
    give = jnp.where(first_core, kv_weight[:, 1], kv_weight[:, 0])
    notes = jnp.concatenate(
        [
            queries.reshape(-1),
            jnp.broadcast_to(row_conv.astype(jnp.bfloat16), (HEAD_DIM,)),
            block_per_slot.astype(jnp.bfloat16),
        ]
    )
    notes = jnp.pad(notes, (0, 8 * split - notes.shape[0])).reshape(8, split)
    sent = jnp.concatenate([give, jnp.pad(notes, ((0, 8), (0, local_width - split)))])
    got = swap_cores(sent)
    part_rows = keep.shape[0]
    got_notes = got[part_rows : part_rows + 8, :split]
    piece_a = jnp.concatenate([keep[:, :split], got[:part_rows, :split], notes, got_notes])
    piece_b = jnp.concatenate([keep[:, split:], got[:part_rows, split:]])
    block_b = jnp.concatenate(
        [piece_b, send(piece_b, 0, 1), send(piece_b, 0, -1), send(piece_b, 0, 2)]
    )
    block_a = jnp.concatenate(ring(piece_a, Z_CHIPS, 1, 0))
    b_blocks = ring(block_b, Z_CHIPS, 1, 0)
    a_blocks = ring(block_a, X_CHIPS, 0, 1)

    normed = normalize(saved, norm_gain).reshape(slot_dev * block_rows, model_width)
    other_normed = swap_cores(normed)
    flat = local_width + HEAD_DIM
    other_blocks = got_notes[flat // split, flat % split : flat % split + slot_dev]
    blocks = jnp.concatenate([block_per_slot, other_blocks.astype(jnp.int32)])
    conv = blocks // blocks_conv
    positions = (blocks % blocks_conv * block_rows)[:, None] + jnp.arange(
        block_rows, dtype=jnp.int32
    )
    live = (positions < lookup(lengths, conv)[:, None]).reshape(-1, 1)
    half_dim = HEAD_DIM // 2
    freq_index = jnp.arange(half_dim, dtype=jnp.float32)
    inverse = jnp.exp(freq_index * (-2.0 * math.log(10000.0) / HEAD_DIM))
    angles = positions.reshape(-1, 1).astype(jnp.float32) * inverse
    cosine, sine = jnp.cos(angles), jnp.sin(angles)
    cosine = jnp.where(first_core, jnp.concatenate([cosine, cosine], axis=-1), 1.0)
    sine = jnp.where(first_core, jnp.concatenate([-sine, sine], axis=-1), 0.0)
    cosine, sine = jnp.where(live, cosine, 0.0), jnp.where(live, sine, 0.0)
    own_rows = slot_dev * block_rows
    key_conv = jnp.where(live[:own_rows, 0], jnp.repeat(conv[:slot_dev], block_rows), -1)
    key_conv = jnp.broadcast_to(key_conv.astype(jnp.float32), (8, own_rows))
    place = jnp.stack([lax.axis_index("z"), lax.axis_index("x"), core]).astype(jnp.int32)

    mine, for_other, tiles = project(
        place, normed, other_normed, cosine, sine, a_blocks, b_blocks
    )
    theirs = swap_cores(for_other)
    parts = attend(place, mine, theirs, tiles, key_conv).reshape(groups, 8, HEAD_DIM)
    merged = merge(exchange(parts, GROUP), queries, new_kv[0])
    attended = exchange(merged, GROUP)[:, :heads].reshape(groups, local_width)
    decoded = jnp.dot(attended, out_weight, preferred_element_type=jnp.float32)
    tp = lax.axis_size("tp")
    decoded = exchange(decoded.reshape(tp, groups // tp, -1), "tp")
    decoded = jnp.sum(decoded, axis=0).astype(jnp.bfloat16)

    keys = jnp.where(first_core, mine, theirs)
    values = jnp.where(first_core, theirs, mine)
    kv_cache = jnp.stack([keys, values], axis=1).reshape(slot_dev, block_rows, 2, local_width)
    return (kv_cache, decoded)


def solution(mesh):
    groups, tp = mesh.devices.shape
    fine = Mesh(
        mesh.devices.reshape(Z_CHIPS, X_CHIPS, groups // (Z_CHIPS * X_CHIPS), tp), GROUP + ("tp",)
    )
    placed = (
        P(GROUP, None, None),
        P(GROUP),
        P(),
        P(),
        P(GROUP, None, "tp"),
        P("tp", GROUP),
        P(GROUP, "tp"),
        P(GROUP, None, "tp"),
        P(GROUP),
    )
    return jax.shard_map(
        per_device,
        mesh=fine,
        in_specs=placed,
        out_specs=(P(GROUP, None, None, "tp"), P("tp", GROUP)),
        check_vma=False,
    )
```

time: 381 us -> 179 us (0.47); the launches traced: 374 us -> 177 us
  blocking collectives: 173 us -> 23.6 us
  starting transfers between devices: 0.08 us -> 92.5 us
  other arithmetic: 77.1 us -> 12.2 us
  local copies, waits for them, and re-layouts: 66.1 us -> 9.33 us
  between operations: 15.6 us -> 1.82 us
  Pallas kernels: 0 us -> 9.86 us
  matrix products: 7.5 us -> 0.77 us
    all_gather x3 -> x0, blocking collectives: 137 us -> none  [the longest x2 85.3 us: joined(): everything = jax.tree.map(lambda part: lax.all_gather(part, axis), shard)]
    ppermute x0 -> x23, starting transfers between devices: none -> 81.2 us  [the longest x20 65.9 us: send(): return lax.ppermute(value, GROUP, pairs)]
    add x126 -> x0, other arithmetic: 68.7 us -> none  [the longest x63 66.2 us: combine(): merged_mix + second_mix.reshape(lead_shape + (head_count, -1)) * factor_s...]
    unnamed x2 -> x0, blocking collectives: 36.8 us -> none
    all_gather x2 -> x0, waiting for transfers between devices: 30.5 us -> none  [the longest x1 30.2 us: per_device(): piece_rows = lax.all_gather(kv_weight, 'group', axis=0, tiled=True)]
    reshape x1, local copies, waits for them, and re-layouts: 28.7 us -> 0.01 us  [per_device(): notes = jnp.pad(notes, (0, 8 * split - notes.shape[0])).reshape(8, split)]
    all_to_all x0 -> x1, blocking collectives: none -> 23.6 us  [exchange(): return lax.all_to_all(value, axis, 0, 0, tiled=True)]
    mul x127 -> x0, local copies, waits for them, and re-layouts: 15.7 us -> none  [the longest x63 7.99 us: combine(): first_mix.reshape(lead_shape + (head_count, -1)) * factor_first[..., None]]
  transfers between devices with their start and end apart: 2 -> 25, of which waited for: 2 -> 8; matrix products, arithmetic and copies ran while one was open for 4% -> 9% of each run, Pallas kernels for 0% -> 0%
where the time goes in v1:
time: 179 us; the launch traced here: 177 us
  starting transfers between devices  92.5 us (52%)
  waiting for transfers between devices  27.4 us (15%)
  blocking collectives  23.6 us (13%)
  other arithmetic  12.2 us (7%)
  Pallas kernels  9.86 us (6%)
  local copies, waits for them, and re-layouts  9.33 us (5%)
  between operations  1.82 us (1%)
    ppermute x20, starting transfers between devices, send(): return lax.ppermute(value, GROUP, pairs)  65.9 us
    all_to_all x1, blocking collectives, exchange(): return lax.all_to_all(value, axis, 0, 0, tiled=True)  23.6 us
    ppermute x3, starting transfers between devices, swap_cores(): return lax.ppermute(value, 'core', [(0, 1), (1, 0)])  15.3 us
    all_to_all x2, waiting for transfers between devices, exchange(): return lax.all_to_all(value, axis, 0, 0, tiled=True)  14.9 us
    ppermute x20, waiting for transfers between devices, send(): return lax.ppermute(value, GROUP, pairs)  11.4 us
    all_to_all x2, starting transfers between devices, exchange(): return lax.all_to_all(value, axis, 0, 0, tiled=True)  11.3 us
    pallas_call x1, Pallas kernels, project(): pl.pallas_call(functools.partial(project_kernel, split), in_specs=[pl.Blo...  6.74 us
  transfers between devices with their start and end apart: 25, of which 8 were waited for; matrix products, arithmetic and copies ran while one was open for 9% of the time, Pallas kernels for 0%

profile of v1, /device:TPU:1, one launch (start us, length us, event | category | flops | bytes accessed | tf_op | source)
XLA Modules:
  0.0 177.4 jit_solution(10047554105291298669)
XLA Ops:
  4.9 8.9 %collective-permute-start.1 = (bf16[96,640]{1,0:T(8,128)(2,1)}, bf16[96,640]{1,0:T(8,128)(2,1)}, u32[]{:S(2)}, u32[]{:S(2)}) collective-permute-start(bf16[96,640]{1,0:T(8,128)(2,1)} %fusion.6), channel_id=1, source_target_pairs={{0,8},{8,0},{1,9},{9,1},{2,10},{10,2},{3,11},{11,3},{4,12},{12,4},... | collective-permute-start | bytes 368648 | tf_op jit(solution)/shard_map/ppermute | solution.py:34
  23.6 3.4 %collective-permute-start.13 = (bf16[160,384]{1,0:T(8,128)(2,1)S(1)}, bf16[160,384]{1,0:T(8,128)(2,1)S(1)}, u32[]{:S(2)}, u32[]{:S(2)}) collective-permute-start(bf16[160,384]{1,0:T(8,128)(2,1)S(1)} %pad_maximum_fusion.1), channel_id=1, source_target_pairs={{0,48},{8,24},{16,0},{24,40},{32,16},{40,56},{48,32},{56,8},{64,11... | collective-permute-start | bytes 368648 | tf_op jit(solution)/shard_map/ppermute | solution.py:210
  28.5 6.3 %collective-permute-start.2 = (bf16[176,256]{1,0:T(8,128)(2,1)S(1)}, bf16[176,256]{1,0:T(8,128)(2,1)S(1)}, u32[]{:S(2)}, u32[]{:S(2)}) collective-permute-start(bf16[176,256]{1,0:T(8,128)(2,1)S(1)} %pad_maximum_fusion.2), channel_id=1, source_target_pairs={{0,64},{8,456},{16,80},{24,472},{32,96},{40,488},{48,112},{56,504}... | collective-permute-start | bytes 270344 | tf_op jit(solution)/shard_map/ppermute | solution.py:210
  36.8 3.6 %collective-permute-start.14 = (bf16[160,384]{1,0:T(8,128)(2,1)S(1)}, bf16[160,384]{1,0:T(8,128)(2,1)S(1)}, u32[]{:S(2)}, u32[]{:S(2)}) collective-permute-start(bf16[160,384]{1,0:T(8,128)(2,1)S(1)} %pad_maximum_fusion.1), channel_id=1, source_target_pairs={{0,32},{8,40},{16,48},{24,56},{32,0},{40,8},{48,16},{56,24},{64,96... | collective-permute-start | bytes 368648 | tf_op jit(solution)/shard_map/ppermute | solution.py:210
  40.5 4.6 %collective-permute-start.4 = (bf16[176,256]{1,0:T(8,128)(2,1)S(1)}, bf16[176,256]{1,0:T(8,128)(2,1)S(1)}, u32[]{:S(2)}, u32[]{:S(2)}) collective-permute-start(bf16[176,256]{1,0:T(8,128)(2,1)S(1)} %collective-permute-done.2), channel_id=1, source_target_pairs={{0,64},{8,456},{16,80},{24,472},{32,96},{40,488},{48,112},{56,504}... | collective-permute-start | bytes 270344 | tf_op jit(solution)/shard_map/ppermute | solution.py:210
  49.3 3.1 %collective-permute-start.5 = (bf16[176,256]{1,0:T(8,128)(2,1)S(1)}, bf16[176,256]{1,0:T(8,128)(2,1)S(1)}, u32[]{:S(2)}, u32[]{:S(2)}) collective-permute-start(bf16[176,256]{1,0:T(8,128)(2,1)S(1)} %collective-permute-done.3), channel_id=1, source_target_pairs={{0,448},{8,72},{16,464},{24,88},{32,480},{40,104},{48,496},{56,120... | collective-permute-start | bytes 270344 | tf_op jit(solution)/shard_map/ppermute | solution.py:210
  54.4 4.6 %collective-permute-start.6 = (bf16[176,256]{1,0:T(8,128)(2,1)S(1)}, bf16[176,256]{1,0:T(8,128)(2,1)S(1)}, u32[]{:S(2)}, u32[]{:S(2)}) collective-permute-start(bf16[176,256]{1,0:T(8,128)(2,1)S(1)} %collective-permute-done.4), channel_id=1, source_target_pairs={{0,64},{8,456},{16,80},{24,472},{32,96},{40,488},{48,112},{56,504}... | collective-permute-start | bytes 270344 | tf_op jit(solution)/shard_map/ppermute | solution.py:210
  61.4 5.3 %collective-permute-start.8 = (bf16[176,256]{1,0:T(8,128)(2,1)S(1)}, bf16[176,256]{1,0:T(8,128)(2,1)S(1)}, u32[]{:S(2)}, u32[]{:S(2)}) collective-permute-start(bf16[176,256]{1,0:T(8,128)(2,1)S(1)} %collective-permute-done.6), channel_id=1, source_target_pairs={{0,64},{8,456},{16,80},{24,472},{32,96},{40,488},{48,112},{56,504}... | collective-permute-start | bytes 270344 | tf_op jit(solution)/shard_map/ppermute | solution.py:210
  68.7 5.2 %collective-permute-start.9 = (bf16[1408,256]{1,0:T(8,128)(2,1)S(1)}, bf16[1408,256]{1,0:T(8,128)(2,1)S(1)}, u32[]{:S(2)}, u32[]{:S(2)}) collective-permute-start(bf16[1408,256]{1,0:T(8,128)(2,1)S(1)} %constant_dynamic-update-slice_fusion.refs_0_), channel_id=1, source_target_pairs={{0,16},{8,56},{16,32},{24,8},{32,48},{40,24},{48,0},{56,40},{64,80... | collective-permute-start | bytes 2162696 | tf_op jit(solution)/shard_map/ppermute | solution.py:210
  74.7 3.1 %collective-permute-start.18 = (bf16[640,384]{1,0:T(8,128)(2,1)S(1)}, bf16[640,384]{1,0:T(8,128)(2,1)S(1)}, u32[]{:S(2)}, u32[]{:S(2)}) collective-permute-start(bf16[640,384]{1,0:T(8,128)(2,1)S(1)} %collective-permute-done.16.refs_6_), channel_id=1, source_target_pairs={{0,448},{8,72},{16,464},{24,88},{32,480},{40,104},{48,496},{56,120... | collective-permute-start | bytes 1474568 | tf_op jit(solution)/shard_map/ppermute | solution.py:210
  77.8 3.4 %collective-permute-start.19 = (bf16[640,384]{1,0:T(8,128)(2,1)S(1)}, bf16[640,384]{1,0:T(8,128)(2,1)S(1)}, u32[]{:S(2)}, u32[]{:S(2)}) collective-permute-start(bf16[640,384]{1,0:T(8,128)(2,1)S(1)} %collective-permute-done.17.refs_7_), channel_id=1, source_target_pairs={{0,64},{8,456},{16,80},{24,472},{32,96},{40,488},{48,112},{56,504}... | collective-permute-start | bytes 1474568 | tf_op jit(solution)/shard_map/ppermute | solution.py:210
  83.2 4.6 %collective-permute-start.11 = (bf16[1408,256]{1,0:T(8,128)(2,1)S(1)}, bf16[1408,256]{1,0:T(8,128)(2,1)S(1)}, u32[]{:S(2)}, u32[]{:S(2)}) collective-permute-start(bf16[1408,256]{1,0:T(8,128)(2,1)S(1)} %collective-permute-done.9.refs_1_), channel_id=1, source_target_pairs={{0,16},{8,56},{16,32},{24,8},{32,48},{40,24},{48,0},{56,40},{64,80... | collective-permute-start | bytes 2162696 | tf_op jit(solution)/shard_map/ppermute | solution.py:210
  88.6 2.5 %collective-permute-start.20 = (bf16[640,384]{1,0:T(8,128)(2,1)S(1)}, bf16[640,384]{1,0:T(8,128)(2,1)S(1)}, u32[]{:S(2)}, u32[]{:S(2)}) collective-permute-start(bf16[640,384]{1,0:T(8,128)(2,1)S(1)} %collective-permute-done.18.refs_8_), channel_id=1, source_target_pairs={{0,448},{8,72},{16,464},{24,88},{32,480},{40,104},{48,496},{56,120... | collective-permute-start | bytes 1474568 | tf_op jit(solution)/shard_map/ppermute | solution.py:210
  92.8 2.5 %collective-permute-start.21 = (bf16[640,384]{1,0:T(8,128)(2,1)S(1)}, bf16[640,384]{1,0:T(8,128)(2,1)S(1)}, u32[]{:S(2)}, u32[]{:S(2)}) collective-permute-start(bf16[640,384]{1,0:T(8,128)(2,1)S(1)} %collective-permute-done.19.refs_9_), channel_id=1, source_target_pairs={{0,64},{8,456},{16,80},{24,472},{32,96},{40,488},{48,112},{56,504}... | collective-permute-start | bytes 1474568 | tf_op jit(solution)/shard_map/ppermute | solution.py:210
  96.8 3.0 %collective-permute-done.20.refs_10_ = bf16[640,384]{1,0:T(8,128)(2,1)S(1)} collective-permute-done((bf16[640,384]{1,0:T(8,128)(2,1)S(1)}, bf16[640,384]{1,0:T(8,128)(2,1)S(1)}, u32[]{:S(2)}, u32[]{:S(2)}) %collective-permute-start.20) | collective-permute-done | bytes 491552 | tf_op jit(solution)/shard_map/ppermute | solution.py:210
  99.7 3.2 %collective-permute-done.11.refs_3_ = bf16[1408,256]{1,0:T(8,128)(2,1)S(1)} collective-permute-done((bf16[1408,256]{1,0:T(8,128)(2,1)S(1)}, bf16[1408,256]{1,0:T(8,128)(2,1)S(1)}, u32[]{:S(2)}, u32[]{:S(2)}) %collective-permute-start.11) | collective-permute-done | bytes 720928 | tf_op jit(solution)/shard_map/ppermute | solution.py:210
  102.9 3.1 %collective-permute-done.21.refs_11_ = bf16[640,384]{1,0:T(8,128)(2,1)S(1)} collective-permute-done((bf16[640,384]{1,0:T(8,128)(2,1)S(1)}, bf16[640,384]{1,0:T(8,128)(2,1)S(1)}, u32[]{:S(2)}, u32[]{:S(2)}) %collective-permute-start.21) | collective-permute-done | bytes 491552 | tf_op jit(solution)/shard_map/ppermute | solution.py:210
  107.1 6.7 %shard_map.104 = (bf16[256,640]{1,0:T(8,128)(2,1)S(1)}, bf16[256,640]{1,0:T(8,128)(2,1)S(1)}, f32[32,16,256]{2,1,0:T(8,128)S(1)}) custom-call(s32[3]{0:T(128)S(1)} %pad_add_fusion.place_ref, bf16[256,5120]{1,0:T(8,128)(2,1)S(1)} %bitcast.31, bf16[256,5120]{1,0:T(8,128)(2,1)} %collective-permute-done.other_ref, f32[512,128]{1,0:T(8,128)S(1)} %get-tuple-element.30.cos_ref, ...), custom_call_target="tpu_custom_call" | custom-call | flops 3355443200 | bytes 11796480 | tf_op jit(solution)/shard_map/pallas_call | solution.py:92
  113.9 4.4 %collective-permute-start.22 = (bf16[256,640]{1,0:T(8,128)(2,1)S(1)}, bf16[256,640]{1,0:T(8,128)(2,1)S(1)}, u32[]{:S(2)}, u32[]{:S(2)}) collective-permute-start(bf16[256,640]{1,0:T(8,128)(2,1)S(1)} %get-tuple-element.6), channel_id=1, source_target_pairs={{0,8},{8,0},{1,9},{9,1},{2,10},{10,2},{3,11},{11,3},{4,12},{12,4},... | collective-permute-start | bytes 983048 | tf_op jit(solution)/shard_map/ppermute | solution.py:34
  121.5 23.6 %all_to_all.15.parts_ref = bf16[64,8,128]{2,1,0:T(8,128)(2,1)S(1)} all-to-all(bf16[64,8,128]{2,1,0:T(8,128)(2,1)S(1)} %bitcast.32), channel_id=1, replica_groups=mesh['z'=8,'x'=4,'core'=2,'tp'=8] {'z','x','core'}, dimensions={0} | all-to-all | bytes 262144 | tf_op jit(solution)/shard_map/all_to_all | solution.py:222
  146.3 4.4 %all-to-all-start.1 = ((bf16[64,8,128]{2,1,0:T(8,128)(2,1)}), bf16[64,8,128]{2,1,0:T(8,128)(2,1)S(1)}, u32[]{:S(2)}, u32[]{:S(2)}) async-start(bf16[64,8,128]{2,1,0:T(8,128)(2,1)} %shard_map.106), calls=%async_computation.1 | async-start | bytes 262144 | tf_op jit(solution)/shard_map/all_to_all | solution.py:222
  151.9 10.2 %all-to-all-done.1 = bf16[64,8,128]{2,1,0:T(8,128)(2,1)S(1)} async-done(((bf16[64,8,128]{2,1,0:T(8,128)(2,1)}), bf16[64,8,128]{2,1,0:T(8,128)(2,1)S(1)}, u32[]{:S(2)}, u32[]{:S(2)}) %all-to-all-start.1) | async-done | bytes 131104 | tf_op jit(solution)/shard_map/all_to_all | solution.py:222
  163.0 6.8 %all-to-all-start.2 = ((f32[8,8,80]{2,1,0:T(8,128)}), f32[8,8,80]{2,1,0:T(8,128)S(1)}, u32[]{:S(2)}, u32[]{:S(2)}) async-start(f32[8,8,80]{2,1,0:T(8,128)} %fusion.7), calls=%async_computation.2 | async-start | bytes 65536 | tf_op jit(solution)/shard_map/all_to_all | solution.py:222
  172.2 4.6 %all-to-all-done.2 = f32[8,8,80]{2,1,0:T(8,128)S(1)} async-done(((f32[8,8,80]{2,1,0:T(8,128)}), f32[8,8,80]{2,1,0:T(8,128)S(1)}, u32[]{:S(2)}, u32[]{:S(2)}) %all-to-all-start.2) | async-done | bytes 20512 | tf_op jit(solution)/shard_map/all_to_all | solution.py:222
  (96 shorter events, 44.3 us)
Async XLA Ops:
  4.9 15.4 %collective-permute-start.1 = (bf16[96,640]{1,0:T(8,128)(2,1)}, bf16[96,640]{1,0:T(8,128)(2,1)}, u32[]{:S(2)}, u32[]{:S(2)}) collective-permute-start(bf16[96,640]{1,0:T(8,128)(2,1)} %fusion.6), channel_id=1, source_target_pairs={{0,8},{8,0},{1,9},{9,1},{2,10},{10,2},{3,11},{11,3},{4,12},{12,4},... | collective-permute-start | bytes 368648 | tf_op jit(solution)/shard_map/ppermute | solution.py:34
  17.6 88.4 %collective-permute-start = (bf16[256,5120]{1,0:T(8,128)(2,1)S(1)}, bf16[256,5120]{1,0:T(8,128)(2,1)}, u32[]{:S(2)}, u32[]{:S(2)}) collective-permute-start(bf16[256,5120]{1,0:T(8,128)(2,1)S(1)} %bitcast.30), channel_id=1, source_target_pairs={{0,8},{8,0},{1,9},{9,1},{2,10},{10,2},{3,11},{11,3},{4,12},{12,4},... | collective-permute-start | bytes 7864328 | tf_op jit(solution)/shard_map/ppermute | solution.py:34
  21.7 18.7 %collective-permute-start.12 = (bf16[160,384]{1,0:T(8,128)(2,1)S(1)}, bf16[160,384]{1,0:T(8,128)(2,1)S(1)}, u32[]{:S(2)}, u32[]{:S(2)}) collective-permute-start(bf16[160,384]{1,0:T(8,128)(2,1)S(1)} %pad_maximum_fusion.1), channel_id=1, source_target_pairs={{0,16},{8,56},{16,32},{24,8},{32,48},{40,24},{48,0},{56,40},{64,80... | collective-permute-start | bytes 368648 | tf_op jit(solution)/shard_map/ppermute | solution.py:210
  23.6 22.1 %collective-permute-start.13 = (bf16[160,384]{1,0:T(8,128)(2,1)S(1)}, bf16[160,384]{1,0:T(8,128)(2,1)S(1)}, u32[]{:S(2)}, u32[]{:S(2)}) collective-permute-start(bf16[160,384]{1,0:T(8,128)(2,1)S(1)} %pad_maximum_fusion.1), channel_id=1, source_target_pairs={{0,48},{8,24},{16,0},{24,40},{32,16},{40,56},{48,32},{56,8},{64,11... | collective-permute-start | bytes 368648 | tf_op jit(solution)/shard_map/ppermute | solution.py:210
  28.5 8.3 %collective-permute-start.2 = (bf16[176,256]{1,0:T(8,128)(2,1)S(1)}, bf16[176,256]{1,0:T(8,128)(2,1)S(1)}, u32[]{:S(2)}, u32[]{:S(2)}) collective-permute-start(bf16[176,256]{1,0:T(8,128)(2,1)S(1)} %pad_maximum_fusion.2), channel_id=1, source_target_pairs={{0,64},{8,456},{16,80},{24,472},{32,96},{40,488},{48,112},{56,504}... | collective-permute-start | bytes 270344 | tf_op jit(solution)/shard_map/ppermute | solution.py:210
  34.9 14.4 %collective-permute-start.3 = (bf16[176,256]{1,0:T(8,128)(2,1)S(1)}, bf16[176,256]{1,0:T(8,128)(2,1)S(1)}, u32[]{:S(2)}, u32[]{:S(2)}) collective-permute-start(bf16[176,256]{1,0:T(8,128)(2,1)S(1)} %pad_maximum_fusion.2), channel_id=1, source_target_pairs={{0,448},{8,72},{16,464},{24,88},{32,480},{40,104},{48,496},{56,120... | collective-permute-start | bytes 270344 | tf_op jit(solution)/shard_map/ppermute | solution.py:210
  36.8 9.6 %collective-permute-start.14 = (bf16[160,384]{1,0:T(8,128)(2,1)S(1)}, bf16[160,384]{1,0:T(8,128)(2,1)S(1)}, u32[]{:S(2)}, u32[]{:S(2)}) collective-permute-start(bf16[160,384]{1,0:T(8,128)(2,1)S(1)} %pad_maximum_fusion.1), channel_id=1, source_target_pairs={{0,32},{8,40},{16,48},{24,56},{32,0},{40,8},{48,16},{56,24},{64,96... | collective-permute-start | bytes 368648 | tf_op jit(solution)/shard_map/ppermute | solution.py:210
  40.5 14.0 %collective-permute-start.4 = (bf16[176,256]{1,0:T(8,128)(2,1)S(1)}, bf16[176,256]{1,0:T(8,128)(2,1)S(1)}, u32[]{:S(2)}, u32[]{:S(2)}) collective-permute-start(bf16[176,256]{1,0:T(8,128)(2,1)S(1)} %collective-permute-done.2), channel_id=1, source_target_pairs={{0,64},{8,456},{16,80},{24,472},{32,96},{40,488},{48,112},{56,504}... | collective-permute-start | bytes 270344 | tf_op jit(solution)/shard_map/ppermute | solution.py:210
  47.0 19.6 %collective-permute-start.15 = (bf16[640,384]{1,0:T(8,128)(2,1)}, bf16[640,384]{1,0:T(8,128)(2,1)S(1)}, u32[]{:S(2)}, u32[]{:S(2)}) collective-permute-start(bf16[640,384]{1,0:T(8,128)(2,1)} %constant_dynamic-update-slice_fusion.11.refs_4_), channel_id=1, source_target_pairs={{0,64},{8,456},{16,80},{24,472},{32,96},{40,488},{48,112},{56,504}... | collective-permute-start | bytes 1474568 | tf_op jit(solution)/shard_map/ppermute | solution.py:210
  49.3 9.7 %collective-permute-start.5 = (bf16[176,256]{1,0:T(8,128)(2,1)S(1)}, bf16[176,256]{1,0:T(8,128)(2,1)S(1)}, u32[]{:S(2)}, u32[]{:S(2)}) collective-permute-start(bf16[176,256]{1,0:T(8,128)(2,1)S(1)} %collective-permute-done.3), channel_id=1, source_target_pairs={{0,448},{8,72},{16,464},{24,88},{32,480},{40,104},{48,496},{56,120... | collective-permute-start | bytes 270344 | tf_op jit(solution)/shard_map/ppermute | solution.py:210
  52.5 22.2 %collective-permute-start.16 = (bf16[640,384]{1,0:T(8,128)(2,1)}, bf16[640,384]{1,0:T(8,128)(2,1)S(1)}, u32[]{:S(2)}, u32[]{:S(2)}) collective-permute-start(bf16[640,384]{1,0:T(8,128)(2,1)} %constant_dynamic-update-slice_fusion.11.refs_4_), channel_id=1, source_target_pairs={{0,448},{8,72},{16,464},{24,88},{32,480},{40,104},{48,496},{56,120... | collective-permute-start | bytes 1474568 | tf_op jit(solution)/shard_map/ppermute | solution.py:210
  54.4 6.9 %collective-permute-start.6 = (bf16[176,256]{1,0:T(8,128)(2,1)S(1)}, bf16[176,256]{1,0:T(8,128)(2,1)S(1)}, u32[]{:S(2)}, u32[]{:S(2)}) collective-permute-start(bf16[176,256]{1,0:T(8,128)(2,1)S(1)} %collective-permute-done.4), channel_id=1, source_target_pairs={{0,64},{8,456},{16,80},{24,472},{32,96},{40,488},{48,112},{56,504}... | collective-permute-start | bytes 270344 | tf_op jit(solution)/shard_map/ppermute | solution.py:210
  59.0 9.6 %collective-permute-start.7 = (bf16[176,256]{1,0:T(8,128)(2,1)S(1)}, bf16[176,256]{1,0:T(8,128)(2,1)S(1)}, u32[]{:S(2)}, u32[]{:S(2)}) collective-permute-start(bf16[176,256]{1,0:T(8,128)(2,1)S(1)} %collective-permute-done.5), channel_id=1, source_target_pairs={{0,448},{8,72},{16,464},{24,88},{32,480},{40,104},{48,496},{56,120... | collective-permute-start | bytes 270344 | tf_op jit(solution)/shard_map/ppermute | solution.py:210
  61.4 7.3 %collective-permute-start.8 = (bf16[176,256]{1,0:T(8,128)(2,1)S(1)}, bf16[176,256]{1,0:T(8,128)(2,1)S(1)}, u32[]{:S(2)}, u32[]{:S(2)}) collective-permute-start(bf16[176,256]{1,0:T(8,128)(2,1)S(1)} %collective-permute-done.6), channel_id=1, source_target_pairs={{0,64},{8,456},{16,80},{24,472},{32,96},{40,488},{48,112},{56,504}... | collective-permute-start | bytes 270344 | tf_op jit(solution)/shard_map/ppermute | solution.py:210
  66.7 11.1 %collective-permute-start.17 = (bf16[640,384]{1,0:T(8,128)(2,1)S(1)}, bf16[640,384]{1,0:T(8,128)(2,1)S(1)}, u32[]{:S(2)}, u32[]{:S(2)}) collective-permute-start(bf16[640,384]{1,0:T(8,128)(2,1)S(1)} %collective-permute-done.15.refs_5_), channel_id=1, source_target_pairs={{0,64},{8,456},{16,80},{24,472},{32,96},{40,488},{48,112},{56,504}... | collective-permute-start | bytes 1474568 | tf_op jit(solution)/shard_map/ppermute | solution.py:210
  68.7 14.5 %collective-permute-start.9 = (bf16[1408,256]{1,0:T(8,128)(2,1)S(1)}, bf16[1408,256]{1,0:T(8,128)(2,1)S(1)}, u32[]{:S(2)}, u32[]{:S(2)}) collective-permute-start(bf16[1408,256]{1,0:T(8,128)(2,1)S(1)} %constant_dynamic-update-slice_fusion.refs_0_), channel_id=1, source_target_pairs={{0,16},{8,56},{16,32},{24,8},{32,48},{40,24},{48,0},{56,40},{64,80... | collective-permute-start | bytes 2162696 | tf_op jit(solution)/shard_map/ppermute | solution.py:210
  74.7 14.0 %collective-permute-start.18 = (bf16[640,384]{1,0:T(8,128)(2,1)S(1)}, bf16[640,384]{1,0:T(8,128)(2,1)S(1)}, u32[]{:S(2)}, u32[]{:S(2)}) collective-permute-start(bf16[640,384]{1,0:T(8,128)(2,1)S(1)} %collective-permute-done.16.refs_6_), channel_id=1, source_target_pairs={{0,448},{8,72},{16,464},{24,88},{32,480},{40,104},{48,496},{56,120... | collective-permute-start | bytes 1474568 | tf_op jit(solution)/shard_map/ppermute | solution.py:210
  77.8 15.0 %collective-permute-start.19 = (bf16[640,384]{1,0:T(8,128)(2,1)S(1)}, bf16[640,384]{1,0:T(8,128)(2,1)S(1)}, u32[]{:S(2)}, u32[]{:S(2)}) collective-permute-start(bf16[640,384]{1,0:T(8,128)(2,1)S(1)} %collective-permute-done.17.refs_7_), channel_id=1, source_target_pairs={{0,64},{8,456},{16,80},{24,472},{32,96},{40,488},{48,112},{56,504}... | collective-permute-start | bytes 1474568 | tf_op jit(solution)/shard_map/ppermute | solution.py:210
  81.3 15.5 %collective-permute-start.10 = (bf16[1408,256]{1,0:T(8,128)(2,1)S(1)}, bf16[1408,256]{1,0:T(8,128)(2,1)S(1)}, u32[]{:S(2)}, u32[]{:S(2)}) collective-permute-start(bf16[1408,256]{1,0:T(8,128)(2,1)S(1)} %constant_dynamic-update-slice_fusion.refs_0_), channel_id=1, source_target_pairs={{0,48},{8,24},{16,0},{24,40},{32,16},{40,56},{48,32},{56,8},{64,11... | collective-permute-start | bytes 2162696 | tf_op jit(solution)/shard_map/ppermute | solution.py:210
  83.2 19.7 %collective-permute-start.11 = (bf16[1408,256]{1,0:T(8,128)(2,1)S(1)}, bf16[1408,256]{1,0:T(8,128)(2,1)S(1)}, u32[]{:S(2)}, u32[]{:S(2)}) collective-permute-start(bf16[1408,256]{1,0:T(8,128)(2,1)S(1)} %collective-permute-done.9.refs_1_), channel_id=1, source_target_pairs={{0,16},{8,56},{16,32},{24,8},{32,48},{40,24},{48,0},{56,40},{64,80... | collective-permute-start | bytes 2162696 | tf_op jit(solution)/shard_map/ppermute | solution.py:210
  88.6 11.1 %collective-permute-start.20 = (bf16[640,384]{1,0:T(8,128)(2,1)S(1)}, bf16[640,384]{1,0:T(8,128)(2,1)S(1)}, u32[]{:S(2)}, u32[]{:S(2)}) collective-permute-start(bf16[640,384]{1,0:T(8,128)(2,1)S(1)} %collective-permute-done.18.refs_8_), channel_id=1, source_target_pairs={{0,448},{8,72},{16,464},{24,88},{32,480},{40,104},{48,496},{56,120... | collective-permute-start | bytes 1474568 | tf_op jit(solution)/shard_map/ppermute | solution.py:210
  92.8 13.2 %collective-permute-start.21 = (bf16[640,384]{1,0:T(8,128)(2,1)S(1)}, bf16[640,384]{1,0:T(8,128)(2,1)S(1)}, u32[]{:S(2)}, u32[]{:S(2)}) collective-permute-start(bf16[640,384]{1,0:T(8,128)(2,1)S(1)} %collective-permute-done.19.refs_9_), channel_id=1, source_target_pairs={{0,64},{8,456},{16,80},{24,472},{32,96},{40,488},{48,112},{56,504}... | collective-permute-start | bytes 1474568 | tf_op jit(solution)/shard_map/ppermute | solution.py:210
  146.3 15.8 %all-to-all-start.1 = ((bf16[64,8,128]{2,1,0:T(8,128)(2,1)}), bf16[64,8,128]{2,1,0:T(8,128)(2,1)S(1)}, u32[]{:S(2)}, u32[]{:S(2)}) async-start(bf16[64,8,128]{2,1,0:T(8,128)(2,1)} %shard_map.106), calls=%async_computation.1 | async-start | bytes 262144 | tf_op jit(solution)/shard_map/all_to_all | solution.py:222
  163.0 13.8 %all-to-all-start.2 = ((f32[8,8,80]{2,1,0:T(8,128)}), f32[8,8,80]{2,1,0:T(8,128)S(1)}, u32[]{:S(2)}, u32[]{:S(2)}) async-start(f32[8,8,80]{2,1,0:T(8,128)} %fusion.7), calls=%async_computation.2 | async-start | bytes 65536 | tf_op jit(solution)/shard_map/all_to_all | solution.py:222
  (9 other events, 410.2 us)

commit v2 on v1

--- a/solution.py
+++ b/solution.py
@@ -34,11 +34,9 @@
     return lax.ppermute(value, "core", [(0, 1), (1, 0)])
 
 
-def chip_of(place_ref, dz, dx):
+def around(place_ref, axis, chips, ring):
     sign = 1 - 2 * place_ref[2]
-    z = lax.rem(place_ref[0] + sign * dz + Z_CHIPS, Z_CHIPS)
-    x = lax.rem(place_ref[1] + sign * dx + X_CHIPS, X_CHIPS)
-    return z * X_CHIPS + x
+    return [lax.rem(place_ref[axis] + sign * step + chips, chips) for step in ring]
 
 
 def project_kernel(split, place_ref, own_ref, other_ref, cos_ref, sin_ref, *refs):
@@ -55,15 +53,17 @@
             to = pl.multiple_of((2 * chip + whose) * half, 16)
             weight[pl.ds(to, half), columns] = piece[pl.ds(at + part * half, half), :]
 
-    for i, dx in enumerate(X_RING):
-        for j, dz in enumerate(Z_RING):
-            chip = chip_of(place_ref, dz, dx)
-            at = j * (2 * half + extra)
-            place(a_refs[i], at, chip, pl.ds(0, split))
-            tiles = a_refs[i][pl.ds(at + 2 * half, extra), :].astype(jnp.float32)
+    for a_ref, x in zip(a_refs, around(place_ref, 1, X_CHIPS, X_RING)):
+        for z in range(Z_CHIPS):
+            chip = z * X_CHIPS + x
+            at = z * (2 * half + extra)
+            place(a_ref, at, chip, pl.ds(0, split))
+            tiles = a_ref[pl.ds(at + 2 * half, extra), :].astype(jnp.float32)
             query_out[chip, pl.ds(pl.multiple_of(core * 8, 8), 8), :] = tiles[:8]
             query_out[chip, pl.ds(pl.multiple_of(8 - core * 8, 8), 8), :] = tiles[8:16]
-            place(b_refs[j], i * 2 * half, chip, pl.ds(split, width - split))
+    for b_ref, z in zip(b_refs, around(place_ref, 0, Z_CHIPS, Z_RING)):
+        for x in range(X_CHIPS):
+            place(b_ref, x * 2 * half, z * X_CHIPS + x, pl.ds(split, width - split))
 
     chunk = 1024 if depth % 1024 == 0 else depth
     for part, (rows_ref, out) in enumerate(((own_ref, own_out), (other_ref, other_out))):
@@ -222,6 +222,11 @@
     return lax.all_to_all(value, axis, 0, 0, tiled=True)
 
 
+def collect(piece, axis, chips):
+    copies = jnp.broadcast_to(piece, (chips,) + piece.shape)
+    return exchange(copies, axis).reshape(chips * piece.shape[0], piece.shape[1])
+
+
 def per_device(
     saved, block_per_slot, lengths, norm_gain, kv_weight, out_weight, queries, new_kv, row_conv
 ):
@@ -236,31 +241,26 @@
     split = 2 * HEAD_DIM
     keep = jnp.where(first_core, kv_weight[:, 0], kv_weight[:, 1])
     give = jnp.where(first_core, kv_weight[:, 1], kv_weight[:, 0])
-    notes = jnp.concatenate(
-        [
-            queries.reshape(-1),
-            jnp.broadcast_to(row_conv.astype(jnp.bfloat16), (HEAD_DIM,)),
-            block_per_slot.astype(jnp.bfloat16),
-        ]
-    )
-    notes = jnp.pad(notes, (0, 8 * split - notes.shape[0])).reshape(8, split)
+    numbers = jnp.broadcast_to(row_conv, (HEAD_DIM,)), jnp.pad(block_per_slot, (0, split - slot_dev))
+    conv_part, block_part = (part.astype(jnp.bfloat16)[None] for part in numbers)
+    wide = jnp.concatenate([queries, conv_part], axis=1)
+    rows = [wide[:, at : at + split] for at in range(0, wide.shape[1], split)] + [block_part]
+    notes = jnp.pad(jnp.concatenate(rows), ((0, 8 - len(rows)), (0, 0)))
     sent = jnp.concatenate([give, jnp.pad(notes, ((0, 8), (0, local_width - split)))])
     got = swap_cores(sent)
     part_rows = keep.shape[0]
     got_notes = got[part_rows : part_rows + 8, :split]
     piece_a = jnp.concatenate([keep[:, :split], got[:part_rows, :split], notes, got_notes])
     piece_b = jnp.concatenate([keep[:, split:], got[:part_rows, split:]])
-    block_b = jnp.concatenate(
-        [piece_b, send(piece_b, 0, 1), send(piece_b, 0, -1), send(piece_b, 0, 2)]
-    )
-    block_a = jnp.concatenate(ring(piece_a, Z_CHIPS, 1, 0))
+    block_b = collect(piece_b, "x", X_CHIPS)
+    block_a = collect(piece_a, "z", Z_CHIPS)
+    saved, block_b = lax.optimization_barrier((saved, block_b))
     b_blocks = ring(block_b, Z_CHIPS, 1, 0)
     a_blocks = ring(block_a, X_CHIPS, 0, 1)
 
     normed = normalize(saved, norm_gain).reshape(slot_dev * block_rows, model_width)
     other_normed = swap_cores(normed)
-    flat = local_width + HEAD_DIM
-    other_blocks = got_notes[flat // split, flat % split : flat % split + slot_dev]
+    other_blocks = got_notes[len(rows) - 1, :slot_dev]
     blocks = jnp.concatenate([block_per_slot, other_blocks.astype(jnp.int32)])
     conv = blocks // blocks_conv
     positions = (blocks % blocks_conv * block_rows)[:, None] + jnp.arange(

time: 179 us -> 167 us (0.933)
  starting transfers between devices: 92.5 us -> 68.1 us
  waiting for transfers between devices: 27.4 us -> 51 us
  blocking collectives: 23.6 us -> 18.6 us
  other arithmetic: 12.2 us -> 8.7 us
  local copies, waits for them, and re-layouts: 9.33 us -> 6.91 us
    ppermute x20 -> x10, starting transfers between devices: 65.9 us -> 32.9 us  [send(): return lax.ppermute(value, GROUP, pairs)]
    ppermute x20 -> x10, waiting for transfers between devices: 11.4 us -> 26.2 us  [send(): return lax.ppermute(value, GROUP, pairs)]
    all_to_all x2 -> x4, starting transfers between devices: 11.3 us -> 20 us  [exchange(): return lax.all_to_all(value, axis, 0, 0, tiled=True)]
    all_to_all x2 -> x4, waiting for transfers between devices: 14.9 us -> 22.8 us  [exchange(): return lax.all_to_all(value, axis, 0, 0, tiled=True)]
    all_to_all x1, blocking collectives: 23.6 us -> 18.6 us  [exchange(): return lax.all_to_all(value, axis, 0, 0, tiled=True)]
    slice x2, local copies, waits for them, and re-layouts: 2.1 us -> 0.01 us  [per_device(): piece_b = jnp.concatenate([keep[:, split:], got[:part_rows, split:]])]
  transfers between devices with their start and end apart: 25 -> 17, of which waited for: 8 -> 10; matrix products, arithmetic and copies ran while one was open for 9% -> 5% of each run, Pallas kernels for 0% -> 0%
where the time goes in v2:
time: 167 us; the launch traced here: 166 us
  starting transfers between devices  68.1 us (41%)
  waiting for transfers between devices  51 us (31%)
  blocking collectives  18.6 us (11%)
  Pallas kernels  10.4 us (6%)
  other arithmetic  8.7 us (5%)
  local copies, waits for them, and re-layouts  6.91 us (4%)
  between operations  1.67 us (1%)
    ppermute x10, starting transfers between devices, send(): return lax.ppermute(value, GROUP, pairs)  32.9 us
    ppermute x10, waiting for transfers between devices, send(): return lax.ppermute(value, GROUP, pairs)  26.2 us
    all_to_all x4, waiting for transfers between devices, exchange(): return lax.all_to_all(value, axis, 0, 0, tiled=True)  22.8 us
    all_to_all x4, starting transfers between devices, exchange(): return lax.all_to_all(value, axis, 0, 0, tiled=True)  20 us
    all_to_all x1, blocking collectives, exchange(): return lax.all_to_all(value, axis, 0, 0, tiled=True)  18.6 us
    ppermute x3, starting transfers between devices, swap_cores(): return lax.ppermute(value, 'core', [(0, 1), (1, 0)])  15.2 us
    pallas_call x1, Pallas kernels, project(): pl.pallas_call(functools.partial(project_kernel, split), in_specs=[pl.Blo...  7.28 us
  transfers between devices with their start and end apart: 17, of which 10 were waited for; matrix products, arithmetic and copies ran while one was open for 5% of the time, Pallas kernels for 0%

profile of v2, /device:TPU:1, one launch (start us, length us, event | category | flops | bytes accessed | tf_op | source)
XLA Modules:
  0.0 166.1 jit_solution(12610160804457050790)
XLA Ops:
  4.2 8.9 %collective-permute-start = (bf16[96,640]{1,0:T(8,128)(2,1)S(1)}, bf16[96,640]{1,0:T(8,128)(2,1)S(1)}, u32[]{:S(2)}, u32[]{:S(2)}) collective-permute-start(bf16[96,640]{1,0:T(8,128)(2,1)S(1)} %fusion.6), channel_id=1, source_target_pairs={{0,8},{8,0},{1,9},{9,1},{2,10},{10,2},{3,11},{11,3},{4,12},{12,4},... | collective-permute-start | bytes 368648 | tf_op jit(solution)/shard_map/ppermute | solution.py:34
  15.0 4.1 %all-to-all-start = ((bf16[4,160,384]{2,1,0:T(8,128)(2,1)}), bf16[4,160,384]{2,1,0:T(8,128)(2,1)}, u32[]{:S(2)}, u32[]{:S(2)}) async-start(bf16[4,160,384]{2,1,0:T(8,128)(2,1)} %broadcast_in_dim.61), calls=%async_computation | async-start | bytes 983040 | tf_op jit(solution)/shard_map/all_to_all | solution.py:222
  19.2 8.9 %all-to-all-done = bf16[4,160,384]{2,1,0:T(8,128)(2,1)} async-done(((bf16[4,160,384]{2,1,0:T(8,128)(2,1)}), bf16[4,160,384]{2,1,0:T(8,128)(2,1)}, u32[]{:S(2)}, u32[]{:S(2)}) %all-to-all-start) | async-done | bytes 491552 | tf_op jit(solution)/shard_map/all_to_all | solution.py:222
  29.0 4.4 %all-to-all-start.1 = ((bf16[8,176,256]{2,1,0:T(8,128)(2,1)}), bf16[8,176,256]{2,1,0:T(8,128)(2,1)S(1)}, u32[]{:S(2)}, u32[]{:S(2)}) async-start(bf16[8,176,256]{2,1,0:T(8,128)(2,1)} %broadcast_in_dim.67), calls=%async_computation.1 | async-start | bytes 1441792 | tf_op jit(solution)/shard_map/all_to_all | solution.py:222
  35.9 3.6 %collective-permute-start.1 = (bf16[256,5120]{1,0:T(8,128)(2,1)S(1)}, bf16[256,5120]{1,0:T(8,128)(2,1)}, u32[]{:S(2)}, u32[]{:S(2)}) collective-permute-start(bf16[256,5120]{1,0:T(8,128)(2,1)S(1)} %bitcast.32), channel_id=1, source_target_pairs={{0,8},{8,0},{1,9},{9,1},{2,10},{10,2},{3,11},{11,3},{4,12},{12,4},... | collective-permute-start | bytes 7864328 | tf_op jit(solution)/shard_map/ppermute | solution.py:34
  39.6 4.9 %collective-permute-start.5 = (bf16[640,384]{1,0:T(8,128)(2,1)}, bf16[640,384]{1,0:T(8,128)(2,1)}, u32[]{:S(2)}, u32[]{:S(2)}) collective-permute-start(bf16[640,384]{1,0:T(8,128)(2,1)} %bitcast.6.refs_4_), channel_id=1, source_target_pairs={{0,64},{8,456},{16,80},{24,472},{32,96},{40,488},{48,112},{56,504}... | collective-permute-start | bytes 1474568 | tf_op jit(solution)/shard_map/ppermute | solution.py:210
  44.4 1.9 %collective-permute-start.6 = (bf16[640,384]{1,0:T(8,128)(2,1)}, bf16[640,384]{1,0:T(8,128)(2,1)}, u32[]{:S(2)}, u32[]{:S(2)}) collective-permute-start(bf16[640,384]{1,0:T(8,128)(2,1)} %bitcast.6.refs_4_), channel_id=1, source_target_pairs={{0,448},{8,72},{16,464},{24,88},{32,480},{40,104},{48,496},{56,120... | collective-permute-start | bytes 1474568 | tf_op jit(solution)/shard_map/ppermute | solution.py:210
  46.4 14.0 %collective-permute-done.5.refs_5_ = bf16[640,384]{1,0:T(8,128)(2,1)} collective-permute-done((bf16[640,384]{1,0:T(8,128)(2,1)}, bf16[640,384]{1,0:T(8,128)(2,1)}, u32[]{:S(2)}, u32[]{:S(2)}) %collective-permute-start.5) | collective-permute-done | bytes 491552 | tf_op jit(solution)/shard_map/ppermute | solution.py:210
  60.4 3.8 %collective-permute-start.7 = (bf16[640,384]{1,0:T(8,128)(2,1)}, bf16[640,384]{1,0:T(8,128)(2,1)}, u32[]{:S(2)}, u32[]{:S(2)}) collective-permute-start(bf16[640,384]{1,0:T(8,128)(2,1)} %collective-permute-done.5.refs_5_), channel_id=1, source_target_pairs={{0,64},{8,456},{16,80},{24,472},{32,96},{40,488},{48,112},{56,504}... | collective-permute-start | bytes 1474568 | tf_op jit(solution)/shard_map/ppermute | solution.py:210
  64.3 2.8 %collective-permute-start.2 = (bf16[1408,256]{1,0:T(8,128)(2,1)S(1)}, bf16[1408,256]{1,0:T(8,128)(2,1)S(1)}, u32[]{:S(2)}, u32[]{:S(2)}) collective-permute-start(bf16[1408,256]{1,0:T(8,128)(2,1)S(1)} %bitcast.34), channel_id=1, source_target_pairs={{0,16},{8,56},{16,32},{24,8},{32,48},{40,24},{48,0},{56,40},{64,80... | collective-permute-start | bytes 2162696 | tf_op jit(solution)/shard_map/ppermute | solution.py:210
  71.0 4.3 %collective-permute-start.9 = (bf16[640,384]{1,0:T(8,128)(2,1)}, bf16[640,384]{1,0:T(8,128)(2,1)S(1)}, u32[]{:S(2)}, u32[]{:S(2)}) collective-permute-start(bf16[640,384]{1,0:T(8,128)(2,1)} %collective-permute-done.7.refs_7_), channel_id=1, source_target_pairs={{0,64},{8,456},{16,80},{24,472},{32,96},{40,488},{48,112},{56,504}... | collective-permute-start | bytes 1474568 | tf_op jit(solution)/shard_map/ppermute | solution.py:210
  75.4 2.2 %collective-permute-start.3 = (bf16[1408,256]{1,0:T(8,128)(2,1)S(1)}, bf16[1408,256]{1,0:T(8,128)(2,1)S(1)}, u32[]{:S(2)}, u32[]{:S(2)}) collective-permute-start(bf16[1408,256]{1,0:T(8,128)(2,1)S(1)} %bitcast.35), channel_id=1, source_target_pairs={{0,48},{8,24},{16,0},{24,40},{32,16},{40,56},{48,32},{56,8},{64,11... | collective-permute-start | bytes 2162696 | tf_op jit(solution)/shard_map/ppermute | solution.py:210
  77.6 4.3 %collective-permute-start.4 = (bf16[1408,256]{1,0:T(8,128)(2,1)S(1)}, bf16[1408,256]{1,0:T(8,128)(2,1)S(1)}, u32[]{:S(2)}, u32[]{:S(2)}) collective-permute-start(bf16[1408,256]{1,0:T(8,128)(2,1)S(1)} %collective-permute-done.2.refs_1_), channel_id=1, source_target_pairs={{0,16},{8,56},{16,32},{24,8},{32,48},{40,24},{48,0},{56,40},{64,80... | collective-permute-start | bytes 2162696 | tf_op jit(solution)/shard_map/ppermute | solution.py:210
  85.3 4.9 %collective-permute-start.11 = (bf16[640,384]{1,0:T(8,128)(2,1)S(1)}, bf16[640,384]{1,0:T(8,128)(2,1)S(1)}, u32[]{:S(2)}, u32[]{:S(2)}) collective-permute-start(bf16[640,384]{1,0:T(8,128)(2,1)S(1)} %collective-permute-done.9.refs_9_), channel_id=1, source_target_pairs={{0,64},{8,456},{16,80},{24,472},{32,96},{40,488},{48,112},{56,504}... | collective-permute-start | bytes 1474568 | tf_op jit(solution)/shard_map/ppermute | solution.py:210
  91.6 2.2 %collective-permute-done.10.refs_10_ = bf16[640,384]{1,0:T(8,128)(2,1)S(1)} collective-permute-done((bf16[640,384]{1,0:T(8,128)(2,1)S(1)}, bf16[640,384]{1,0:T(8,128)(2,1)S(1)}, u32[]{:S(2)}, u32[]{:S(2)}) %collective-permute-start.10) | collective-permute-done | bytes 491552 | tf_op jit(solution)/shard_map/ppermute | solution.py:210
  93.8 7.4 %collective-permute-done.11.refs_11_ = bf16[640,384]{1,0:T(8,128)(2,1)S(1)} collective-permute-done((bf16[640,384]{1,0:T(8,128)(2,1)S(1)}, bf16[640,384]{1,0:T(8,128)(2,1)S(1)}, u32[]{:S(2)}, u32[]{:S(2)}) %collective-permute-start.11) | collective-permute-done | bytes 491552 | tf_op jit(solution)/shard_map/ppermute | solution.py:210
  101.3 7.3 %shard_map.104 = (bf16[256,640]{1,0:T(8,128)(2,1)S(1)}, bf16[256,640]{1,0:T(8,128)(2,1)S(1)}, f32[32,16,256]{2,1,0:T(8,128)S(1)}) custom-call(s32[3]{0:T(128)S(1)} %pad_add_fusion.place_ref, bf16[256,5120]{1,0:T(8,128)(2,1)S(1)} %bitcast.33, bf16[256,5120]{1,0:T(8,128)(2,1)} %collective-permute-done.1.other_ref, f32[512,128]{1,0:T(8,128)S(1)} %get-tuple-element.27.cos_ref, ...), custom_call_target="tpu_custom_call" | custom-call | flops 3355443200 | bytes 11796480 | tf_op jit(solution)/shard_map/pallas_call | solution.py:92
  108.6 2.6 %collective-permute-start.12 = (bf16[256,640]{1,0:T(8,128)(2,1)S(1)}, bf16[256,640]{1,0:T(8,128)(2,1)S(1)}, u32[]{:S(2)}, u32[]{:S(2)}) collective-permute-start(bf16[256,640]{1,0:T(8,128)(2,1)S(1)} %get-tuple-element.10), channel_id=1, source_target_pairs={{0,8},{8,0},{1,9},{9,1},{2,10},{10,2},{3,11},{11,3},{4,12},{12,4},... | collective-permute-start | bytes 983048 | tf_op jit(solution)/shard_map/ppermute | solution.py:34
  115.1 18.6 %all_to_all.25.parts_ref = bf16[64,8,128]{2,1,0:T(8,128)(2,1)S(1)} all-to-all(bf16[64,8,128]{2,1,0:T(8,128)(2,1)S(1)} %bitcast.37), channel_id=1, replica_groups=mesh['z'=8,'x'=4,'core'=2,'tp'=8] {'z','x','core'}, dimensions={0} | all-to-all | bytes 262144 | tf_op jit(solution)/shard_map/all_to_all | solution.py:222
  134.9 4.6 %all-to-all-start.3 = ((bf16[64,8,128]{2,1,0:T(8,128)(2,1)}), bf16[64,8,128]{2,1,0:T(8,128)(2,1)S(1)}, u32[]{:S(2)}, u32[]{:S(2)}) async-start(bf16[64,8,128]{2,1,0:T(8,128)(2,1)} %shard_map.106), calls=%async_computation.3 | async-start | bytes 262144 | tf_op jit(solution)/shard_map/all_to_all | solution.py:222
  141.6 9.3 %all-to-all-done.3 = bf16[64,8,128]{2,1,0:T(8,128)(2,1)S(1)} async-done(((bf16[64,8,128]{2,1,0:T(8,128)(2,1)}), bf16[64,8,128]{2,1,0:T(8,128)(2,1)S(1)}, u32[]{:S(2)}, u32[]{:S(2)}) %all-to-all-start.3) | async-done | bytes 131104 | tf_op jit(solution)/shard_map/all_to_all | solution.py:222
  151.8 6.8 %all-to-all-start.4 = ((f32[8,8,80]{2,1,0:T(8,128)}), f32[8,8,80]{2,1,0:T(8,128)S(1)}, u32[]{:S(2)}, u32[]{:S(2)}) async-start(f32[8,8,80]{2,1,0:T(8,128)} %fusion.7), calls=%async_computation.4 | async-start | bytes 65536 | tf_op jit(solution)/shard_map/all_to_all | solution.py:222
  158.6 2.3 %pad_maximum_fusion = bf16[2,128,2,640]{3,2,1,0:T(2,128)(2,1)} fusion(bf16[2,128,1,640]{3,2,1,0:T(2,128)(2,1)S(1)} %copy.24, bf16[2,128,1,640]{3,2,1,0:T(2,128)(2,1)S(1)} %copy.23), kind=kLoop, calls=%fused_computation.5 | loop fusion | flops 1310720 | bytes 1310720 | tf_op jit(solution)/shard_map/stack | solution.py:297
  160.9 4.6 %all-to-all-done.4 = f32[8,8,80]{2,1,0:T(8,128)S(1)} async-done(((f32[8,8,80]{2,1,0:T(8,128)}), f32[8,8,80]{2,1,0:T(8,128)S(1)}, u32[]{:S(2)}, u32[]{:S(2)}) %all-to-all-start.4) | async-done | bytes 20512 | tf_op jit(solution)/shard_map/all_to_all | solution.py:222
  (75 shorter events, 25.5 us)
Async XLA Ops:
  0.6 150.3 %copy-start = (bf16[640,80]{0,1:T(8,128)(2,1)S(1)}, bf16[640,80]{0,1:T(8,128)(2,1)}, u32[]{:S(2)}) copy-start(bf16[640,80]{0,1:T(8,128)(2,1)} %param.14) | copy-start | bytes 307204
  0.6 18.5 %copy-start.7 = (bf16[5120]{0:T(1024)(128)(2,1)S(1)}, bf16[5120]{0:T(1024)(128)(2,1)}, u32[]{:S(2)}) copy-start(bf16[5120]{0:T(1024)(128)(2,1)} %param.12) | copy-start | bytes 30724
  4.2 29.3 %copy-start.4 = (bf16[2,128,5120]{2,1,0:T(8,128)(2,1)S(1)}, bf16[2,128,5120]{2,1,0:T(8,128)(2,1)}, u32[]{:S(2)}) copy-start(bf16[2,128,5120]{2,1,0:T(8,128)(2,1)} %param.9) | copy-start | bytes 7864324
  4.2 9.9 %collective-permute-start = (bf16[96,640]{1,0:T(8,128)(2,1)S(1)}, bf16[96,640]{1,0:T(8,128)(2,1)S(1)}, u32[]{:S(2)}, u32[]{:S(2)}) collective-permute-start(bf16[96,640]{1,0:T(8,128)(2,1)S(1)} %fusion.6), channel_id=1, source_target_pairs={{0,8},{8,0},{1,9},{9,1},{2,10},{10,2},{3,11},{11,3},{4,12},{12,4},... | collective-permute-start | bytes 368648 | tf_op jit(solution)/shard_map/ppermute | solution.py:34
  15.0 13.1 %all-to-all-start = ((bf16[4,160,384]{2,1,0:T(8,128)(2,1)}), bf16[4,160,384]{2,1,0:T(8,128)(2,1)}, u32[]{:S(2)}, u32[]{:S(2)}) async-start(bf16[4,160,384]{2,1,0:T(8,128)(2,1)} %broadcast_in_dim.61), calls=%async_computation | async-start | bytes 983040 | tf_op jit(solution)/shard_map/all_to_all | solution.py:222
  29.0 35.3 %all-to-all-start.1 = ((bf16[8,176,256]{2,1,0:T(8,128)(2,1)}), bf16[8,176,256]{2,1,0:T(8,128)(2,1)S(1)}, u32[]{:S(2)}, u32[]{:S(2)}) async-start(bf16[8,176,256]{2,1,0:T(8,128)(2,1)} %broadcast_in_dim.67), calls=%async_computation.1 | async-start | bytes 1441792 | tf_op jit(solution)/shard_map/all_to_all | solution.py:222
  35.2 32.6 %copy-start.8 = (s32[2]{0:T(128)S(1)}, s32[2]{0:T(128)}, u32[]{:S(2)}) copy-start(s32[2]{0:T(128)} %param.10) | copy-start | bytes 28
  35.2 46.7 %copy-start.9 = (s32[4]{0:T(128)S(1)}, s32[4]{0:T(128)}, u32[]{:S(2)}) copy-start(s32[4]{0:T(128)} %param.11) | copy-start | bytes 52
  35.9 65.3 %collective-permute-start.1 = (bf16[256,5120]{1,0:T(8,128)(2,1)S(1)}, bf16[256,5120]{1,0:T(8,128)(2,1)}, u32[]{:S(2)}, u32[]{:S(2)}) collective-permute-start(bf16[256,5120]{1,0:T(8,128)(2,1)S(1)} %bitcast.32), channel_id=1, source_target_pairs={{0,8},{8,0},{1,9},{9,1},{2,10},{10,2},{3,11},{11,3},{4,12},{12,4},... | collective-permute-start | bytes 7864328 | tf_op jit(solution)/shard_map/ppermute | solution.py:34
  39.6 20.8 %collective-permute-start.5 = (bf16[640,384]{1,0:T(8,128)(2,1)}, bf16[640,384]{1,0:T(8,128)(2,1)}, u32[]{:S(2)}, u32[]{:S(2)}) collective-permute-start(bf16[640,384]{1,0:T(8,128)(2,1)} %bitcast.6.refs_4_), channel_id=1, source_target_pairs={{0,64},{8,456},{16,80},{24,472},{32,96},{40,488},{48,112},{56,504}... | collective-permute-start | bytes 1474568 | tf_op jit(solution)/shard_map/ppermute | solution.py:210
  44.4 23.5 %collective-permute-start.6 = (bf16[640,384]{1,0:T(8,128)(2,1)}, bf16[640,384]{1,0:T(8,128)(2,1)}, u32[]{:S(2)}, u32[]{:S(2)}) collective-permute-start(bf16[640,384]{1,0:T(8,128)(2,1)} %bitcast.6.refs_4_), channel_id=1, source_target_pairs={{0,448},{8,72},{16,464},{24,88},{32,480},{40,104},{48,496},{56,120... | collective-permute-start | bytes 1474568 | tf_op jit(solution)/shard_map/ppermute | solution.py:210
  60.4 10.6 %collective-permute-start.7 = (bf16[640,384]{1,0:T(8,128)(2,1)}, bf16[640,384]{1,0:T(8,128)(2,1)}, u32[]{:S(2)}, u32[]{:S(2)}) collective-permute-start(bf16[640,384]{1,0:T(8,128)(2,1)} %collective-permute-done.5.refs_5_), channel_id=1, source_target_pairs={{0,64},{8,456},{16,80},{24,472},{32,96},{40,488},{48,112},{56,504}... | collective-permute-start | bytes 1474568 | tf_op jit(solution)/shard_map/ppermute | solution.py:210
  64.3 13.3 %collective-permute-start.2 = (bf16[1408,256]{1,0:T(8,128)(2,1)S(1)}, bf16[1408,256]{1,0:T(8,128)(2,1)S(1)}, u32[]{:S(2)}, u32[]{:S(2)}) collective-permute-start(bf16[1408,256]{1,0:T(8,128)(2,1)S(1)} %bitcast.34), channel_id=1, source_target_pairs={{0,16},{8,56},{16,32},{24,8},{32,48},{40,24},{48,0},{56,40},{64,80... | collective-permute-start | bytes 2162696 | tf_op jit(solution)/shard_map/ppermute | solution.py:210
  67.9 14.2 %collective-permute-start.8 = (bf16[640,384]{1,0:T(8,128)(2,1)}, bf16[640,384]{1,0:T(8,128)(2,1)S(1)}, u32[]{:S(2)}, u32[]{:S(2)}) collective-permute-start(bf16[640,384]{1,0:T(8,128)(2,1)} %collective-permute-done.6.refs_6_), channel_id=1, source_target_pairs={{0,448},{8,72},{16,464},{24,88},{32,480},{40,104},{48,496},{56,120... | collective-permute-start | bytes 1474568 | tf_op jit(solution)/shard_map/ppermute | solution.py:210
  71.0 14.3 %collective-permute-start.9 = (bf16[640,384]{1,0:T(8,128)(2,1)}, bf16[640,384]{1,0:T(8,128)(2,1)S(1)}, u32[]{:S(2)}, u32[]{:S(2)}) collective-permute-start(bf16[640,384]{1,0:T(8,128)(2,1)} %collective-permute-done.7.refs_7_), channel_id=1, source_target_pairs={{0,64},{8,456},{16,80},{24,472},{32,96},{40,488},{48,112},{56,504}... | collective-permute-start | bytes 1474568 | tf_op jit(solution)/shard_map/ppermute | solution.py:210
  75.4 18.4 %collective-permute-start.3 = (bf16[1408,256]{1,0:T(8,128)(2,1)S(1)}, bf16[1408,256]{1,0:T(8,128)(2,1)S(1)}, u32[]{:S(2)}, u32[]{:S(2)}) collective-permute-start(bf16[1408,256]{1,0:T(8,128)(2,1)S(1)} %bitcast.35), channel_id=1, source_target_pairs={{0,48},{8,24},{16,0},{24,40},{32,16},{40,56},{48,32},{56,8},{64,11... | collective-permute-start | bytes 2162696 | tf_op jit(solution)/shard_map/ppermute | solution.py:210
  77.6 23.7 %collective-permute-start.4 = (bf16[1408,256]{1,0:T(8,128)(2,1)S(1)}, bf16[1408,256]{1,0:T(8,128)(2,1)S(1)}, u32[]{:S(2)}, u32[]{:S(2)}) collective-permute-start(bf16[1408,256]{1,0:T(8,128)(2,1)S(1)} %collective-permute-done.2.refs_1_), channel_id=1, source_target_pairs={{0,16},{8,56},{16,32},{24,8},{32,48},{40,24},{48,0},{56,40},{64,80... | collective-permute-start | bytes 2162696 | tf_op jit(solution)/shard_map/ppermute | solution.py:210
  82.1 11.7 %collective-permute-start.10 = (bf16[640,384]{1,0:T(8,128)(2,1)S(1)}, bf16[640,384]{1,0:T(8,128)(2,1)S(1)}, u32[]{:S(2)}, u32[]{:S(2)}) collective-permute-start(bf16[640,384]{1,0:T(8,128)(2,1)S(1)} %collective-permute-done.8.refs_8_), channel_id=1, source_target_pairs={{0,448},{8,72},{16,464},{24,88},{32,480},{40,104},{48,496},{56,120... | collective-permute-start | bytes 1474568 | tf_op jit(solution)/shard_map/ppermute | solution.py:210
  85.3 15.9 %collective-permute-start.11 = (bf16[640,384]{1,0:T(8,128)(2,1)S(1)}, bf16[640,384]{1,0:T(8,128)(2,1)S(1)}, u32[]{:S(2)}, u32[]{:S(2)}) collective-permute-start(bf16[640,384]{1,0:T(8,128)(2,1)S(1)} %collective-permute-done.9.refs_9_), channel_id=1, source_target_pairs={{0,64},{8,456},{16,80},{24,472},{32,96},{40,488},{48,112},{56,504}... | collective-permute-start | bytes 1474568 | tf_op jit(solution)/shard_map/ppermute | solution.py:210
  101.3 32.4 %copy-start.2 = (bf16[1,640]{1,0:T(2,128)(2,1)S(1)}, bf16[1,640]{1,0:T(2,128)(2,1)}, u32[]{:S(2)}) copy-start(bf16[1,640]{1,0:T(2,128)(2,1)} %query_ref.1) | copy-start | bytes 3844
  101.3 32.4 %copy-start.3 = (bf16[1,2,640]{2,1,0:T(2,128)(2,1)S(1)}, bf16[1,2,640]{2,1,0:T(2,128)(2,1)}, u32[]{:S(2)}) copy-start(bf16[1,2,640]{2,1,0:T(2,128)(2,1)} %param.16) | copy-start | bytes 7684
  108.6 3.9 %collective-permute-start.12 = (bf16[256,640]{1,0:T(8,128)(2,1)S(1)}, bf16[256,640]{1,0:T(8,128)(2,1)S(1)}, u32[]{:S(2)}, u32[]{:S(2)}) collective-permute-start(bf16[256,640]{1,0:T(8,128)(2,1)S(1)} %get-tuple-element.10), channel_id=1, source_target_pairs={{0,8},{8,0},{1,9},{9,1},{2,10},{10,2},{3,11},{11,3},{4,12},{12,4},... | collective-permute-start | bytes 983048 | tf_op jit(solution)/shard_map/ppermute | solution.py:34
  134.9 16.0 %all-to-all-start.3 = ((bf16[64,8,128]{2,1,0:T(8,128)(2,1)}), bf16[64,8,128]{2,1,0:T(8,128)(2,1)S(1)}, u32[]{:S(2)}, u32[]{:S(2)}) async-start(bf16[64,8,128]{2,1,0:T(8,128)(2,1)} %shard_map.106), calls=%async_computation.3 | async-start | bytes 262144 | tf_op jit(solution)/shard_map/all_to_all | solution.py:222
  151.8 13.8 %all-to-all-start.4 = ((f32[8,8,80]{2,1,0:T(8,128)}), f32[8,8,80]{2,1,0:T(8,128)S(1)}, u32[]{:S(2)}, u32[]{:S(2)}) async-start(f32[8,8,80]{2,1,0:T(8,128)} %fusion.7), calls=%async_computation.4 | async-start | bytes 65536 | tf_op jit(solution)/shard_map/all_to_all | solution.py:222
  (3 other events, 17.3 us)

commit v3 on v2

--- a/solution.py
+++ b/solution.py
@@ -39,31 +39,15 @@
     return [lax.rem(place_ref[axis] + sign * step + chips, chips) for step in ring]
 
 
-def project_kernel(split, place_ref, own_ref, other_ref, cos_ref, sin_ref, *refs):
-    a_refs, b_refs = refs[: len(X_RING)], refs[len(X_RING) : len(X_RING) + len(Z_RING)]
-    own_out, other_out, query_out, weight = refs[len(X_RING) + len(Z_RING) :]
-    core = place_ref[2]
+def project_rows(core, half, place_pieces, refs):
+    own_ref, other_ref, cos_ref, sin_ref, own_out, other_out, weight = refs
     rows, depth = own_ref.shape
     width = weight.shape[1]
-    half = depth // (2 * Z_CHIPS * X_CHIPS)
-    extra = a_refs[0].shape[0] // len(Z_RING) - 2 * half
-
-    def place(piece, at, chip, columns):
+
+    for chip, ref, at in place_pieces:
         for part, whose in ((0, core), (1, 1 - core)):
             to = pl.multiple_of((2 * chip + whose) * half, 16)
-            weight[pl.ds(to, half), columns] = piece[pl.ds(at + part * half, half), :]
-
-    for a_ref, x in zip(a_refs, around(place_ref, 1, X_CHIPS, X_RING)):
-        for z in range(Z_CHIPS):
-            chip = z * X_CHIPS + x
-            at = z * (2 * half + extra)
-            place(a_ref, at, chip, pl.ds(0, split))
-            tiles = a_ref[pl.ds(at + 2 * half, extra), :].astype(jnp.float32)
-            query_out[chip, pl.ds(pl.multiple_of(core * 8, 8), 8), :] = tiles[:8]
-            query_out[chip, pl.ds(pl.multiple_of(8 - core * 8, 8), 8), :] = tiles[8:16]
-    for b_ref, z in zip(b_refs, around(place_ref, 0, Z_CHIPS, Z_RING)):
-        for x in range(X_CHIPS):
-            place(b_ref, x * 2 * half, z * X_CHIPS + x, pl.ds(split, width - split))
+            weight[pl.ds(to, half), :] = ref[pl.ds(at + part * half, half), :]
 
     chunk = 1024 if depth % 1024 == 0 else depth
     for part, (rows_ref, out) in enumerate(((own_ref, own_out), (other_ref, other_out))):
@@ -81,33 +65,64 @@
             out[:, pl.ds(head * HEAD_DIM, HEAD_DIM)] = turned.astype(out.dtype)
 
 
-def project(place, own, other, cosine, sine, a_blocks, b_blocks):
-    rows, depth = own.shape
-    split = a_blocks[0].shape[1]
-    width = split + b_blocks[0].shape[1]
-    out = jax.ShapeDtypeStruct((rows, width), jnp.bfloat16)
-    tiles = jax.ShapeDtypeStruct((Z_CHIPS * X_CHIPS, 16, split), jnp.float32)
+def project_a_kernel(place_ref, *refs):
+    rows_refs, a_refs = refs[:4], refs[4 : 4 + len(X_RING)]
+    own_out, other_out, query_out, weight = refs[4 + len(X_RING) :]
+    core = place_ref[2]
+    half = weight.shape[0] // (2 * Z_CHIPS * X_CHIPS)
+    each = a_refs[0].shape[0] // Z_CHIPS
+    pieces = []
+    for ref, x in zip(a_refs, around(place_ref, 1, X_CHIPS, X_RING)):
+        for z in range(Z_CHIPS):
+            chip = z * X_CHIPS + x
+            pieces.append((chip, ref, z * each))
+            notes = ref[pl.ds(z * each + 2 * half, each - 2 * half), :].astype(jnp.float32)
+            query_out[chip, pl.ds(pl.multiple_of(core * 8, 8), 8), :] = notes[:8]
+            query_out[chip, pl.ds(pl.multiple_of(8 - core * 8, 8), 8), :] = notes[8:16]
+    project_rows(core, half, pieces, (*rows_refs, own_out, other_out, weight))
+
+
+def project_b_kernel(place_ref, *refs):
+    rows_refs, b_refs = refs[:4], refs[4 : 4 + len(Z_RING)]
+    own_out, other_out, weight = refs[4 + len(Z_RING) :]
+    half = weight.shape[0] // (2 * Z_CHIPS * X_CHIPS)
+    pieces = []
+    for ref, z in zip(b_refs, around(place_ref, 0, Z_CHIPS, Z_RING)):
+        for i, x in enumerate(around(place_ref, 1, X_CHIPS, X_RING)):
+            pieces.append((z * X_CHIPS + x, ref, i * 2 * half))
+    project_rows(place_ref[2], half, pieces, (*rows_refs, own_out, other_out, weight))
+
+
+def project(kernel, place, rows, tables, blocks, extra_out=()):
+    count, depth = rows[0].shape
+    width = blocks[0].shape[1]
+    out = jax.ShapeDtypeStruct((count, width), jnp.bfloat16)
     vmem = pl.BlockSpec(memory_space=pltpu.VMEM)
-    operands = (own, other, cosine, sine, *a_blocks, *b_blocks)
+    operands = (*rows, *tables, *blocks)
     return pl.pallas_call(
-        functools.partial(project_kernel, split),
+        kernel,
         in_specs=[pl.BlockSpec(memory_space=pltpu.SMEM)] + [vmem] * len(operands),
-        out_specs=[vmem] * 3,
-        out_shape=[out, out, tiles],
+        out_specs=[vmem] * (2 + len(extra_out)),
+        out_shape=[out, out, *extra_out],
         scratch_shapes=[pltpu.VMEM((depth, width), jnp.bfloat16)],
-        compiler_params=pltpu.CompilerParams(vmem_limit_bytes=40 * MIB),
+        compiler_params=pltpu.CompilerParams(vmem_limit_bytes=32 * MIB),
         cost_estimate=pl.CostEstimate(
-            flops=4 * rows * depth * width,
-            bytes_accessed=4 * rows * depth + 2 * depth * width,
+            flops=4 * count * depth * width,
+            bytes_accessed=4 * count * depth + 2 * depth * width,
             transcendentals=0,
         ),
     )(place, *operands)
 
 
-def attend_kernel(place_ref, mine_ref, theirs_ref, query_ref, keys_ref, out_ref, tiles):
+def attend_kernel(place_ref, mine_a, theirs_a, mine_b, theirs_b, query_ref, keys_ref, out_ref, tiles):
     has_keys = place_ref[2] == 0
     chips = query_ref.shape[0]
-    heads = mine_ref.shape[1] // HEAD_DIM
+    halves = [
+        (mine, theirs, head * HEAD_DIM)
+        for mine, theirs in ((mine_a, theirs_a), (mine_b, theirs_b))
+        for head in range(mine.shape[1] // HEAD_DIM)
+    ]
+    heads = len(halves)
     key_conv = keys_ref[0:1, :]
 
     def rows_of(part):
@@ -122,8 +137,8 @@
         for core in (0, 1):
             tiles[:, core, row, :] = value[core * chips : (core + 1) * chips]
 
-    for head in range(heads):
-        lanes = pl.ds(head * HEAD_DIM, HEAD_DIM)
+    for head, (mine_ref, theirs_ref, first) in enumerate(halves):
+        lanes = pl.ds(first, HEAD_DIM)
         mine, theirs = mine_ref[:, lanes], theirs_ref[:, lanes]
         keys = jnp.where(has_keys, mine, theirs)
         values = jnp.where(has_keys, theirs, mine)
@@ -151,17 +166,17 @@
     out_ref[...] = tiles[...].astype(jnp.bfloat16)
 
 
-def attend(place, mine, theirs, queries, key_conv):
+def attend(place, halves, queries, key_conv):
     shape = (queries.shape[0], 2, 8, HEAD_DIM)
     vmem = pl.BlockSpec(memory_space=pltpu.VMEM)
     return pl.pallas_call(
         attend_kernel,
-        in_specs=[pl.BlockSpec(memory_space=pltpu.SMEM)] + [vmem] * 4,
+        in_specs=[pl.BlockSpec(memory_space=pltpu.SMEM)] + [vmem] * 6,
         out_specs=vmem,
         out_shape=jax.ShapeDtypeStruct(shape, jnp.bfloat16),
         scratch_shapes=[pltpu.VMEM(shape, jnp.float32)],
         compiler_params=pltpu.CompilerParams(vmem_limit_bytes=16 * MIB),
-    )(place, mine, theirs, queries, key_conv)
+    )(place, *halves, queries, key_conv)
 
 
 def merge_kernel(heads, parts_ref, query_ref, new_ref, out_ref, parts, tile):
@@ -222,11 +237,6 @@
     return lax.all_to_all(value, axis, 0, 0, tiled=True)
 
 
-def collect(piece, axis, chips):
-    copies = jnp.broadcast_to(piece, (chips,) + piece.shape)
-    return exchange(copies, axis).reshape(chips * piece.shape[0], piece.shape[1])
-
-
 def per_device(
     saved, block_per_slot, lengths, norm_gain, kv_weight, out_weight, queries, new_kv, row_conv
 ):
@@ -244,23 +254,27 @@
     numbers = jnp.broadcast_to(row_conv, (HEAD_DIM,)), jnp.pad(block_per_slot, (0, split - slot_dev))
     conv_part, block_part = (part.astype(jnp.bfloat16)[None] for part in numbers)
     wide = jnp.concatenate([queries, conv_part], axis=1)
-    rows = [wide[:, at : at + split] for at in range(0, wide.shape[1], split)] + [block_part]
-    notes = jnp.pad(jnp.concatenate(rows), ((0, 8 - len(rows)), (0, 0)))
+    lines = [wide[:, at : at + split] for at in range(0, wide.shape[1], split)] + [block_part]
+    notes = jnp.pad(jnp.concatenate(lines), ((0, 8 - len(lines)), (0, 0)))
     sent = jnp.concatenate([give, jnp.pad(notes, ((0, 8), (0, local_width - split)))])
     got = swap_cores(sent)
     part_rows = keep.shape[0]
     got_notes = got[part_rows : part_rows + 8, :split]
     piece_a = jnp.concatenate([keep[:, :split], got[:part_rows, :split], notes, got_notes])
     piece_b = jnp.concatenate([keep[:, split:], got[:part_rows, split:]])
-    block_b = collect(piece_b, "x", X_CHIPS)
-    block_a = collect(piece_a, "z", Z_CHIPS)
-    saved, block_b = lax.optimization_barrier((saved, block_b))
+    copies_a = jnp.broadcast_to(piece_a, (Z_CHIPS,) + piece_a.shape)
+    copies_a, piece_b = lax.optimization_barrier((copies_a, piece_b))
+    block_a = exchange(copies_a, "z").reshape(Z_CHIPS * piece_a.shape[0], split)
+    block_b = jnp.concatenate(
+        [piece_b, send(piece_b, 0, 1), send(piece_b, 0, -1), send(piece_b, 0, 2)]
+    )
     b_blocks = ring(block_b, Z_CHIPS, 1, 0)
     a_blocks = ring(block_a, X_CHIPS, 0, 1)
+    saved, b_blocks[1] = lax.optimization_barrier((saved, b_blocks[1]))
 
     normed = normalize(saved, norm_gain).reshape(slot_dev * block_rows, model_width)
     other_normed = swap_cores(normed)
-    other_blocks = got_notes[len(rows) - 1, :slot_dev]
+    other_blocks = got_notes[len(lines) - 1, :slot_dev]
     blocks = jnp.concatenate([block_per_slot, other_blocks.astype(jnp.int32)])
     conv = blocks // blocks_conv
     positions = (blocks % blocks_conv * block_rows)[:, None] + jnp.arange(
@@ -280,11 +294,14 @@
     key_conv = jnp.broadcast_to(key_conv.astype(jnp.float32), (8, own_rows))
     place = jnp.stack([lax.axis_index("z"), lax.axis_index("x"), core]).astype(jnp.int32)
 
-    mine, for_other, tiles = project(
-        place, normed, other_normed, cosine, sine, a_blocks, b_blocks
-    )
-    theirs = swap_cores(for_other)
-    parts = attend(place, mine, theirs, tiles, key_conv).reshape(groups, 8, HEAD_DIM)
+    rows, tables = (normed, other_normed), (cosine, sine)
+    tiles = jax.ShapeDtypeStruct((Z_CHIPS * X_CHIPS, 16, split), jnp.float32)
+    mine_a, give_a, tiles = project(project_a_kernel, place, rows, tables, a_blocks, (tiles,))
+    theirs_a = swap_cores(give_a)
+    mine_b, give_b = project(project_b_kernel, place, rows, tables, b_blocks)
+    theirs_b = swap_cores(give_b)
+    halves = (mine_a, theirs_a, mine_b, theirs_b)
+    parts = attend(place, halves, tiles, key_conv).reshape(groups, 8, HEAD_DIM)
     merged = merge(exchange(parts, GROUP), queries, new_kv[0])
     attended = exchange(merged, GROUP)[:, :heads].reshape(groups, local_width)
     decoded = jnp.dot(attended, out_weight, preferred_element_type=jnp.float32)
@@ -292,6 +309,8 @@
     decoded = exchange(decoded.reshape(tp, groups // tp, -1), "tp")
     decoded = jnp.sum(decoded, axis=0).astype(jnp.bfloat16)
 
+    mine = jnp.concatenate([mine_a, mine_b], axis=1)
+    theirs = jnp.concatenate([theirs_a, theirs_b], axis=1)
     keys = jnp.where(first_core, mine, theirs)
     values = jnp.where(first_core, theirs, mine)
     kv_cache = jnp.stack([keys, values], axis=1).reshape(slot_dev, block_rows, 2, local_width)

time: 167 us -> 176 us (1.054)
  starting transfers between devices: 68.1 us -> 97.2 us
  blocking collectives: 18.6 us -> 0 us
  waiting for transfers between devices: 51 us -> 43.5 us
  Pallas kernels: 10.4 us -> 12.8 us
  other arithmetic: 8.7 us -> 10.9 us
    all_to_all x1 -> x0, blocking collectives: 18.6 us -> none  [exchange(): return lax.all_to_all(value, axis, 0, 0, tiled=True)]
    ppermute x10 -> x13, starting transfers between devices: 32.9 us -> 49.8 us  [send(): return lax.ppermute(value, GROUP, pairs)]
    ppermute x3 -> x4, starting transfers between devices: 15.2 us -> 26.4 us  [swap_cores(): return lax.ppermute(value, 'core', [(0, 1), (1, 0)])]
    ppermute x10 -> x13, waiting for transfers between devices: 26.2 us -> 17.6 us  [send(): return lax.ppermute(value, GROUP, pairs)]
    reduce_sum x1, other arithmetic: 0.6 us -> 2.52 us  [normalize(): jnp.mean(as_float * as_float, axis=-1, keepdims=True) + EPSILON]
    pallas_call x1 -> x2, Pallas kernels: 7.28 us -> 9.05 us  [project(): pl.pallas_call(kernel, in_specs=[pl.BlockSpec(memory_space=pltpu.SMEM)] +...]
  transfers between devices with their start and end apart: 17 -> 21, of which waited for: 10 -> 13; matrix products, arithmetic and copies ran while one was open for 5% -> 7% of each run, Pallas kernels for 0% -> 5%
where the time goes in v3:
time: 176 us; the launch traced here: 175 us
  starting transfers between devices  97.2 us (55%)
  waiting for transfers between devices  43.5 us (25%)
  Pallas kernels  12.8 us (7%)
  other arithmetic  10.9 us (6%)
  local copies, waits for them, and re-layouts  8.08 us (5%)
  between operations  1.8 us (1%)
    ppermute x13, starting transfers between devices, send(): return lax.ppermute(value, GROUP, pairs)  49.8 us
    ppermute x4, starting transfers between devices, swap_cores(): return lax.ppermute(value, 'core', [(0, 1), (1, 0)])  26.4 us
    all_to_all x4, waiting for transfers between devices, exchange(): return lax.all_to_all(value, axis, 0, 0, tiled=True)  24.2 us
    all_to_all x4, starting transfers between devices, exchange(): return lax.all_to_all(value, axis, 0, 0, tiled=True)  21.1 us
    ppermute x13, waiting for transfers between devices, send(): return lax.ppermute(value, GROUP, pairs)  17.6 us
    pallas_call x2, Pallas kernels, project(): pl.pallas_call(kernel, in_specs=[pl.BlockSpec(memory_space=pltpu.SMEM)] +...  9.05 us
  transfers between devices with their start and end apart: 21, of which 13 were waited for; matrix products, arithmetic and copies ran while one was open for 7% of the time, Pallas kernels for 5%

profile of v3, /device:TPU:1, one launch (start us, length us, event | category | flops | bytes accessed | tf_op | source)
XLA Modules:
  0.0 175.1 jit_solution(12094354292728382744)
XLA Ops:
  4.2 8.8 %collective-permute-start = (bf16[96,640]{1,0:T(8,128)(2,1)S(1)}, bf16[96,640]{1,0:T(8,128)(2,1)S(1)}, u32[]{:S(2)}, u32[]{:S(2)}) collective-permute-start(bf16[96,640]{1,0:T(8,128)(2,1)S(1)} %fusion.6), channel_id=1, source_target_pairs={{0,8},{8,0},{1,9},{9,1},{2,10},{10,2},{3,11},{11,3},{4,12},{12,4},... | collective-permute-start | bytes 368648 | tf_op jit(solution)/shard_map/ppermute | solution.py:34
  17.4 3.4 %collective-permute-start.2 = (bf16[160,384]{1,0:T(8,128)(2,1)S(1)}, bf16[160,384]{1,0:T(8,128)(2,1)S(1)}, u32[]{:S(2)}, u32[]{:S(2)}) collective-permute-start(bf16[160,384]{1,0:T(8,128)(2,1)S(1)} %pad_maximum_fusion.1), channel_id=1, source_target_pairs={{0,48},{8,24},{16,0},{24,40},{32,16},{40,56},{48,32},{56,8},{64,11... | collective-permute-start | bytes 368648 | tf_op jit(solution)/shard_map/ppermute | solution.py:225
  24.5 3.5 %collective-permute-done.3 = bf16[160,384]{1,0:T(8,128)(2,1)S(1)} collective-permute-done((bf16[160,384]{1,0:T(8,128)(2,1)S(1)}, bf16[160,384]{1,0:T(8,128)(2,1)S(1)}, u32[]{:S(2)}, u32[]{:S(2)}) %collective-permute-start.3) | collective-permute-done | bytes 122912 | tf_op jit(solution)/shard_map/ppermute | solution.py:225
  28.0 6.3 %collective-permute-start.4 = (bf16[640,384]{1,0:T(8,128)(2,1)S(1)}, bf16[640,384]{1,0:T(8,128)(2,1)S(1)}, u32[]{:S(2)}, u32[]{:S(2)}) collective-permute-start(bf16[640,384]{1,0:T(8,128)(2,1)S(1)} %constant_dynamic-update-slice_fusion.refs_4_), channel_id=1, source_target_pairs={{0,64},{8,456},{16,80},{24,472},{32,96},{40,488},{48,112},{56,504}... | collective-permute-start | bytes 1474568 | tf_op jit(solution)/shard_map/ppermute | solution.py:225
  34.3 3.6 %all-to-all-start = ((bf16[8,176,256]{2,1,0:T(8,128)(2,1)}), bf16[8,176,256]{2,1,0:T(8,128)(2,1)S(1)}, u32[]{:S(2)}, u32[]{:S(2)}) async-start(bf16[8,176,256]{2,1,0:T(8,128)(2,1)} %broadcast_in_dim.58), calls=%async_computation | async-start | bytes 1441792 | tf_op jit(solution)/shard_map/all_to_all | solution.py:237
  40.1 2.5 %fusion = f32[2,128]{1,0:T(2,128)S(1)} fusion(bf16[2,128,5120]{2,1,0:T(8,128)(2,1)} %param.9), kind=kLoop, calls=%fused_computation.2 | loop fusion | flops 3931904 | bytes 2622464 | tf_op jit(solution)/shard_map/reduce_sum | solution.py:24
  43.4 8.0 %collective-permute-start.5 = (bf16[256,5120]{1,0:T(8,128)(2,1)S(1)}, bf16[256,5120]{1,0:T(8,128)(2,1)}, u32[]{:S(2)}, u32[]{:S(2)}) collective-permute-start(bf16[256,5120]{1,0:T(8,128)(2,1)S(1)} %bitcast.33), channel_id=1, source_target_pairs={{0,8},{8,0},{1,9},{9,1},{2,10},{10,2},{3,11},{11,3},{4,12},{12,4},... | collective-permute-start | bytes 7864328 | tf_op jit(solution)/shard_map/ppermute | solution.py:34
  53.5 6.1 %collective-permute-start.10 = (bf16[640,384]{1,0:T(8,128)(2,1)}, bf16[640,384]{1,0:T(8,128)(2,1)}, u32[]{:S(2)}, u32[]{:S(2)}) collective-permute-start(bf16[640,384]{1,0:T(8,128)(2,1)} %copy-done.4), channel_id=1, source_target_pairs={{0,64},{8,456},{16,80},{24,472},{32,96},{40,488},{48,112},{56,504}... | collective-permute-start | bytes 1474568 | tf_op jit(solution)/shard_map/ppermute | solution.py:225
  60.4 5.1 %collective-permute-start.6 = (bf16[1408,256]{1,0:T(8,128)(2,1)S(1)}, bf16[1408,256]{1,0:T(8,128)(2,1)S(1)}, u32[]{:S(2)}, u32[]{:S(2)}) collective-permute-start(bf16[1408,256]{1,0:T(8,128)(2,1)S(1)} %bitcast.36), channel_id=1, source_target_pairs={{0,16},{8,56},{16,32},{24,8},{32,48},{40,24},{48,0},{56,40},{64,80... | collective-permute-start | bytes 2162696 | tf_op jit(solution)/shard_map/ppermute | solution.py:225
  69.5 5.2 %collective-permute-start.12 = (bf16[640,384]{1,0:T(8,128)(2,1)}, bf16[640,384]{1,0:T(8,128)(2,1)S(1)}, u32[]{:S(2)}, u32[]{:S(2)}) collective-permute-start(bf16[640,384]{1,0:T(8,128)(2,1)} %collective-permute-done.10.refs_7_), channel_id=1, source_target_pairs={{0,64},{8,456},{16,80},{24,472},{32,96},{40,488},{48,112},{56,504}... | collective-permute-start | bytes 1474568 | tf_op jit(solution)/shard_map/ppermute | solution.py:225
  79.2 5.4 %collective-permute-start.7 = (bf16[1408,256]{1,0:T(8,128)(2,1)S(1)}, bf16[1408,256]{1,0:T(8,128)(2,1)S(1)}, u32[]{:S(2)}, u32[]{:S(2)}) collective-permute-start(bf16[1408,256]{1,0:T(8,128)(2,1)S(1)} %bitcast.37), channel_id=1, source_target_pairs={{0,48},{8,24},{16,0},{24,40},{32,16},{40,56},{48,32},{56,8},{64,11... | collective-permute-start | bytes 2162696 | tf_op jit(solution)/shard_map/ppermute | solution.py:225
  85.4 4.9 %collective-permute-start.14 = (bf16[640,384]{1,0:T(8,128)(2,1)S(1)}, bf16[640,384]{1,0:T(8,128)(2,1)S(1)}, u32[]{:S(2)}, u32[]{:S(2)}) collective-permute-start(bf16[640,384]{1,0:T(8,128)(2,1)S(1)} %collective-permute-done.12.refs_9_), channel_id=1, source_target_pairs={{0,64},{8,456},{16,80},{24,472},{32,96},{40,488},{48,112},{56,504}... | collective-permute-start | bytes 1474568 | tf_op jit(solution)/shard_map/ppermute | solution.py:225
  90.4 3.9 %collective-permute-start.8 = (bf16[1408,256]{1,0:T(8,128)(2,1)S(1)}, bf16[1408,256]{1,0:T(8,128)(2,1)S(1)}, u32[]{:S(2)}, u32[]{:S(2)}) collective-permute-start(bf16[1408,256]{1,0:T(8,128)(2,1)S(1)} %collective-permute-done.6.refs_5_), channel_id=1, source_target_pairs={{0,16},{8,56},{16,32},{24,8},{32,48},{40,24},{48,0},{56,40},{64,80... | collective-permute-start | bytes 2162696 | tf_op jit(solution)/shard_map/ppermute | solution.py:225
  95.7 5.1 %collective-permute-done.14.refs_11_ = bf16[640,384]{1,0:T(8,128)(2,1)S(1)} collective-permute-done((bf16[640,384]{1,0:T(8,128)(2,1)S(1)}, bf16[640,384]{1,0:T(8,128)(2,1)S(1)}, u32[]{:S(2)}, u32[]{:S(2)}) %collective-permute-start.14) | collective-permute-done | bytes 491552 | tf_op jit(solution)/shard_map/ppermute | solution.py:225
  102.8 5.4 %shard_map.105 = (bf16[256,384]{1,0:T(8,128)(2,1)S(1)}, bf16[256,384]{1,0:T(8,128)(2,1)S(1)}) custom-call(s32[3]{0:T(128)S(1)} %pad_add_fusion.place_ref, bf16[256,5120]{1,0:T(8,128)(2,1)S(1)} %bitcast.34, bf16[256,5120]{1,0:T(8,128)(2,1)} %collective-permute-done.5.refs_1_, f32[512,128]{1,0:T(8,128)S(1)} %get-tuple-element.35.refs_2_, ...), custom_call_target="tpu_custom_call" | custom-call | flops 2013265920 | bytes 9175040 | tf_op jit(solution)/shard_map/pallas_call | solution.py:102
  108.2 7.7 %collective-permute-start.16 = (bf16[256,384]{1,0:T(8,128)(2,1)S(1)}, bf16[256,384]{1,0:T(8,128)(2,1)S(1)}, u32[]{:S(2)}, u32[]{:S(2)}) collective-permute-start(bf16[256,384]{1,0:T(8,128)(2,1)S(1)} %get-tuple-element.18), channel_id=1, source_target_pairs={{0,8},{8,0},{1,9},{9,1},{2,10},{10,2},{3,11},{11,3},{4,12},{12,4},... | collective-permute-start | bytes 589832 | tf_op jit(solution)/shard_map/ppermute | solution.py:34
  115.9 3.7 %shard_map.104 = (bf16[256,256]{1,0:T(8,128)(2,1)S(1)}, bf16[256,256]{1,0:T(8,128)(2,1)S(1)}, f32[32,16,256]{2,1,0:T(8,128)S(1)}) custom-call(s32[3]{0:T(128)S(1)} %pad_add_fusion.place_ref, bf16[256,5120]{1,0:T(8,128)(2,1)S(1)} %bitcast.35, bf16[256,5120]{1,0:T(8,128)(2,1)} %collective-permute-done.5.refs_1_, f32[512,128]{1,0:T(8,128)S(1)} %get-tuple-element.35.refs_2_, ...), custom_call_target="tpu_custom_call" | custom-call | flops 1342177280 | bytes 7864320 | tf_op jit(solution)/shard_map/pallas_call | solution.py:102
  122.9 2.6 %shard_map.106 = bf16[32,2,8,128]{3,2,1,0:T(8,128)(2,1)} custom-call(s32[3]{0:T(128)S(1)} %pad_add_fusion.place_ref, bf16[256,256]{1,0:T(8,128)(2,1)S(1)} %get-tuple-element.14.mine_a, bf16[256,256]{1,0:T(8,128)(2,1)S(1)} %collective-permute-done.15.theirs_a, bf16[256,384]{1,0:T(8,128)(2,1)S(1)} %get-tuple-element.16.mine_b, ...), custom_call_target="tpu_custom_call" | custom-call | tf_op jit(solution)/shard_map/pallas_call | solution.py:172
  125.4 6.2 %all-to-all-start.1 = ((bf16[64,8,128]{2,1,0:T(8,128)(2,1)}), bf16[64,8,128]{2,1,0:T(8,128)(2,1)S(1)}, u32[]{:S(2)}, u32[]{:S(2)}) async-start(bf16[64,8,128]{2,1,0:T(8,128)(2,1)} %bitcast.16), calls=%async_computation.1 | async-start | bytes 262144 | tf_op jit(solution)/shard_map/all_to_all | solution.py:237
  133.2 9.6 %all-to-all-done.1.parts_ref = bf16[64,8,128]{2,1,0:T(8,128)(2,1)S(1)} async-done(((bf16[64,8,128]{2,1,0:T(8,128)(2,1)}), bf16[64,8,128]{2,1,0:T(8,128)(2,1)S(1)}, u32[]{:S(2)}, u32[]{:S(2)}) %all-to-all-start.1) | async-done | bytes 131104 | tf_op jit(solution)/shard_map/all_to_all | solution.py:237
  144.0 4.4 %all-to-all-start.2 = ((bf16[64,8,128]{2,1,0:T(8,128)(2,1)}), bf16[64,8,128]{2,1,0:T(8,128)(2,1)S(1)}, u32[]{:S(2)}, u32[]{:S(2)}) async-start(bf16[64,8,128]{2,1,0:T(8,128)(2,1)} %shard_map.107), calls=%async_computation.2 | async-start | bytes 262144 | tf_op jit(solution)/shard_map/all_to_all | solution.py:237
  149.8 10.0 %all-to-all-done.2 = bf16[64,8,128]{2,1,0:T(8,128)(2,1)S(1)} async-done(((bf16[64,8,128]{2,1,0:T(8,128)(2,1)}), bf16[64,8,128]{2,1,0:T(8,128)(2,1)S(1)}, u32[]{:S(2)}, u32[]{:S(2)}) %all-to-all-start.2) | async-done | bytes 131104 | tf_op jit(solution)/shard_map/all_to_all | solution.py:237
  160.7 6.8 %all-to-all-start.3 = ((f32[8,8,80]{2,1,0:T(8,128)}), f32[8,8,80]{2,1,0:T(8,128)S(1)}, u32[]{:S(2)}, u32[]{:S(2)}) async-start(f32[8,8,80]{2,1,0:T(8,128)} %fusion.7), calls=%async_computation.3 | async-start | bytes 65536 | tf_op jit(solution)/shard_map/all_to_all | solution.py:237
  169.9 4.6 %all-to-all-done.3 = f32[8,8,80]{2,1,0:T(8,128)S(1)} async-done(((f32[8,8,80]{2,1,0:T(8,128)}), f32[8,8,80]{2,1,0:T(8,128)S(1)}, u32[]{:S(2)}, u32[]{:S(2)}) %all-to-all-start.3) | async-done | bytes 20512 | tf_op jit(solution)/shard_map/all_to_all | solution.py:237
  (94 shorter events, 40.7 us)
Async XLA Ops:
  0.6 159.3 %copy-start = (bf16[640,80]{0,1:T(8,128)(2,1)S(1)}, bf16[640,80]{0,1:T(8,128)(2,1)}, u32[]{:S(2)}) copy-start(bf16[640,80]{0,1:T(8,128)(2,1)} %param.14) | copy-start | bytes 307204
  0.6 33.7 %copy-start.10 = (bf16[5120]{0:T(1024)(128)(2,1)S(1)}, bf16[5120]{0:T(1024)(128)(2,1)}, u32[]{:S(2)}) copy-start(bf16[5120]{0:T(1024)(128)(2,1)} %param.12) | copy-start | bytes 30724
  4.2 9.7 %collective-permute-start = (bf16[96,640]{1,0:T(8,128)(2,1)S(1)}, bf16[96,640]{1,0:T(8,128)(2,1)S(1)}, u32[]{:S(2)}, u32[]{:S(2)}) collective-permute-start(bf16[96,640]{1,0:T(8,128)(2,1)S(1)} %fusion.6), channel_id=1, source_target_pairs={{0,8},{8,0},{1,9},{9,1},{2,10},{10,2},{3,11},{11,3},{4,12},{12,4},... | collective-permute-start | bytes 368648 | tf_op jit(solution)/shard_map/ppermute | solution.py:34
  15.5 7.2 %collective-permute-start.1 = (bf16[160,384]{1,0:T(8,128)(2,1)S(1)}, bf16[160,384]{1,0:T(8,128)(2,1)S(1)}, u32[]{:S(2)}, u32[]{:S(2)}) collective-permute-start(bf16[160,384]{1,0:T(8,128)(2,1)S(1)} %pad_maximum_fusion.1), channel_id=1, source_target_pairs={{0,16},{8,56},{16,32},{24,8},{32,48},{40,24},{48,0},{56,40},{64,80... | collective-permute-start | bytes 368648 | tf_op jit(solution)/shard_map/ppermute | solution.py:225
  17.4 7.0 %collective-permute-start.2 = (bf16[160,384]{1,0:T(8,128)(2,1)S(1)}, bf16[160,384]{1,0:T(8,128)(2,1)S(1)}, u32[]{:S(2)}, u32[]{:S(2)}) collective-permute-start(bf16[160,384]{1,0:T(8,128)(2,1)S(1)} %pad_maximum_fusion.1), channel_id=1, source_target_pairs={{0,48},{8,24},{16,0},{24,40},{32,16},{40,56},{48,32},{56,8},{64,11... | collective-permute-start | bytes 368648 | tf_op jit(solution)/shard_map/ppermute | solution.py:225
  20.8 7.1 %collective-permute-start.3 = (bf16[160,384]{1,0:T(8,128)(2,1)S(1)}, bf16[160,384]{1,0:T(8,128)(2,1)S(1)}, u32[]{:S(2)}, u32[]{:S(2)}) collective-permute-start(bf16[160,384]{1,0:T(8,128)(2,1)S(1)} %pad_maximum_fusion.1), channel_id=1, source_target_pairs={{0,32},{8,40},{16,48},{24,56},{32,0},{40,8},{48,16},{56,24},{64,96... | collective-permute-start | bytes 368648 | tf_op jit(solution)/shard_map/ppermute | solution.py:225
  28.0 12.1 %collective-permute-start.4 = (bf16[640,384]{1,0:T(8,128)(2,1)S(1)}, bf16[640,384]{1,0:T(8,128)(2,1)S(1)}, u32[]{:S(2)}, u32[]{:S(2)}) collective-permute-start(bf16[640,384]{1,0:T(8,128)(2,1)S(1)} %constant_dynamic-update-slice_fusion.refs_4_), channel_id=1, source_target_pairs={{0,64},{8,456},{16,80},{24,472},{32,96},{40,488},{48,112},{56,504}... | collective-permute-start | bytes 1474568 | tf_op jit(solution)/shard_map/ppermute | solution.py:225
  34.3 26.0 %all-to-all-start = ((bf16[8,176,256]{2,1,0:T(8,128)(2,1)}), bf16[8,176,256]{2,1,0:T(8,128)(2,1)S(1)}, u32[]{:S(2)}, u32[]{:S(2)}) async-start(bf16[8,176,256]{2,1,0:T(8,128)(2,1)} %broadcast_in_dim.58), calls=%async_computation | async-start | bytes 1441792 | tf_op jit(solution)/shard_map/all_to_all | solution.py:237
  43.4 57.3 %collective-permute-start.5 = (bf16[256,5120]{1,0:T(8,128)(2,1)S(1)}, bf16[256,5120]{1,0:T(8,128)(2,1)}, u32[]{:S(2)}, u32[]{:S(2)}) collective-permute-start(bf16[256,5120]{1,0:T(8,128)(2,1)S(1)} %bitcast.33), channel_id=1, source_target_pairs={{0,8},{8,0},{1,9},{9,1},{2,10},{10,2},{3,11},{11,3},{4,12},{12,4},... | collective-permute-start | bytes 7864328 | tf_op jit(solution)/shard_map/ppermute | solution.py:34
  51.5 14.7 %collective-permute-start.9 = (bf16[640,384]{1,0:T(8,128)(2,1)}, bf16[640,384]{1,0:T(8,128)(2,1)}, u32[]{:S(2)}, u32[]{:S(2)}) collective-permute-start(bf16[640,384]{1,0:T(8,128)(2,1)} %copy-done.2), channel_id=1, source_target_pairs={{0,448},{8,72},{16,464},{24,88},{32,480},{40,104},{48,496},{56,120... | collective-permute-start | bytes 1474568 | tf_op jit(solution)/shard_map/ppermute | solution.py:225
  53.5 16.0 %collective-permute-start.10 = (bf16[640,384]{1,0:T(8,128)(2,1)}, bf16[640,384]{1,0:T(8,128)(2,1)}, u32[]{:S(2)}, u32[]{:S(2)}) collective-permute-start(bf16[640,384]{1,0:T(8,128)(2,1)} %copy-done.4), channel_id=1, source_target_pairs={{0,64},{8,456},{16,80},{24,472},{32,96},{40,488},{48,112},{56,504}... | collective-permute-start | bytes 1474568 | tf_op jit(solution)/shard_map/ppermute | solution.py:225
  60.4 30.0 %collective-permute-start.6 = (bf16[1408,256]{1,0:T(8,128)(2,1)S(1)}, bf16[1408,256]{1,0:T(8,128)(2,1)S(1)}, u32[]{:S(2)}, u32[]{:S(2)}) collective-permute-start(bf16[1408,256]{1,0:T(8,128)(2,1)S(1)} %bitcast.36), channel_id=1, source_target_pairs={{0,16},{8,56},{16,32},{24,8},{32,48},{40,24},{48,0},{56,40},{64,80... | collective-permute-start | bytes 2162696 | tf_op jit(solution)/shard_map/ppermute | solution.py:225
  66.3 11.0 %collective-permute-start.11 = (bf16[640,384]{1,0:T(8,128)(2,1)}, bf16[640,384]{1,0:T(8,128)(2,1)S(1)}, u32[]{:S(2)}, u32[]{:S(2)}) collective-permute-start(bf16[640,384]{1,0:T(8,128)(2,1)} %collective-permute-done.9.refs_6_), channel_id=1, source_target_pairs={{0,448},{8,72},{16,464},{24,88},{32,480},{40,104},{48,496},{56,120... | collective-permute-start | bytes 1474568 | tf_op jit(solution)/shard_map/ppermute | solution.py:225
  69.5 16.0 %collective-permute-start.12 = (bf16[640,384]{1,0:T(8,128)(2,1)}, bf16[640,384]{1,0:T(8,128)(2,1)S(1)}, u32[]{:S(2)}, u32[]{:S(2)}) collective-permute-start(bf16[640,384]{1,0:T(8,128)(2,1)} %collective-permute-done.10.refs_7_), channel_id=1, source_target_pairs={{0,64},{8,456},{16,80},{24,472},{32,96},{40,488},{48,112},{56,504}... | collective-permute-start | bytes 1474568 | tf_op jit(solution)/shard_map/ppermute | solution.py:225
  77.2 18.4 %collective-permute-start.13 = (bf16[640,384]{1,0:T(8,128)(2,1)S(1)}, bf16[640,384]{1,0:T(8,128)(2,1)S(1)}, u32[]{:S(2)}, u32[]{:S(2)}) collective-permute-start(bf16[640,384]{1,0:T(8,128)(2,1)S(1)} %collective-permute-done.11.refs_8_), channel_id=1, source_target_pairs={{0,448},{8,72},{16,464},{24,88},{32,480},{40,104},{48,496},{56,120... | collective-permute-start | bytes 1474568 | tf_op jit(solution)/shard_map/ppermute | solution.py:225
  79.2 36.8 %collective-permute-start.7 = (bf16[1408,256]{1,0:T(8,128)(2,1)S(1)}, bf16[1408,256]{1,0:T(8,128)(2,1)S(1)}, u32[]{:S(2)}, u32[]{:S(2)}) collective-permute-start(bf16[1408,256]{1,0:T(8,128)(2,1)S(1)} %bitcast.37), channel_id=1, source_target_pairs={{0,48},{8,24},{16,0},{24,40},{32,16},{40,56},{48,32},{56,8},{64,11... | collective-permute-start | bytes 2162696 | tf_op jit(solution)/shard_map/ppermute | solution.py:225
  85.4 15.3 %collective-permute-start.14 = (bf16[640,384]{1,0:T(8,128)(2,1)S(1)}, bf16[640,384]{1,0:T(8,128)(2,1)S(1)}, u32[]{:S(2)}, u32[]{:S(2)}) collective-permute-start(bf16[640,384]{1,0:T(8,128)(2,1)S(1)} %collective-permute-done.12.refs_9_), channel_id=1, source_target_pairs={{0,64},{8,456},{16,80},{24,472},{32,96},{40,488},{48,112},{56,504}... | collective-permute-start | bytes 1474568 | tf_op jit(solution)/shard_map/ppermute | solution.py:225
  90.4 25.6 %collective-permute-start.8 = (bf16[1408,256]{1,0:T(8,128)(2,1)S(1)}, bf16[1408,256]{1,0:T(8,128)(2,1)S(1)}, u32[]{:S(2)}, u32[]{:S(2)}) collective-permute-start(bf16[1408,256]{1,0:T(8,128)(2,1)S(1)} %collective-permute-done.6.refs_5_), channel_id=1, source_target_pairs={{0,16},{8,56},{16,32},{24,8},{32,48},{40,24},{48,0},{56,40},{64,80... | collective-permute-start | bytes 2162696 | tf_op jit(solution)/shard_map/ppermute | solution.py:225
  108.2 14.6 %collective-permute-start.16 = (bf16[256,384]{1,0:T(8,128)(2,1)S(1)}, bf16[256,384]{1,0:T(8,128)(2,1)S(1)}, u32[]{:S(2)}, u32[]{:S(2)}) collective-permute-start(bf16[256,384]{1,0:T(8,128)(2,1)S(1)} %get-tuple-element.18), channel_id=1, source_target_pairs={{0,8},{8,0},{1,9},{9,1},{2,10},{10,2},{3,11},{11,3},{4,12},{12,4},... | collective-permute-start | bytes 589832 | tf_op jit(solution)/shard_map/ppermute | solution.py:34
  119.6 23.2 %copy-start.6 = (bf16[1,640]{1,0:T(2,128)(2,1)S(1)}, bf16[1,640]{1,0:T(2,128)(2,1)}, u32[]{:S(2)}) copy-start(bf16[1,640]{1,0:T(2,128)(2,1)} %query_ref.1) | copy-start | bytes 3844
  119.6 3.2 %collective-permute-start.15 = (bf16[256,256]{1,0:T(8,128)(2,1)S(1)}, bf16[256,256]{1,0:T(8,128)(2,1)S(1)}, u32[]{:S(2)}, u32[]{:S(2)}) collective-permute-start(bf16[256,256]{1,0:T(8,128)(2,1)S(1)} %get-tuple-element.17), channel_id=1, source_target_pairs={{0,8},{8,0},{1,9},{9,1},{2,10},{10,2},{3,11},{11,3},{4,12},{12,4},... | collective-permute-start | bytes 393224 | tf_op jit(solution)/shard_map/ppermute | solution.py:34
  125.4 17.4 %all-to-all-start.1 = ((bf16[64,8,128]{2,1,0:T(8,128)(2,1)}), bf16[64,8,128]{2,1,0:T(8,128)(2,1)S(1)}, u32[]{:S(2)}, u32[]{:S(2)}) async-start(bf16[64,8,128]{2,1,0:T(8,128)(2,1)} %bitcast.16), calls=%async_computation.1 | async-start | bytes 262144 | tf_op jit(solution)/shard_map/all_to_all | solution.py:237
  144.0 15.8 %all-to-all-start.2 = ((bf16[64,8,128]{2,1,0:T(8,128)(2,1)}), bf16[64,8,128]{2,1,0:T(8,128)(2,1)S(1)}, u32[]{:S(2)}, u32[]{:S(2)}) async-start(bf16[64,8,128]{2,1,0:T(8,128)(2,1)} %shard_map.107), calls=%async_computation.2 | async-start | bytes 262144 | tf_op jit(solution)/shard_map/all_to_all | solution.py:237
  160.7 13.8 %all-to-all-start.3 = ((f32[8,8,80]{2,1,0:T(8,128)}), f32[8,8,80]{2,1,0:T(8,128)S(1)}, u32[]{:S(2)}, u32[]{:S(2)}) async-start(f32[8,8,80]{2,1,0:T(8,128)} %fusion.7), calls=%async_computation.3 | async-start | bytes 65536 | tf_op jit(solution)/shard_map/all_to_all | solution.py:237
  (10 other events, 90.7 us)

commit v4 on v2

--- a/solution.py
+++ b/solution.py
@@ -15,7 +15,6 @@
 GROUP = ("z", "x", "core")
 MIB = 1 << 20
 Z_CHIPS, X_CHIPS = 8, 4
-Z_RING, X_RING = (0, -1, 1, -2, 2, -3, 3, 4), (0, -1, 1, 2)
 TOP_PARTS, SUM_PARTS = 3, 2
 
 
@@ -39,69 +38,70 @@
     return [lax.rem(place_ref[axis] + sign * step + chips, chips) for step in ring]
 
 
-def project_kernel(split, place_ref, own_ref, other_ref, cos_ref, sin_ref, *refs):
-    a_refs, b_refs = refs[: len(X_RING)], refs[len(X_RING) : len(X_RING) + len(Z_RING)]
-    own_out, other_out, query_out, weight = refs[len(X_RING) + len(Z_RING) :]
-    core = place_ref[2]
+def a_kernel(place_ref, own_ref, other_ref, a_ref, total_out, query_out, weight):
     rows, depth = own_ref.shape
-    width = weight.shape[1]
-    half = depth // (2 * Z_CHIPS * X_CHIPS)
-    extra = a_refs[0].shape[0] // len(Z_RING) - 2 * half
-
-    def place(piece, at, chip, columns):
-        for part, whose in ((0, core), (1, 1 - core)):
-            to = pl.multiple_of((2 * chip + whose) * half, 16)
-            weight[pl.ds(to, half), columns] = piece[pl.ds(at + part * half, half), :]
-
-    for a_ref, x in zip(a_refs, around(place_ref, 1, X_CHIPS, X_RING)):
-        for z in range(Z_CHIPS):
-            chip = z * X_CHIPS + x
-            at = z * (2 * half + extra)
-            place(a_ref, at, chip, pl.ds(0, split))
-            tiles = a_ref[pl.ds(at + 2 * half, extra), :].astype(jnp.float32)
-            query_out[chip, pl.ds(pl.multiple_of(core * 8, 8), 8), :] = tiles[:8]
-            query_out[chip, pl.ds(pl.multiple_of(8 - core * 8, 8), 8), :] = tiles[8:16]
-    for b_ref, z in zip(b_refs, around(place_ref, 0, Z_CHIPS, Z_RING)):
-        for x in range(X_CHIPS):
-            place(b_ref, x * 2 * half, z * X_CHIPS + x, pl.ds(split, width - split))
-
-    chunk = 1024 if depth % 1024 == 0 else depth
+    chips = query_out.shape[0]
+    span, each = depth // chips, a_ref.shape[0] // chips
+    for chip in range(chips):
+        at = chip * each
+        weight[pl.ds(chip * span, span), :] = a_ref[pl.ds(at, span), :]
+        query_out[chip] = a_ref[pl.ds(at + span, each - span), :].astype(jnp.float32)
+    for part, rows_ref in enumerate((own_ref, other_ref)):
+        total_out[pl.ds(part * rows, rows), :] = jnp.dot(
+            rows_ref[...], weight[...], preferred_element_type=jnp.float32
+        )
+
+
+def b_total(place_ref, steps, rows_ref, blocks):
+    total = None
+    for block, z in zip(blocks, around(place_ref, 0, Z_CHIPS, steps)):
+        features = block.shape[0]
+        lanes = pl.ds(pl.multiple_of(z * features, HEAD_DIM), features)
+        product = jnp.dot(rows_ref[:, lanes], block[...], preferred_element_type=jnp.float32)
+        total = product if total is None else total + product
+    return total
+
+
+def b_kernel(steps, place_ref, own_ref, other_ref, *refs):
+    *blocks, total_out = refs
+    rows = own_ref.shape[0]
+    for part, rows_ref in enumerate((own_ref, other_ref)):
+        total_out[pl.ds(part * rows, rows), :] = b_total(place_ref, steps, rows_ref, blocks)
+
+
+def last_kernel(steps, place_ref, own_ref, other_ref, a_ref, b_ref, cos_ref, sin_ref, *refs):
+    *blocks, own_out, other_out = refs
+    rows = own_ref.shape[0]
     for part, (rows_ref, out) in enumerate(((own_ref, own_out), (other_ref, other_out))):
         span = pl.ds(part * rows, rows)
-        total = jnp.zeros((rows, width), jnp.float32)
-        for k in range(depth // chunk):
-            lanes = pl.ds(k * chunk, chunk)
-            total += jnp.dot(
-                rows_ref[:, lanes], weight[lanes, :], preferred_element_type=jnp.float32
-            )
         cosine, sine = cos_ref[span, :], sin_ref[span, :]
-        for head in range(width // HEAD_DIM):
-            value = total[:, head * HEAD_DIM : (head + 1) * HEAD_DIM]
-            turned = value * cosine + pltpu.roll(value, HEAD_DIM // 2, 1) * sine
-            out[:, pl.ds(head * HEAD_DIM, HEAD_DIM)] = turned.astype(out.dtype)
-
-
-def project(place, own, other, cosine, sine, a_blocks, b_blocks):
-    rows, depth = own.shape
-    split = a_blocks[0].shape[1]
-    width = split + b_blocks[0].shape[1]
-    out = jax.ShapeDtypeStruct((rows, width), jnp.bfloat16)
-    tiles = jax.ShapeDtypeStruct((Z_CHIPS * X_CHIPS, 16, split), jnp.float32)
+        rest = b_ref[span, :] + b_total(place_ref, steps, rows_ref, blocks)
+        at = 0
+        for total in (a_ref[span, :], rest):
+            for first in range(0, total.shape[1], HEAD_DIM):
+                value = total[:, first : first + HEAD_DIM]
+                turned = value * cosine + pltpu.roll(value, HEAD_DIM // 2, 1) * sine
+                out[:, pl.ds(at, HEAD_DIM)] = turned.astype(out.dtype)
+                at += HEAD_DIM
+
+
+def project(kernel, place, operands, blocks, out_shape, features, scratch=()):
     vmem = pl.BlockSpec(memory_space=pltpu.VMEM)
-    operands = (own, other, cosine, sine, *a_blocks, *b_blocks)
+    width = blocks[0].shape[1]
+    count = 2 * operands[0].shape[0]
     return pl.pallas_call(
-        functools.partial(project_kernel, split),
-        in_specs=[pl.BlockSpec(memory_space=pltpu.SMEM)] + [vmem] * len(operands),
-        out_specs=[vmem] * 3,
-        out_shape=[out, out, tiles],
-        scratch_shapes=[pltpu.VMEM((depth, width), jnp.bfloat16)],
-        compiler_params=pltpu.CompilerParams(vmem_limit_bytes=40 * MIB),
+        kernel,
+        in_specs=[pl.BlockSpec(memory_space=pltpu.SMEM)] + [vmem] * (len(operands) + len(blocks)),
+        out_specs=[vmem] * len(out_shape),
+        out_shape=out_shape,
+        scratch_shapes=scratch,
+        compiler_params=pltpu.CompilerParams(vmem_limit_bytes=32 * MIB),
         cost_estimate=pl.CostEstimate(
-            flops=4 * rows * depth * width,
-            bytes_accessed=4 * rows * depth + 2 * depth * width,
+            flops=2 * count * features * width,
+            bytes_accessed=2 * count * features + 2 * features * width,
             transcendentals=0,
         ),
-    )(place, *operands)
+    )(place, *operands, *blocks)
 
 
 def attend_kernel(place_ref, mine_ref, theirs_ref, query_ref, keys_ref, out_ref, tiles):
@@ -200,31 +200,18 @@
     )(parts, query, new_pair)
 
 
-def send(value, dz, dx):
+def send(value, step):
     pairs = []
     for z in range(Z_CHIPS):
         for x in range(X_CHIPS):
             for core, sign in ((0, 1), (1, -1)):
-                to = ((z + sign * dz) % Z_CHIPS * X_CHIPS + (x + sign * dx) % X_CHIPS) * 2 + core
+                to = ((z + sign * step) % Z_CHIPS * X_CHIPS + x) * 2 + core
                 pairs.append(((z * X_CHIPS + x) * 2 + core, to))
     return lax.ppermute(value, GROUP, pairs)
 
 
-def ring(value, chips, dz, dx):
-    behind, ahead, found = value, value, [value]
-    for _ in range(chips // 2 - 1):
-        behind, ahead = send(behind, dz, dx), send(ahead, -dz, -dx)
-        found += [behind, ahead]
-    return found + [send(behind, dz, dx)]
-
-
 def exchange(value, axis):
     return lax.all_to_all(value, axis, 0, 0, tiled=True)
-
-
-def collect(piece, axis, chips):
-    copies = jnp.broadcast_to(piece, (chips,) + piece.shape)
-    return exchange(copies, axis).reshape(chips * piece.shape[0], piece.shape[1])
 
 
 def per_device(
@@ -239,28 +226,35 @@
     first_core = core == 0
 
     split = 2 * HEAD_DIM
-    keep = jnp.where(first_core, kv_weight[:, 0], kv_weight[:, 1])
-    give = jnp.where(first_core, kv_weight[:, 1], kv_weight[:, 0])
-    numbers = jnp.broadcast_to(row_conv, (HEAD_DIM,)), jnp.pad(block_per_slot, (0, split - slot_dev))
-    conv_part, block_part = (part.astype(jnp.bfloat16)[None] for part in numbers)
-    wide = jnp.concatenate([queries, conv_part], axis=1)
-    rows = [wide[:, at : at + split] for at in range(0, wide.shape[1], split)] + [block_part]
-    notes = jnp.pad(jnp.concatenate(rows), ((0, 8 - len(rows)), (0, 0)))
-    sent = jnp.concatenate([give, jnp.pad(notes, ((0, 8), (0, local_width - split)))])
+    given = jnp.stack([kv_weight[:, kind, split:] for kind in (0, 1)])
+    given = jnp.broadcast_to(given, (X_CHIPS,) + given.shape)
+    block_b = exchange(given.reshape(-1, *given.shape[2:]), ("x", "core"))
+    block_b = block_b.reshape(-1, local_width - split)
+    keep = jnp.where(first_core, kv_weight[:, 0, :split], kv_weight[:, 1, :split])
+    give = jnp.where(first_core, kv_weight[:, 1, :split], kv_weight[:, 0, :split])
+    part_rows = keep.shape[0]
+    numbers = jnp.concatenate([row_conv, block_per_slot]).astype(jnp.bfloat16)
+    numbers = jnp.broadcast_to(numbers[:, None], (1 + slot_dev, split))
+    wide = jnp.concatenate([queries, numbers[:1, :HEAD_DIM]], axis=1)
+    lines = [wide[:, at : at + split] for at in range(0, wide.shape[1], split)]
+    notes = jnp.concatenate([*lines, numbers[1:]])
+    notes = jnp.pad(notes, ((0, 8 - notes.shape[0]), (0, 0)))
+    sent = jnp.concatenate([give, jnp.pad(notes, ((0, 8), (0, 0)))])
     got = swap_cores(sent)
-    part_rows = keep.shape[0]
-    got_notes = got[part_rows : part_rows + 8, :split]
-    piece_a = jnp.concatenate([keep[:, :split], got[:part_rows, :split], notes, got_notes])
-    piece_b = jnp.concatenate([keep[:, split:], got[:part_rows, split:]])
-    block_b = collect(piece_b, "x", X_CHIPS)
-    block_a = collect(piece_a, "z", Z_CHIPS)
+    got_notes = got[part_rows : part_rows + 8]
+    got = got[:part_rows]
+    first = jnp.where(first_core, keep, got), jnp.where(first_core, notes, got_notes)
+    second = jnp.where(first_core, got, keep), jnp.where(first_core, got_notes, notes)
+    piece_a = jnp.concatenate([first[0], second[0], first[1], second[1]])
+    all_a = lax.all_gather(piece_a, ("z", "x"), axis=0, tiled=True)
     saved, block_b = lax.optimization_barrier((saved, block_b))
-    b_blocks = ring(block_b, Z_CHIPS, 1, 0)
-    a_blocks = ring(block_a, X_CHIPS, 0, 1)
+    behind1, ahead1 = send(block_b, 1), send(block_b, -1)
+    behind2, ahead2 = send(behind1, 1), send(ahead1, -1)
+    behind3, ahead3 = send(behind2, 1), send(ahead2, -1)
 
     normed = normalize(saved, norm_gain).reshape(slot_dev * block_rows, model_width)
     other_normed = swap_cores(normed)
-    other_blocks = got_notes[len(rows) - 1, :slot_dev]
+    other_blocks = got_notes[len(lines) : len(lines) + slot_dev, 0]
     blocks = jnp.concatenate([block_per_slot, other_blocks.astype(jnp.int32)])
     conv = blocks // blocks_conv
     positions = (blocks % blocks_conv * block_rows)[:, None] + jnp.arange(
@@ -280,10 +274,30 @@
     key_conv = jnp.broadcast_to(key_conv.astype(jnp.float32), (8, own_rows))
     place = jnp.stack([lax.axis_index("z"), lax.axis_index("x"), core]).astype(jnp.int32)
 
-    mine, for_other, tiles = project(
-        place, normed, other_normed, cosine, sine, a_blocks, b_blocks
-    )
-    theirs = swap_cores(for_other)
+    rows, count = (normed, other_normed), 2 * own_rows
+    shapes = [(count, local_width - split), (count, split), (Z_CHIPS * X_CHIPS, 16, split)]
+    b_out, a_out, query_out = (jax.ShapeDtypeStruct(shape, jnp.float32) for shape in shapes)
+    early, late = (0, -1, 1, -2, 2), (-3, 3, 4)
+    features = model_width // Z_CHIPS
+    blocks = (block_b, behind1, ahead1, behind2, ahead2)
+    (b_part,) = project(
+        functools.partial(b_kernel, early), place, rows, blocks, [b_out], len(early) * features
+    )
+    behind3, b_part = lax.optimization_barrier((behind3, b_part))
+    weight = pltpu.VMEM((model_width, split), jnp.bfloat16)
+    outs = [a_out, query_out]
+    a_part, tiles = project(a_kernel, place, rows, (all_a,), outs, model_width, (weight,))
+    blocks = (behind3, ahead3, send(behind3, 1))
+    out = jax.ShapeDtypeStruct((own_rows, local_width), jnp.bfloat16)
+    mine, give = project(
+        functools.partial(last_kernel, late),
+        place,
+        (*rows, a_part, b_part, cosine, sine),
+        blocks,
+        [out, out],
+        len(late) * features,
+    )
+    theirs = swap_cores(give)
     parts = attend(place, mine, theirs, tiles, key_conv).reshape(groups, 8, HEAD_DIM)
     merged = merge(exchange(parts, GROUP), queries, new_kv[0])
     attended = exchange(merged, GROUP)[:, :heads].reshape(groups, local_width)

time: 167 us -> 182 us (1.090)
  between operations: 1.67 us -> 15.1 us
  starting transfers between devices: 68.1 us -> 58.9 us
  Pallas kernels: 10.4 us -> 14.1 us
  waiting for transfers between devices: 51 us -> 54.4 us
  local copies, waits for them, and re-layouts: 6.91 us -> 10.1 us
    all_gather x0 -> x1, waiting for transfers between devices: none -> 14.1 us  [per_device(): all_a = lax.all_gather(piece_a, ('z', 'x'), axis=0, tiled=True)]
    ppermute x10 -> x7, waiting for transfers between devices: 26.2 us -> 16.2 us  [send(): return lax.ppermute(value, GROUP, pairs)]
    all_to_all x4 -> x3, starting transfers between devices: 20 us -> 14.4 us  [exchange(): return lax.all_to_all(value, axis, 0, 0, tiled=True)]
    ppermute x10 -> x7, starting transfers between devices: 32.9 us -> 28.1 us  [send(): return lax.ppermute(value, GROUP, pairs)]
    pallas_call x1 -> x3, Pallas kernels: 7.28 us -> 11 us  [project(): pl.pallas_call(kernel, in_specs=[pl.BlockSpec(memory_space=pltpu.SMEM)] +...]
    unnamed x20 -> x28, local copies, waits for them, and re-layouts: 1.88 us -> 4.95 us
    all_to_all x4 -> x3, waiting for transfers between devices: 22.8 us -> 23 us  [exchange(): return lax.all_to_all(value, axis, 0, 0, tiled=True)]
  transfers between devices with their start and end apart: 17 -> 14, of which waited for: 10 -> 8; matrix products, arithmetic and copies ran while one was open for 5% -> 6% of each run, Pallas kernels for 0% -> 4%
where the time goes in v4:
time: 182 us; the launch traced here: 181 us
  starting transfers between devices  58.9 us (32%)
  waiting for transfers between devices  54.4 us (30%)
  blocking collectives  18 us (10%)
  between operations  15.1 us (8%)
  Pallas kernels  14.1 us (8%)
  local copies, waits for them, and re-layouts  10.1 us (6%)
  other arithmetic  9.64 us (5%)
    ppermute x7, starting transfers between devices, send(): return lax.ppermute(value, GROUP, pairs)  28.1 us
    all_to_all x3, waiting for transfers between devices, exchange(): return lax.all_to_all(value, axis, 0, 0, tiled=True)  23 us
    all_to_all x1, blocking collectives, exchange(): return lax.all_to_all(value, axis, 0, 0, tiled=True)  18 us
    ppermute x3, starting transfers between devices, swap_cores(): return lax.ppermute(value, 'core', [(0, 1), (1, 0)])  16.4 us
    ppermute x7, waiting for transfers between devices, send(): return lax.ppermute(value, GROUP, pairs)  16.2 us
    all_to_all x3, starting transfers between devices, exchange(): return lax.all_to_all(value, axis, 0, 0, tiled=True)  14.4 us
    all_gather x1, waiting for transfers between devices, per_device(): all_a = lax.all_gather(piece_a, ('z', 'x'), axis=0, tiled=True)  14.1 us
    pallas_call x3, Pallas kernels, project(): pl.pallas_call(kernel, in_specs=[pl.BlockSpec(memory_space=pltpu.SMEM)] +...  11 us
  transfers between devices with their start and end apart: 14, of which 8 were waited for; matrix products, arithmetic and copies ran while one was open for 6% of the time, Pallas kernels for 4%

profile of v4, /device:TPU:1, one launch (start us, length us, event | category | flops | bytes accessed | tf_op | source)
XLA Modules:
  0.0 181.1 jit_solution(3515047229493524103)
XLA Ops:
  10.7 8.8 %collective-permute-start.1 = (bf16[96,256]{1,0:T(8,128)(2,1)S(1)}, bf16[96,256]{1,0:T(8,128)(2,1)S(1)}, u32[]{:S(2)}, u32[]{:S(2)}) collective-permute-start(bf16[96,256]{1,0:T(8,128)(2,1)S(1)} %fusion.9), channel_id=1, source_target_pairs={{0,8},{8,0},{1,9},{9,1},{2,10},{10,2},{3,11},{11,3},{4,12},{12,4},... | collective-permute-start | bytes 147464 | tf_op jit(solution)/shard_map/ppermute | solution.py:33
  22.3 3.4 %all-to-all-start = ((bf16[8,80,384]{2,1,0:T(8,128)(2,1)}), bf16[8,80,384]{2,1,0:T(8,128)(2,1)S(1)}, u32[]{:S(2)}, u32[]{:S(2)}) async-start(bf16[8,80,384]{2,1,0:T(8,128)(2,1)} %bitcast.41), calls=%async_computation | async-start | bytes 983040 | tf_op jit(solution)/shard_map/all_to_all | solution.py:214
  25.8 9.1 %all-to-all-done = bf16[8,80,384]{2,1,0:T(8,128)(2,1)S(1)} async-done(((bf16[8,80,384]{2,1,0:T(8,128)(2,1)}), bf16[8,80,384]{2,1,0:T(8,128)(2,1)S(1)}, u32[]{:S(2)}, u32[]{:S(2)}) %all-to-all-start) | async-done | bytes 491552 | tf_op jit(solution)/shard_map/all_to_all | solution.py:214
  37.6 2.8 %collective-permute-start = (bf16[256,5120]{1,0:T(8,128)(2,1)S(1)}, bf16[256,5120]{1,0:T(8,128)(2,1)}, u32[]{:S(2)}, u32[]{:S(2)}) collective-permute-start(bf16[256,5120]{1,0:T(8,128)(2,1)S(1)} %bitcast.32), channel_id=1, source_target_pairs={{0,8},{8,0},{1,9},{9,1},{2,10},{10,2},{3,11},{11,3},{4,12},{12,4},... | collective-permute-start | bytes 7864328 | tf_op jit(solution)/shard_map/ppermute | solution.py:33
  40.4 6.3 %collective-permute-start.2 = (bf16[640,384]{1,0:T(8,128)(2,1)S(1)}, bf16[640,384]{1,0:T(8,128)(2,1)}, u32[]{:S(2)}, u32[]{:S(2)}) collective-permute-start(bf16[640,384]{1,0:T(8,128)(2,1)S(1)} %bitcast.36), channel_id=1, source_target_pairs={{0,64},{8,456},{16,80},{24,472},{32,96},{40,488},{48,112},{56,504}... | collective-permute-start | bytes 1474568 | tf_op jit(solution)/shard_map/ppermute | solution.py:210
  46.7 1.9 %collective-permute-start.5 = (bf16[640,384]{1,0:T(8,128)(2,1)S(1)}, bf16[640,384]{1,0:T(8,128)(2,1)S(1)}, u32[]{:S(2)}, u32[]{:S(2)}) collective-permute-start(bf16[640,384]{1,0:T(8,128)(2,1)S(1)} %bitcast.37), channel_id=1, source_target_pairs={{0,448},{8,72},{16,464},{24,88},{32,480},{40,104},{48,496},{56,120... | collective-permute-start | bytes 1474568 | tf_op jit(solution)/shard_map/ppermute | solution.py:210
  48.6 8.6 %collective-permute-done.2.refs_1_ = bf16[640,384]{1,0:T(8,128)(2,1)} collective-permute-done((bf16[640,384]{1,0:T(8,128)(2,1)S(1)}, bf16[640,384]{1,0:T(8,128)(2,1)}, u32[]{:S(2)}, u32[]{:S(2)}) %collective-permute-start.2) | collective-permute-done | bytes 491552 | tf_op jit(solution)/shard_map/ppermute | solution.py:210
  57.2 5.3 %collective-permute-start.3 = (bf16[640,384]{1,0:T(8,128)(2,1)}, bf16[640,384]{1,0:T(8,128)(2,1)S(1)}, u32[]{:S(2)}, u32[]{:S(2)}) collective-permute-start(bf16[640,384]{1,0:T(8,128)(2,1)} %collective-permute-done.2.refs_1_), channel_id=1, source_target_pairs={{0,64},{8,456},{16,80},{24,472},{32,96},{40,488},{48,112},{56,504}... | collective-permute-start | bytes 1474568 | tf_op jit(solution)/shard_map/ppermute | solution.py:210
  62.9 1.9 %collective-permute-start.6 = (bf16[640,384]{1,0:T(8,128)(2,1)S(1)}, bf16[640,384]{1,0:T(8,128)(2,1)}, u32[]{:S(2)}, u32[]{:S(2)}) collective-permute-start(bf16[640,384]{1,0:T(8,128)(2,1)S(1)} %collective-permute-done.5.refs_2_), channel_id=1, source_target_pairs={{0,448},{8,72},{16,464},{24,88},{32,480},{40,104},{48,496},{56,120... | collective-permute-start | bytes 1474568 | tf_op jit(solution)/shard_map/ppermute | solution.py:210
  64.8 6.0 %collective-permute-done.3.refs_3_ = bf16[640,384]{1,0:T(8,128)(2,1)S(1)} collective-permute-done((bf16[640,384]{1,0:T(8,128)(2,1)}, bf16[640,384]{1,0:T(8,128)(2,1)S(1)}, u32[]{:S(2)}, u32[]{:S(2)}) %collective-permute-start.3) | collective-permute-done | bytes 491552 | tf_op jit(solution)/shard_map/ppermute | solution.py:210
  70.8 5.3 %collective-permute-start.4 = (bf16[640,384]{1,0:T(8,128)(2,1)S(1)}, bf16[640,384]{1,0:T(8,128)(2,1)}, u32[]{:S(2)}, u32[]{:S(2)}) collective-permute-start(bf16[640,384]{1,0:T(8,128)(2,1)S(1)} %collective-permute-done.3.refs_3_), channel_id=1, source_target_pairs={{0,64},{8,456},{16,80},{24,472},{32,96},{40,488},{48,112},{56,504}... | collective-permute-start | bytes 1474568 | tf_op jit(solution)/shard_map/ppermute | solution.py:210
  77.4 1.9 %collective-permute-start.7 = (bf16[640,384]{1,0:T(8,128)(2,1)}, bf16[640,384]{1,0:T(8,128)(2,1)}, u32[]{:S(2)}, u32[]{:S(2)}) collective-permute-start(bf16[640,384]{1,0:T(8,128)(2,1)} %collective-permute-done.6.refs_4_), channel_id=1, source_target_pairs={{0,448},{8,72},{16,464},{24,88},{32,480},{40,104},{48,496},{56,120... | collective-permute-start | bytes 1474568 | tf_op jit(solution)/shard_map/ppermute | solution.py:210
  80.3 4.0 %shard_map.105.b_ref = f32[512,384]{1,0:T(8,128)S(1)} custom-call(s32[3]{0:T(128)S(1)} %pad_add_fusion.place_ref, bf16[256,5120]{1,0:T(8,128)(2,1)S(1)} %bitcast.33, bf16[256,5120]{1,0:T(8,128)(2,1)} %collective-permute-done.other_ref, bf16[640,384]{1,0:T(8,128)(2,1)S(1)} %bitcast.38, bf16[640,384]{1,0:T(8,128)(2,1)} %collective-permute-done.2.refs_1_, ...), custom_call_target="tpu_custom_call" | custom-call | flops 1258291200 | bytes 5734400 | tf_op jit(solution)/shard_map/pallas_call | solution.py:92
  86.0 5.4 %collective-permute-start.8 = (bf16[640,384]{1,0:T(8,128)(2,1)}, bf16[640,384]{1,0:T(8,128)(2,1)}, u32[]{:S(2)}, u32[]{:S(2)}) collective-permute-start(bf16[640,384]{1,0:T(8,128)(2,1)} %collective-permute-done.4.refs_0_), channel_id=1, source_target_pairs={{0,64},{8,456},{16,80},{24,472},{32,96},{40,488},{48,112},{56,504}... | collective-permute-start | bytes 1474568 | tf_op jit(solution)/shard_map/ppermute | solution.py:210
  92.6 14.1 %all-gather.2.cloned.1.call-done.a_ref = bf16[5632,256]{1,0:T(8,128)(2,1)} async-done(((bf16[176,256]{1,0:T(8,128)(2,1)}), bf16[5632,256]{1,0:T(8,128)(2,1)}) %all-gather.2.cloned.1.call-update) | async-done | bytes 2883600 | tf_op jit(solution)/shard_map/all_gather | solution.py:249
  108.5 3.4 %shard_map.104 = (f32[512,256]{1,0:T(8,128)S(1)}, f32[32,16,256]{2,1,0:T(8,128)S(1)}) custom-call(s32[3]{0:T(128)S(1)} %pad_add_fusion.place_ref, bf16[256,5120]{1,0:T(8,128)(2,1)S(1)} %bitcast.34, bf16[256,5120]{1,0:T(8,128)(2,1)} %collective-permute-done.other_ref, bf16[5632,256]{1,0:T(8,128)(2,1)S(1)} %copy-done.1), custom_call_target="tpu_custom_call" | custom-call | flops 1342177280 | bytes 7864320 | tf_op jit(solution)/shard_map/pallas_call | solution.py:92
  111.9 3.6 %shard_map.106 = (bf16[256,640]{1,0:T(8,128)(2,1)S(1)}, bf16[256,640]{1,0:T(8,128)(2,1)S(1)}) custom-call(s32[3]{0:T(128)S(1)} %pad_add_fusion.place_ref, bf16[256,5120]{1,0:T(8,128)(2,1)S(1)} %bitcast.35, bf16[256,5120]{1,0:T(8,128)(2,1)} %collective-permute-done.other_ref, f32[512,256]{1,0:T(8,128)S(1)} %get-tuple-element.11.a_ref, ...), custom_call_target="tpu_custom_call" | custom-call | flops 754974720 | bytes 3440640 | tf_op jit(solution)/shard_map/pallas_call | solution.py:92
  115.6 4.9 %collective-permute-start.9 = (bf16[256,640]{1,0:T(8,128)(2,1)S(1)}, bf16[256,640]{1,0:T(8,128)(2,1)S(1)}, u32[]{:S(2)}, u32[]{:S(2)}) collective-permute-start(bf16[256,640]{1,0:T(8,128)(2,1)S(1)} %get-tuple-element.16), channel_id=1, source_target_pairs={{0,8},{8,0},{1,9},{9,1},{2,10},{10,2},{3,11},{11,3},{4,12},{12,4},... | collective-permute-start | bytes 983048 | tf_op jit(solution)/shard_map/ppermute | solution.py:33
  124.3 18.0 %all_to_all.20.parts_ref = bf16[64,8,128]{2,1,0:T(8,128)(2,1)S(1)} all-to-all(bf16[64,8,128]{2,1,0:T(8,128)(2,1)S(1)} %bitcast.39), channel_id=1, replica_groups=mesh['z'=8,'x'=4,'core'=2,'tp'=8] {'z','x','core'}, dimensions={0} | all-to-all | bytes 262144 | tf_op jit(solution)/shard_map/all_to_all | solution.py:214
  143.5 4.6 %all-to-all-start.2 = ((bf16[64,8,128]{2,1,0:T(8,128)(2,1)}), bf16[64,8,128]{2,1,0:T(8,128)(2,1)S(1)}, u32[]{:S(2)}, u32[]{:S(2)}) async-start(bf16[64,8,128]{2,1,0:T(8,128)(2,1)} %shard_map.108), calls=%async_computation.2 | async-start | bytes 262144 | tf_op jit(solution)/shard_map/all_to_all | solution.py:214
  150.2 9.3 %all-to-all-done.2 = bf16[64,8,128]{2,1,0:T(8,128)(2,1)S(1)} async-done(((bf16[64,8,128]{2,1,0:T(8,128)(2,1)}), bf16[64,8,128]{2,1,0:T(8,128)(2,1)S(1)}, u32[]{:S(2)}, u32[]{:S(2)}) %all-to-all-start.2) | async-done | bytes 131104 | tf_op jit(solution)/shard_map/all_to_all | solution.py:214
  160.4 6.3 %all-to-all-start.3 = ((f32[8,8,80]{2,1,0:T(8,128)}), f32[8,8,80]{2,1,0:T(8,128)S(1)}, u32[]{:S(2)}, u32[]{:S(2)}) async-start(f32[8,8,80]{2,1,0:T(8,128)} %fusion.5), calls=%async_computation.3 | async-start | bytes 65536 | tf_op jit(solution)/shard_map/all_to_all | solution.py:214
  166.7 2.3 %pad_maximum_fusion = bf16[2,128,2,640]{3,2,1,0:T(2,128)(2,1)} fusion(bf16[2,128,1,640]{3,2,1,0:T(2,128)(2,1)S(1)} %copy.27, bf16[2,128,1,640]{3,2,1,0:T(2,128)(2,1)S(1)} %copy.26), kind=kLoop, calls=%fused_computation.5 | loop fusion | flops 1310720 | bytes 1310720 | tf_op jit(solution)/shard_map/stack | solution.py:311
  169.0 4.6 %all-to-all-done.3 = f32[8,8,80]{2,1,0:T(8,128)S(1)} async-done(((f32[8,8,80]{2,1,0:T(8,128)}), f32[8,8,80]{2,1,0:T(8,128)S(1)}, u32[]{:S(2)}, u32[]{:S(2)}) %all-to-all-start.3) | async-done | bytes 20512 | tf_op jit(solution)/shard_map/all_to_all | solution.py:214
  (79 shorter events, 24.1 us)
Async XLA Ops:
  7.2 152.5 %copy-start = (bf16[640,80]{0,1:T(8,128)(2,1)S(1)}, bf16[640,80]{0,1:T(8,128)(2,1)}, u32[]{:S(2)}) copy-start(bf16[640,80]{0,1:T(8,128)(2,1)} %param.14) | copy-start | bytes 307204
  7.2 18.6 %copy-start.11 = (bf16[5120]{0:T(1024)(128)(2,1)S(1)}, bf16[5120]{0:T(1024)(128)(2,1)}, u32[]{:S(2)}) copy-start(bf16[5120]{0:T(1024)(128)(2,1)} %param.12) | copy-start | bytes 30724
  7.2 27.7 %copy-start.9 = (bf16[2,128,5120]{2,1,0:T(8,128)(2,1)S(1)}, bf16[2,128,5120]{2,1,0:T(8,128)(2,1)}, u32[]{:S(2)}) copy-start(bf16[2,128,5120]{2,1,0:T(8,128)(2,1)} %param.9) | copy-start | bytes 7864324
  7.2 99.5 %all-gather.2.cloned.1.call-start = ((), (), s32[]{:S(2)}) async-start(), calls=%async_computation.4 | async-start | bytes 2973696 | tf_op jit(solution)/shard_map/all_gather | solution.py:249
  10.7 10.0 %collective-permute-start.1 = (bf16[96,256]{1,0:T(8,128)(2,1)S(1)}, bf16[96,256]{1,0:T(8,128)(2,1)S(1)}, u32[]{:S(2)}, u32[]{:S(2)}) collective-permute-start(bf16[96,256]{1,0:T(8,128)(2,1)S(1)} %fusion.9), channel_id=1, source_target_pairs={{0,8},{8,0},{1,9},{9,1},{2,10},{10,2},{3,11},{11,3},{4,12},{12,4},... | collective-permute-start | bytes 147464 | tf_op jit(solution)/shard_map/ppermute | solution.py:33
  22.3 12.5 %all-to-all-start = ((bf16[8,80,384]{2,1,0:T(8,128)(2,1)}), bf16[8,80,384]{2,1,0:T(8,128)(2,1)S(1)}, u32[]{:S(2)}, u32[]{:S(2)}) async-start(bf16[8,80,384]{2,1,0:T(8,128)(2,1)} %bitcast.41), calls=%async_computation | async-start | bytes 983040 | tf_op jit(solution)/shard_map/all_to_all | solution.py:214
  34.9 11.8 %copy-start.2 = (bf16[8,80,384]{2,1,0:T(8,128)(2,1)}, bf16[8,80,384]{2,1,0:T(8,128)(2,1)S(1)}, u32[]{:S(2)}) copy-start(bf16[8,80,384]{2,1,0:T(8,128)(2,1)S(1)} %all-to-all-done) | copy-start | bytes 1474564
  36.8 25.9 %copy-start.12 = (s32[2]{0:T(128)S(1)}, s32[2]{0:T(128)}, u32[]{:S(2)}) copy-start(s32[2]{0:T(128)} %param.10) | copy-start | bytes 28
  36.8 39.4 %copy-start.13 = (s32[4]{0:T(128)S(1)}, s32[4]{0:T(128)}, u32[]{:S(2)}) copy-start(s32[4]{0:T(128)} %param.11) | copy-start | bytes 52
  37.6 41.7 %collective-permute-start = (bf16[256,5120]{1,0:T(8,128)(2,1)S(1)}, bf16[256,5120]{1,0:T(8,128)(2,1)}, u32[]{:S(2)}, u32[]{:S(2)}) collective-permute-start(bf16[256,5120]{1,0:T(8,128)(2,1)S(1)} %bitcast.32), channel_id=1, source_target_pairs={{0,8},{8,0},{1,9},{9,1},{2,10},{10,2},{3,11},{11,3},{4,12},{12,4},... | collective-permute-start | bytes 7864328 | tf_op jit(solution)/shard_map/ppermute | solution.py:33
  40.4 16.8 %collective-permute-start.2 = (bf16[640,384]{1,0:T(8,128)(2,1)S(1)}, bf16[640,384]{1,0:T(8,128)(2,1)}, u32[]{:S(2)}, u32[]{:S(2)}) collective-permute-start(bf16[640,384]{1,0:T(8,128)(2,1)S(1)} %bitcast.36), channel_id=1, source_target_pairs={{0,64},{8,456},{16,80},{24,472},{32,96},{40,488},{48,112},{56,504}... | collective-permute-start | bytes 1474568 | tf_op jit(solution)/shard_map/ppermute | solution.py:210
  46.7 16.2 %collective-permute-start.5 = (bf16[640,384]{1,0:T(8,128)(2,1)S(1)}, bf16[640,384]{1,0:T(8,128)(2,1)S(1)}, u32[]{:S(2)}, u32[]{:S(2)}) collective-permute-start(bf16[640,384]{1,0:T(8,128)(2,1)S(1)} %bitcast.37), channel_id=1, source_target_pairs={{0,448},{8,72},{16,464},{24,88},{32,480},{40,104},{48,496},{56,120... | collective-permute-start | bytes 1474568 | tf_op jit(solution)/shard_map/ppermute | solution.py:210
  57.2 13.5 %collective-permute-start.3 = (bf16[640,384]{1,0:T(8,128)(2,1)}, bf16[640,384]{1,0:T(8,128)(2,1)S(1)}, u32[]{:S(2)}, u32[]{:S(2)}) collective-permute-start(bf16[640,384]{1,0:T(8,128)(2,1)} %collective-permute-done.2.refs_1_), channel_id=1, source_target_pairs={{0,64},{8,456},{16,80},{24,472},{32,96},{40,488},{48,112},{56,504}... | collective-permute-start | bytes 1474568 | tf_op jit(solution)/shard_map/ppermute | solution.py:210
  62.9 14.5 %collective-permute-start.6 = (bf16[640,384]{1,0:T(8,128)(2,1)S(1)}, bf16[640,384]{1,0:T(8,128)(2,1)}, u32[]{:S(2)}, u32[]{:S(2)}) collective-permute-start(bf16[640,384]{1,0:T(8,128)(2,1)S(1)} %collective-permute-done.5.refs_2_), channel_id=1, source_target_pairs={{0,448},{8,72},{16,464},{24,88},{32,480},{40,104},{48,496},{56,120... | collective-permute-start | bytes 1474568 | tf_op jit(solution)/shard_map/ppermute | solution.py:210
  70.8 15.2 %collective-permute-start.4 = (bf16[640,384]{1,0:T(8,128)(2,1)S(1)}, bf16[640,384]{1,0:T(8,128)(2,1)}, u32[]{:S(2)}, u32[]{:S(2)}) collective-permute-start(bf16[640,384]{1,0:T(8,128)(2,1)S(1)} %collective-permute-done.3.refs_3_), channel_id=1, source_target_pairs={{0,64},{8,456},{16,80},{24,472},{32,96},{40,488},{48,112},{56,504}... | collective-permute-start | bytes 1474568 | tf_op jit(solution)/shard_map/ppermute | solution.py:210
  77.4 34.5 %collective-permute-start.7 = (bf16[640,384]{1,0:T(8,128)(2,1)}, bf16[640,384]{1,0:T(8,128)(2,1)}, u32[]{:S(2)}, u32[]{:S(2)}) collective-permute-start(bf16[640,384]{1,0:T(8,128)(2,1)} %collective-permute-done.6.refs_4_), channel_id=1, source_target_pairs={{0,448},{8,72},{16,464},{24,88},{32,480},{40,104},{48,496},{56,120... | collective-permute-start | bytes 1474568 | tf_op jit(solution)/shard_map/ppermute | solution.py:210
  86.0 25.9 %collective-permute-start.8 = (bf16[640,384]{1,0:T(8,128)(2,1)}, bf16[640,384]{1,0:T(8,128)(2,1)}, u32[]{:S(2)}, u32[]{:S(2)}) collective-permute-start(bf16[640,384]{1,0:T(8,128)(2,1)} %collective-permute-done.4.refs_0_), channel_id=1, source_target_pairs={{0,64},{8,456},{16,80},{24,472},{32,96},{40,488},{48,112},{56,504}... | collective-permute-start | bytes 1474568 | tf_op jit(solution)/shard_map/ppermute | solution.py:210
  108.5 3.4 %copy-start.5 = (f32[512,128]{1,0:T(8,128)S(1)}, f32[512,128]{1,0:T(8,128)}, u32[]{:S(2)}) copy-start(f32[512,128]{1,0:T(8,128)} %get-tuple-element.36.sin_ref) | copy-start | bytes 786436
  108.5 3.4 %copy-start.6 = (f32[512,128]{1,0:T(8,128)S(1)}, f32[512,128]{1,0:T(8,128)}, u32[]{:S(2)}) copy-start(f32[512,128]{1,0:T(8,128)} %get-tuple-element.37.cos_ref) | copy-start | bytes 786436
  111.9 30.4 %copy-start.7 = (bf16[1,640]{1,0:T(2,128)(2,1)S(1)}, bf16[1,640]{1,0:T(2,128)(2,1)}, u32[]{:S(2)}) copy-start(bf16[1,640]{1,0:T(2,128)(2,1)} %query_ref.1) | copy-start | bytes 3844
  111.9 30.4 %copy-start.8 = (bf16[1,2,640]{2,1,0:T(2,128)(2,1)S(1)}, bf16[1,2,640]{2,1,0:T(2,128)(2,1)}, u32[]{:S(2)}) copy-start(bf16[1,2,640]{2,1,0:T(2,128)(2,1)} %param.16) | copy-start | bytes 7684
  115.6 6.1 %collective-permute-start.9 = (bf16[256,640]{1,0:T(8,128)(2,1)S(1)}, bf16[256,640]{1,0:T(8,128)(2,1)S(1)}, u32[]{:S(2)}, u32[]{:S(2)}) collective-permute-start(bf16[256,640]{1,0:T(8,128)(2,1)S(1)} %get-tuple-element.16), channel_id=1, source_target_pairs={{0,8},{8,0},{1,9},{9,1},{2,10},{10,2},{3,11},{11,3},{4,12},{12,4},... | collective-permute-start | bytes 983048 | tf_op jit(solution)/shard_map/ppermute | solution.py:33
  143.5 16.0 %all-to-all-start.2 = ((bf16[64,8,128]{2,1,0:T(8,128)(2,1)}), bf16[64,8,128]{2,1,0:T(8,128)(2,1)S(1)}, u32[]{:S(2)}, u32[]{:S(2)}) async-start(bf16[64,8,128]{2,1,0:T(8,128)(2,1)} %shard_map.108), calls=%async_computation.2 | async-start | bytes 262144 | tf_op jit(solution)/shard_map/all_to_all | solution.py:214
  160.4 13.3 %all-to-all-start.3 = ((f32[8,8,80]{2,1,0:T(8,128)}), f32[8,8,80]{2,1,0:T(8,128)S(1)}, u32[]{:S(2)}, u32[]{:S(2)}) async-start(f32[8,8,80]{2,1,0:T(8,128)} %fusion.5), calls=%async_computation.3 | async-start | bytes 65536 | tf_op jit(solution)/shard_map/all_to_all | solution.py:214
  (4 other events, 5.5 us)
Sparse Core Ops, SparseCore 0:
  21.6 85.0 all-gather.1

commit v5 on v4

--- a/solution.py
+++ b/solution.py
@@ -15,6 +15,7 @@
 GROUP = ("z", "x", "core")
 MIB = 1 << 20
 Z_CHIPS, X_CHIPS = 8, 4
+X_RING = (0, -1, 1, 2)
 TOP_PARTS, SUM_PARTS = 3, 2
 
 
@@ -38,14 +39,18 @@
     return [lax.rem(place_ref[axis] + sign * step + chips, chips) for step in ring]
 
 
-def a_kernel(place_ref, own_ref, other_ref, a_ref, total_out, query_out, weight):
+def a_kernel(place_ref, own_ref, other_ref, *refs):
+    a_refs = refs[: len(X_RING)]
+    total_out, query_out, weight = refs[len(X_RING) :]
     rows, depth = own_ref.shape
-    chips = query_out.shape[0]
-    span, each = depth // chips, a_ref.shape[0] // chips
-    for chip in range(chips):
-        at = chip * each
-        weight[pl.ds(chip * span, span), :] = a_ref[pl.ds(at, span), :]
-        query_out[chip] = a_ref[pl.ds(at + span, each - span), :].astype(jnp.float32)
+    span = depth // (Z_CHIPS * X_CHIPS)
+    each = a_refs[0].shape[0] // Z_CHIPS
+    for ref, x in zip(a_refs, around(place_ref, 1, X_CHIPS, X_RING)):
+        for z in range(Z_CHIPS):
+            chip = z * X_CHIPS + x
+            weight[pl.ds(pl.multiple_of(chip * span, 16), span), :] = ref[pl.ds(z * each, span), :]
+            notes = ref[pl.ds(z * each + span, each - span), :]
+            query_out[chip] = notes.astype(jnp.float32)
     for part, rows_ref in enumerate((own_ref, other_ref)):
         total_out[pl.ds(part * rows, rows), :] = jnp.dot(
             rows_ref[...], weight[...], preferred_element_type=jnp.float32
@@ -200,12 +205,12 @@
     )(parts, query, new_pair)
 
 
-def send(value, step):
+def send(value, dz, dx):
     pairs = []
     for z in range(Z_CHIPS):
         for x in range(X_CHIPS):
             for core, sign in ((0, 1), (1, -1)):
-                to = ((z + sign * step) % Z_CHIPS * X_CHIPS + x) * 2 + core
+                to = ((z + sign * dz) % Z_CHIPS * X_CHIPS + (x + sign * dx) % X_CHIPS) * 2 + core
                 pairs.append(((z * X_CHIPS + x) * 2 + core, to))
     return lax.ppermute(value, GROUP, pairs)
 
@@ -228,6 +233,7 @@
     split = 2 * HEAD_DIM
     given = jnp.stack([kv_weight[:, kind, split:] for kind in (0, 1)])
     given = jnp.broadcast_to(given, (X_CHIPS,) + given.shape)
+    given, kv_weight, a_queries = lax.optimization_barrier((given, kv_weight, queries))
     block_b = exchange(given.reshape(-1, *given.shape[2:]), ("x", "core"))
     block_b = block_b.reshape(-1, local_width - split)
     keep = jnp.where(first_core, kv_weight[:, 0, :split], kv_weight[:, 1, :split])
@@ -235,7 +241,7 @@
     part_rows = keep.shape[0]
     numbers = jnp.concatenate([row_conv, block_per_slot]).astype(jnp.bfloat16)
     numbers = jnp.broadcast_to(numbers[:, None], (1 + slot_dev, split))
-    wide = jnp.concatenate([queries, numbers[:1, :HEAD_DIM]], axis=1)
+    wide = jnp.concatenate([a_queries, numbers[:1, :HEAD_DIM]], axis=1)
     lines = [wide[:, at : at + split] for at in range(0, wide.shape[1], split)]
     notes = jnp.concatenate([*lines, numbers[1:]])
     notes = jnp.pad(notes, ((0, 8 - notes.shape[0]), (0, 0)))
@@ -246,11 +252,14 @@
     first = jnp.where(first_core, keep, got), jnp.where(first_core, notes, got_notes)
     second = jnp.where(first_core, got, keep), jnp.where(first_core, got_notes, notes)
     piece_a = jnp.concatenate([first[0], second[0], first[1], second[1]])
-    all_a = lax.all_gather(piece_a, ("z", "x"), axis=0, tiled=True)
-    saved, block_b = lax.optimization_barrier((saved, block_b))
-    behind1, ahead1 = send(block_b, 1), send(block_b, -1)
-    behind2, ahead2 = send(behind1, 1), send(ahead1, -1)
-    behind3, ahead3 = send(behind2, 1), send(ahead2, -1)
+    copies_a = jnp.broadcast_to(piece_a, (Z_CHIPS,) + piece_a.shape)
+    saved, block_b, copies_a = lax.optimization_barrier((saved, block_b, copies_a))
+    block_a = exchange(copies_a, "z").reshape(-1, split)
+    a_behind, a_ahead = send(block_a, 0, 1), send(block_a, 0, -1)
+    a_blocks = (block_a, a_behind, a_ahead, send(a_behind, 0, 1))
+    behind1, ahead1 = send(block_b, 1, 0), send(block_b, -1, 0)
+    behind2, ahead2 = send(behind1, 1, 0), send(ahead1, -1, 0)
+    behind3, ahead3 = send(behind2, 1, 0), send(ahead2, -1, 0)
 
     normed = normalize(saved, norm_gain).reshape(slot_dev * block_rows, model_width)
     other_normed = swap_cores(normed)
@@ -286,8 +295,8 @@
     behind3, b_part = lax.optimization_barrier((behind3, b_part))
     weight = pltpu.VMEM((model_width, split), jnp.bfloat16)
     outs = [a_out, query_out]
-    a_part, tiles = project(a_kernel, place, rows, (all_a,), outs, model_width, (weight,))
-    blocks = (behind3, ahead3, send(behind3, 1))
+    a_part, tiles = project(a_kernel, place, rows, a_blocks, outs, model_width, (weight,))
+    blocks = (behind3, ahead3, send(behind3, 1, 0))
     out = jax.ShapeDtypeStruct((own_rows, local_width), jnp.bfloat16)
     mine, give = project(
         functools.partial(last_kernel, late),

time: 182 us -> 173 us (0.951)
  between operations: 15.1 us -> 1.72 us
  starting transfers between devices: 58.9 us -> 71.8 us
  waiting for transfers between devices: 54.4 us -> 51.9 us
  other arithmetic: 9.64 us -> 7.2 us
  local copies, waits for them, and re-layouts: 10.1 us -> 7.68 us
    all_gather x1 -> x0, waiting for transfers between devices: 14.1 us -> none  [per_device(): all_a = lax.all_gather(piece_a, ('z', 'x'), axis=0, tiled=True)]
    ppermute x7 -> x10, waiting for transfers between devices: 16.2 us -> 26.9 us  [send(): return lax.ppermute(value, GROUP, pairs)]
    all_to_all x3 -> x4, starting transfers between devices: 14.4 us -> 20.4 us  [exchange(): return lax.all_to_all(value, axis, 0, 0, tiled=True)]
    ppermute x7 -> x10, starting transfers between devices: 28.1 us -> 32 us  [send(): return lax.ppermute(value, GROUP, pairs)]
    unnamed x28 -> x20, local copies, waits for them, and re-layouts: 4.95 us -> 1.71 us
    ppermute x3, starting transfers between devices: 16.4 us -> 19.5 us  [swap_cores(): return lax.ppermute(value, 'core', [(0, 1), (1, 0)])]
    all_to_all x3 -> x4, waiting for transfers between devices: 23 us -> 23.9 us  [exchange(): return lax.all_to_all(value, axis, 0, 0, tiled=True)]
  transfers between devices with their start and end apart: 14 -> 17, of which waited for: 8 -> 8; matrix products, arithmetic and copies ran while one was open for 6% -> 3% of each run, Pallas kernels for 4% -> 4%
where the time goes in v5:
time: 173 us; the launch traced here: 172 us
  starting transfers between devices  71.8 us (42%)
  waiting for transfers between devices  51.9 us (30%)
  blocking collectives  17 us (10%)
  Pallas kernels  14 us (8%)
  local copies, waits for them, and re-layouts  7.68 us (4%)
  other arithmetic  7.2 us (4%)
    ppermute x10, starting transfers between devices, send(): return lax.ppermute(value, GROUP, pairs)  32 us
    ppermute x10, waiting for transfers between devices, send(): return lax.ppermute(value, GROUP, pairs)  26.9 us
    all_to_all x4, waiting for transfers between devices, exchange(): return lax.all_to_all(value, axis, 0, 0, tiled=True)  23.9 us
    all_to_all x4, starting transfers between devices, exchange(): return lax.all_to_all(value, axis, 0, 0, tiled=True)  20.4 us
    ppermute x3, starting transfers between devices, swap_cores(): return lax.ppermute(value, 'core', [(0, 1), (1, 0)])  19.5 us
    all_to_all x1, blocking collectives, exchange(): return lax.all_to_all(value, axis, 0, 0, tiled=True)  17 us
    pallas_call x3, Pallas kernels, project(): pl.pallas_call(kernel, in_specs=[pl.BlockSpec(memory_space=pltpu.SMEM)] +...  10.9 us
  transfers between devices with their start and end apart: 17, of which 8 were waited for; matrix products, arithmetic and copies ran while one was open for 3% of the time, Pallas kernels for 4%

profile of v5, /device:TPU:1, one launch (start us, length us, event | category | flops | bytes accessed | tf_op | source)
XLA Modules:
  0.0 172.1 jit_solution(16625407374942113821)
XLA Ops:
  6.1 8.8 %collective-permute-start = (bf16[96,256]{1,0:T(8,128)(2,1)S(1)}, bf16[96,256]{1,0:T(8,128)(2,1)S(1)}, u32[]{:S(2)}, u32[]{:S(2)}) collective-permute-start(bf16[96,256]{1,0:T(8,128)(2,1)S(1)} %fusion.9), channel_id=1, source_target_pairs={{0,8},{8,0},{1,9},{9,1},{2,10},{10,2},{3,11},{11,3},{4,12},{12,4},... | collective-permute-start | bytes 147464 | tf_op jit(solution)/shard_map/ppermute | solution.py:34
  14.9 3.4 %all-to-all-start = ((bf16[8,80,384]{2,1,0:T(8,128)(2,1)}), bf16[8,80,384]{2,1,0:T(8,128)(2,1)S(1)}, u32[]{:S(2)}, u32[]{:S(2)}) async-start(bf16[8,80,384]{2,1,0:T(8,128)(2,1)} %bitcast.45), calls=%async_computation | async-start | bytes 983040 | tf_op jit(solution)/shard_map/all_to_all | solution.py:219
  18.4 9.0 %all-to-all-done = bf16[8,80,384]{2,1,0:T(8,128)(2,1)S(1)} async-done(((bf16[8,80,384]{2,1,0:T(8,128)(2,1)}), bf16[8,80,384]{2,1,0:T(8,128)(2,1)S(1)}, u32[]{:S(2)}, u32[]{:S(2)}) %all-to-all-start) | async-done | bytes 491552 | tf_op jit(solution)/shard_map/all_to_all | solution.py:219
  30.4 2.8 %collective-permute-start.1 = (bf16[256,5120]{1,0:T(8,128)(2,1)S(1)}, bf16[256,5120]{1,0:T(8,128)(2,1)}, u32[]{:S(2)}, u32[]{:S(2)}) collective-permute-start(bf16[256,5120]{1,0:T(8,128)(2,1)S(1)} %bitcast.33), channel_id=1, source_target_pairs={{0,8},{8,0},{1,9},{9,1},{2,10},{10,2},{3,11},{11,3},{4,12},{12,4},... | collective-permute-start | bytes 7864328 | tf_op jit(solution)/shard_map/ppermute | solution.py:34
  33.2 5.7 %all-to-all-start.1 = ((bf16[8,176,256]{2,1,0:T(8,128)(2,1)}), bf16[8,176,256]{2,1,0:T(8,128)(2,1)S(1)}, u32[]{:S(2)}, u32[]{:S(2)}) async-start(bf16[8,176,256]{2,1,0:T(8,128)(2,1)} %broadcast_in_dim.61), calls=%async_computation.1 | async-start | bytes 1441792 | tf_op jit(solution)/shard_map/all_to_all | solution.py:219
  38.8 4.6 %collective-permute-start.5 = (bf16[640,384]{1,0:T(8,128)(2,1)}, bf16[640,384]{1,0:T(8,128)(2,1)}, u32[]{:S(2)}, u32[]{:S(2)}) collective-permute-start(bf16[640,384]{1,0:T(8,128)(2,1)} %bitcast.40), channel_id=1, source_target_pairs={{0,64},{8,456},{16,80},{24,472},{32,96},{40,488},{48,112},{56,504}... | collective-permute-start | bytes 1474568 | tf_op jit(solution)/shard_map/ppermute | solution.py:215
  43.4 1.9 %collective-permute-start.8 = (bf16[640,384]{1,0:T(8,128)(2,1)}, bf16[640,384]{1,0:T(8,128)(2,1)}, u32[]{:S(2)}, u32[]{:S(2)}) collective-permute-start(bf16[640,384]{1,0:T(8,128)(2,1)} %bitcast.41), channel_id=1, source_target_pairs={{0,448},{8,72},{16,464},{24,88},{32,480},{40,104},{48,496},{56,120... | collective-permute-start | bytes 1474568 | tf_op jit(solution)/shard_map/ppermute | solution.py:215
  45.4 21.7 %collective-permute-done.5.refs_1_ = bf16[640,384]{1,0:T(8,128)(2,1)} collective-permute-done((bf16[640,384]{1,0:T(8,128)(2,1)}, bf16[640,384]{1,0:T(8,128)(2,1)}, u32[]{:S(2)}, u32[]{:S(2)}) %collective-permute-start.5) | collective-permute-done | bytes 491552 | tf_op jit(solution)/shard_map/ppermute | solution.py:215
  67.1 3.4 %collective-permute-start.6 = (bf16[640,384]{1,0:T(8,128)(2,1)}, bf16[640,384]{1,0:T(8,128)(2,1)}, u32[]{:S(2)}, u32[]{:S(2)}) collective-permute-start(bf16[640,384]{1,0:T(8,128)(2,1)} %collective-permute-done.5.refs_1_), channel_id=1, source_target_pairs={{0,64},{8,456},{16,80},{24,472},{32,96},{40,488},{48,112},{56,504}... | collective-permute-start | bytes 1474568 | tf_op jit(solution)/shard_map/ppermute | solution.py:215
  70.6 2.8 %collective-permute-start.2 = (bf16[1408,256]{1,0:T(8,128)(2,1)S(1)}, bf16[1408,256]{1,0:T(8,128)(2,1)S(1)}, u32[]{:S(2)}, u32[]{:S(2)}) collective-permute-start(bf16[1408,256]{1,0:T(8,128)(2,1)S(1)} %bitcast.37), channel_id=1, source_target_pairs={{0,16},{8,56},{16,32},{24,8},{32,48},{40,24},{48,0},{56,40},{64,80... | collective-permute-start | bytes 2162696 | tf_op jit(solution)/shard_map/ppermute | solution.py:215
  77.3 4.3 %collective-permute-start.7 = (bf16[640,384]{1,0:T(8,128)(2,1)}, bf16[640,384]{1,0:T(8,128)(2,1)S(1)}, u32[]{:S(2)}, u32[]{:S(2)}) collective-permute-start(bf16[640,384]{1,0:T(8,128)(2,1)} %collective-permute-done.6.refs_3_), channel_id=1, source_target_pairs={{0,64},{8,456},{16,80},{24,472},{32,96},{40,488},{48,112},{56,504}... | collective-permute-start | bytes 1474568 | tf_op jit(solution)/shard_map/ppermute | solution.py:215
  81.7 2.2 %collective-permute-start.3 = (bf16[1408,256]{1,0:T(8,128)(2,1)S(1)}, bf16[1408,256]{1,0:T(8,128)(2,1)S(1)}, u32[]{:S(2)}, u32[]{:S(2)}) collective-permute-start(bf16[1408,256]{1,0:T(8,128)(2,1)S(1)} %bitcast.38), channel_id=1, source_target_pairs={{0,48},{8,24},{16,0},{24,40},{32,16},{40,56},{48,32},{56,8},{64,11... | collective-permute-start | bytes 2162696 | tf_op jit(solution)/shard_map/ppermute | solution.py:215
  83.9 4.3 %collective-permute-start.4 = (bf16[1408,256]{1,0:T(8,128)(2,1)S(1)}, bf16[1408,256]{1,0:T(8,128)(2,1)S(1)}, u32[]{:S(2)}, u32[]{:S(2)}) collective-permute-start(bf16[1408,256]{1,0:T(8,128)(2,1)S(1)} %collective-permute-done.2.refs_1_), channel_id=1, source_target_pairs={{0,16},{8,56},{16,32},{24,8},{32,48},{40,24},{48,0},{56,40},{64,80... | collective-permute-start | bytes 2162696 | tf_op jit(solution)/shard_map/ppermute | solution.py:215
  92.4 4.2 %shard_map.105.b_ref = f32[512,384]{1,0:T(8,128)S(1)} custom-call(s32[3]{0:T(128)S(1)} %pad_add_fusion.place_ref, bf16[256,5120]{1,0:T(8,128)(2,1)S(1)} %bitcast.34, bf16[256,5120]{1,0:T(8,128)(2,1)} %collective-permute-done.1.other_ref, bf16[640,384]{1,0:T(8,128)(2,1)S(1)} %bitcast.42, bf16[640,384]{1,0:T(8,128)(2,1)} %collective-permute-done.5.refs_1_, ...), custom_call_target="tpu_custom_call" | custom-call | flops 1258291200 | bytes 5734400 | tf_op jit(solution)/shard_map/pallas_call | solution.py:97
  96.6 4.6 %collective-permute-start.11 = (bf16[640,384]{1,0:T(8,128)(2,1)S(1)}, bf16[640,384]{1,0:T(8,128)(2,1)S(1)}, u32[]{:S(2)}, u32[]{:S(2)}) collective-permute-start(bf16[640,384]{1,0:T(8,128)(2,1)S(1)} %collective-permute-done.7.refs_0_), channel_id=1, source_target_pairs={{0,64},{8,456},{16,80},{24,472},{32,96},{40,488},{48,112},{56,504}... | collective-permute-start | bytes 1474568 | tf_op jit(solution)/shard_map/ppermute | solution.py:215
  103.2 3.5 %shard_map.104 = (f32[512,256]{1,0:T(8,128)S(1)}, f32[32,16,256]{2,1,0:T(8,128)S(1)}) custom-call(s32[3]{0:T(128)S(1)} %pad_add_fusion.place_ref, bf16[256,5120]{1,0:T(8,128)(2,1)S(1)} %bitcast.35, bf16[256,5120]{1,0:T(8,128)(2,1)} %collective-permute-done.1.other_ref, bf16[1408,256]{1,0:T(8,128)(2,1)S(1)} %bitcast.39, ...), custom_call_target="tpu_custom_call" | custom-call | flops 1342177280 | bytes 7864320 | tf_op jit(solution)/shard_map/pallas_call | solution.py:97
  108.5 3.3 %shard_map.106 = (bf16[256,640]{1,0:T(8,128)(2,1)S(1)}, bf16[256,640]{1,0:T(8,128)(2,1)S(1)}) custom-call(s32[3]{0:T(128)S(1)} %pad_add_fusion.place_ref, bf16[256,5120]{1,0:T(8,128)(2,1)S(1)} %bitcast.36, bf16[256,5120]{1,0:T(8,128)(2,1)} %collective-permute-done.1.other_ref, f32[512,256]{1,0:T(8,128)S(1)} %get-tuple-element.19.a_ref, ...), custom_call_target="tpu_custom_call" | custom-call | flops 754974720 | bytes 3440640 | tf_op jit(solution)/shard_map/pallas_call | solution.py:97
  111.8 7.9 %collective-permute-start.12 = (bf16[256,640]{1,0:T(8,128)(2,1)S(1)}, bf16[256,640]{1,0:T(8,128)(2,1)S(1)}, u32[]{:S(2)}, u32[]{:S(2)}) collective-permute-start(bf16[256,640]{1,0:T(8,128)(2,1)S(1)} %get-tuple-element.24), channel_id=1, source_target_pairs={{0,8},{8,0},{1,9},{9,1},{2,10},{10,2},{3,11},{11,3},{4,12},{12,4},... | collective-permute-start | bytes 983048 | tf_op jit(solution)/shard_map/ppermute | solution.py:34
  122.9 17.0 %all_to_all.25.parts_ref = bf16[64,8,128]{2,1,0:T(8,128)(2,1)S(1)} all-to-all(bf16[64,8,128]{2,1,0:T(8,128)(2,1)S(1)} %bitcast.43), channel_id=1, replica_groups=mesh['z'=8,'x'=4,'core'=2,'tp'=8] {'z','x','core'}, dimensions={0} | all-to-all | bytes 262144 | tf_op jit(solution)/shard_map/all_to_all | solution.py:219
  141.0 4.4 %all-to-all-start.3 = ((bf16[64,8,128]{2,1,0:T(8,128)(2,1)}), bf16[64,8,128]{2,1,0:T(8,128)(2,1)S(1)}, u32[]{:S(2)}, u32[]{:S(2)}) async-start(bf16[64,8,128]{2,1,0:T(8,128)(2,1)} %shard_map.108), calls=%async_computation.3 | async-start | bytes 262144 | tf_op jit(solution)/shard_map/all_to_all | solution.py:219
  146.6 10.2 %all-to-all-done.3 = bf16[64,8,128]{2,1,0:T(8,128)(2,1)S(1)} async-done(((bf16[64,8,128]{2,1,0:T(8,128)(2,1)}), bf16[64,8,128]{2,1,0:T(8,128)(2,1)S(1)}, u32[]{:S(2)}, u32[]{:S(2)}) %all-to-all-start.3) | async-done | bytes 131104 | tf_op jit(solution)/shard_map/all_to_all | solution.py:219
  157.7 6.8 %all-to-all-start.4 = ((f32[8,8,80]{2,1,0:T(8,128)}), f32[8,8,80]{2,1,0:T(8,128)S(1)}, u32[]{:S(2)}, u32[]{:S(2)}) async-start(f32[8,8,80]{2,1,0:T(8,128)} %fusion.5), calls=%async_computation.4 | async-start | bytes 65536 | tf_op jit(solution)/shard_map/all_to_all | solution.py:219
  164.6 2.3 %pad_maximum_fusion = bf16[2,128,2,640]{3,2,1,0:T(2,128)(2,1)} fusion(bf16[2,128,1,640]{3,2,1,0:T(2,128)(2,1)S(1)} %copy.29, bf16[2,128,1,640]{3,2,1,0:T(2,128)(2,1)S(1)} %copy.28), kind=kLoop, calls=%fused_computation.5 | loop fusion | flops 1310720 | bytes 1310720 | tf_op jit(solution)/shard_map/stack | solution.py:320
  166.9 4.6 %all-to-all-done.4 = f32[8,8,80]{2,1,0:T(8,128)S(1)} async-done(((f32[8,8,80]{2,1,0:T(8,128)}), f32[8,8,80]{2,1,0:T(8,128)S(1)}, u32[]{:S(2)}, u32[]{:S(2)}) %all-to-all-start.4) | async-done | bytes 20512 | tf_op jit(solution)/shard_map/all_to_all | solution.py:219
  (76 shorter events, 26.6 us)
Async XLA Ops:
  0.6 156.3 %copy-start = (bf16[640,80]{0,1:T(8,128)(2,1)S(1)}, bf16[640,80]{0,1:T(8,128)(2,1)}, u32[]{:S(2)}) copy-start(bf16[640,80]{0,1:T(8,128)(2,1)} %param.14) | copy-start | bytes 307204
  0.6 17.7 %copy-start.7 = (bf16[5120]{0:T(1024)(128)(2,1)S(1)}, bf16[5120]{0:T(1024)(128)(2,1)}, u32[]{:S(2)}) copy-start(bf16[5120]{0:T(1024)(128)(2,1)} %param.12) | copy-start | bytes 30724
  0.7 27.7 %copy-start.5 = (bf16[2,128,5120]{2,1,0:T(8,128)(2,1)S(1)}, bf16[2,128,5120]{2,1,0:T(8,128)(2,1)}, u32[]{:S(2)}) copy-start(bf16[2,128,5120]{2,1,0:T(8,128)(2,1)} %param.9) | copy-start | bytes 7864324
  6.1 12.3 %collective-permute-start = (bf16[96,256]{1,0:T(8,128)(2,1)S(1)}, bf16[96,256]{1,0:T(8,128)(2,1)S(1)}, u32[]{:S(2)}, u32[]{:S(2)}) collective-permute-start(bf16[96,256]{1,0:T(8,128)(2,1)S(1)} %fusion.9), channel_id=1, source_target_pairs={{0,8},{8,0},{1,9},{9,1},{2,10},{10,2},{3,11},{11,3},{4,12},{12,4},... | collective-permute-start | bytes 147464 | tf_op jit(solution)/shard_map/ppermute | solution.py:34
  14.9 12.6 %all-to-all-start = ((bf16[8,80,384]{2,1,0:T(8,128)(2,1)}), bf16[8,80,384]{2,1,0:T(8,128)(2,1)S(1)}, u32[]{:S(2)}, u32[]{:S(2)}) async-start(bf16[8,80,384]{2,1,0:T(8,128)(2,1)} %bitcast.45), calls=%async_computation | async-start | bytes 983040 | tf_op jit(solution)/shard_map/all_to_all | solution.py:219
  29.6 44.0 %copy-start.8 = (s32[2]{0:T(128)S(1)}, s32[2]{0:T(128)}, u32[]{:S(2)}) copy-start(s32[2]{0:T(128)} %param.10) | copy-start | bytes 28
  29.6 59.6 %copy-start.9 = (s32[4]{0:T(128)S(1)}, s32[4]{0:T(128)}, u32[]{:S(2)}) copy-start(s32[4]{0:T(128)} %param.11) | copy-start | bytes 52
  30.4 61.0 %collective-permute-start.1 = (bf16[256,5120]{1,0:T(8,128)(2,1)S(1)}, bf16[256,5120]{1,0:T(8,128)(2,1)}, u32[]{:S(2)}, u32[]{:S(2)}) collective-permute-start(bf16[256,5120]{1,0:T(8,128)(2,1)S(1)} %bitcast.33), channel_id=1, source_target_pairs={{0,8},{8,0},{1,9},{9,1},{2,10},{10,2},{3,11},{11,3},{4,12},{12,4},... | collective-permute-start | bytes 7864328 | tf_op jit(solution)/shard_map/ppermute | solution.py:34
  33.2 37.4 %all-to-all-start.1 = ((bf16[8,176,256]{2,1,0:T(8,128)(2,1)}), bf16[8,176,256]{2,1,0:T(8,128)(2,1)S(1)}, u32[]{:S(2)}, u32[]{:S(2)}) async-start(bf16[8,176,256]{2,1,0:T(8,128)(2,1)} %broadcast_in_dim.61), calls=%async_computation.1 | async-start | bytes 1441792 | tf_op jit(solution)/shard_map/all_to_all | solution.py:219
  38.8 28.3 %collective-permute-start.5 = (bf16[640,384]{1,0:T(8,128)(2,1)}, bf16[640,384]{1,0:T(8,128)(2,1)}, u32[]{:S(2)}, u32[]{:S(2)}) collective-permute-start(bf16[640,384]{1,0:T(8,128)(2,1)} %bitcast.40), channel_id=1, source_target_pairs={{0,64},{8,456},{16,80},{24,472},{32,96},{40,488},{48,112},{56,504}... | collective-permute-start | bytes 1474568 | tf_op jit(solution)/shard_map/ppermute | solution.py:215
  43.4 30.2 %collective-permute-start.8 = (bf16[640,384]{1,0:T(8,128)(2,1)}, bf16[640,384]{1,0:T(8,128)(2,1)}, u32[]{:S(2)}, u32[]{:S(2)}) collective-permute-start(bf16[640,384]{1,0:T(8,128)(2,1)} %bitcast.41), channel_id=1, source_target_pairs={{0,448},{8,72},{16,464},{24,88},{32,480},{40,104},{48,496},{56,120... | collective-permute-start | bytes 1474568 | tf_op jit(solution)/shard_map/ppermute | solution.py:215
  67.1 10.2 %collective-permute-start.6 = (bf16[640,384]{1,0:T(8,128)(2,1)}, bf16[640,384]{1,0:T(8,128)(2,1)}, u32[]{:S(2)}, u32[]{:S(2)}) collective-permute-start(bf16[640,384]{1,0:T(8,128)(2,1)} %collective-permute-done.5.refs_1_), channel_id=1, source_target_pairs={{0,64},{8,456},{16,80},{24,472},{32,96},{40,488},{48,112},{56,504}... | collective-permute-start | bytes 1474568 | tf_op jit(solution)/shard_map/ppermute | solution.py:215
  70.6 13.3 %collective-permute-start.2 = (bf16[1408,256]{1,0:T(8,128)(2,1)S(1)}, bf16[1408,256]{1,0:T(8,128)(2,1)S(1)}, u32[]{:S(2)}, u32[]{:S(2)}) collective-permute-start(bf16[1408,256]{1,0:T(8,128)(2,1)S(1)} %bitcast.37), channel_id=1, source_target_pairs={{0,16},{8,56},{16,32},{24,8},{32,48},{40,24},{48,0},{56,40},{64,80... | collective-permute-start | bytes 2162696 | tf_op jit(solution)/shard_map/ppermute | solution.py:215
  73.7 15.7 %collective-permute-start.9 = (bf16[640,384]{1,0:T(8,128)(2,1)}, bf16[640,384]{1,0:T(8,128)(2,1)S(1)}, u32[]{:S(2)}, u32[]{:S(2)}) collective-permute-start(bf16[640,384]{1,0:T(8,128)(2,1)} %collective-permute-done.8.refs_2_), channel_id=1, source_target_pairs={{0,448},{8,72},{16,464},{24,88},{32,480},{40,104},{48,496},{56,120... | collective-permute-start | bytes 1474568 | tf_op jit(solution)/shard_map/ppermute | solution.py:215
  77.3 19.3 %collective-permute-start.7 = (bf16[640,384]{1,0:T(8,128)(2,1)}, bf16[640,384]{1,0:T(8,128)(2,1)S(1)}, u32[]{:S(2)}, u32[]{:S(2)}) collective-permute-start(bf16[640,384]{1,0:T(8,128)(2,1)} %collective-permute-done.6.refs_3_), channel_id=1, source_target_pairs={{0,64},{8,456},{16,80},{24,472},{32,96},{40,488},{48,112},{56,504}... | collective-permute-start | bytes 1474568 | tf_op jit(solution)/shard_map/ppermute | solution.py:215
  81.7 19.8 %collective-permute-start.3 = (bf16[1408,256]{1,0:T(8,128)(2,1)S(1)}, bf16[1408,256]{1,0:T(8,128)(2,1)S(1)}, u32[]{:S(2)}, u32[]{:S(2)}) collective-permute-start(bf16[1408,256]{1,0:T(8,128)(2,1)S(1)} %bitcast.38), channel_id=1, source_target_pairs={{0,48},{8,24},{16,0},{24,40},{32,16},{40,56},{48,32},{56,8},{64,11... | collective-permute-start | bytes 2162696 | tf_op jit(solution)/shard_map/ppermute | solution.py:215
  83.9 19.2 %collective-permute-start.4 = (bf16[1408,256]{1,0:T(8,128)(2,1)S(1)}, bf16[1408,256]{1,0:T(8,128)(2,1)S(1)}, u32[]{:S(2)}, u32[]{:S(2)}) collective-permute-start(bf16[1408,256]{1,0:T(8,128)(2,1)S(1)} %collective-permute-done.2.refs_1_), channel_id=1, source_target_pairs={{0,16},{8,56},{16,32},{24,8},{32,48},{40,24},{48,0},{56,40},{64,80... | collective-permute-start | bytes 2162696 | tf_op jit(solution)/shard_map/ppermute | solution.py:215
  89.4 17.2 %collective-permute-start.10 = (bf16[640,384]{1,0:T(8,128)(2,1)S(1)}, bf16[640,384]{1,0:T(8,128)(2,1)S(1)}, u32[]{:S(2)}, u32[]{:S(2)}) collective-permute-start(bf16[640,384]{1,0:T(8,128)(2,1)S(1)} %collective-permute-done.9.refs_4_), channel_id=1, source_target_pairs={{0,448},{8,72},{16,464},{24,88},{32,480},{40,104},{48,496},{56,120... | collective-permute-start | bytes 1474568 | tf_op jit(solution)/shard_map/ppermute | solution.py:215
  96.6 11.9 %collective-permute-start.11 = (bf16[640,384]{1,0:T(8,128)(2,1)S(1)}, bf16[640,384]{1,0:T(8,128)(2,1)S(1)}, u32[]{:S(2)}, u32[]{:S(2)}) collective-permute-start(bf16[640,384]{1,0:T(8,128)(2,1)S(1)} %collective-permute-done.7.refs_0_), channel_id=1, source_target_pairs={{0,64},{8,456},{16,80},{24,472},{32,96},{40,488},{48,112},{56,504}... | collective-permute-start | bytes 1474568 | tf_op jit(solution)/shard_map/ppermute | solution.py:215
  108.5 31.3 %copy-start.3 = (bf16[1,640]{1,0:T(2,128)(2,1)S(1)}, bf16[1,640]{1,0:T(2,128)(2,1)}, u32[]{:S(2)}) copy-start(bf16[1,640]{1,0:T(2,128)(2,1)} %query_ref.1) | copy-start | bytes 3844
  108.5 31.3 %copy-start.4 = (bf16[1,2,640]{2,1,0:T(2,128)(2,1)S(1)}, bf16[1,2,640]{2,1,0:T(2,128)(2,1)}, u32[]{:S(2)}) copy-start(bf16[1,2,640]{2,1,0:T(2,128)(2,1)} %param.16) | copy-start | bytes 7684
  111.8 9.1 %collective-permute-start.12 = (bf16[256,640]{1,0:T(8,128)(2,1)S(1)}, bf16[256,640]{1,0:T(8,128)(2,1)S(1)}, u32[]{:S(2)}, u32[]{:S(2)}) collective-permute-start(bf16[256,640]{1,0:T(8,128)(2,1)S(1)} %get-tuple-element.24), channel_id=1, source_target_pairs={{0,8},{8,0},{1,9},{9,1},{2,10},{10,2},{3,11},{11,3},{4,12},{12,4},... | collective-permute-start | bytes 983048 | tf_op jit(solution)/shard_map/ppermute | solution.py:34
  141.0 15.8 %all-to-all-start.3 = ((bf16[64,8,128]{2,1,0:T(8,128)(2,1)}), bf16[64,8,128]{2,1,0:T(8,128)(2,1)S(1)}, u32[]{:S(2)}, u32[]{:S(2)}) async-start(bf16[64,8,128]{2,1,0:T(8,128)(2,1)} %shard_map.108), calls=%async_computation.3 | async-start | bytes 262144 | tf_op jit(solution)/shard_map/all_to_all | solution.py:219
  157.7 13.8 %all-to-all-start.4 = ((f32[8,8,80]{2,1,0:T(8,128)}), f32[8,8,80]{2,1,0:T(8,128)S(1)}, u32[]{:S(2)}, u32[]{:S(2)}) async-start(f32[8,8,80]{2,1,0:T(8,128)} %fusion.5), calls=%async_computation.4 | async-start | bytes 65536 | tf_op jit(solution)/shard_map/all_to_all | solution.py:219
  (3 other events, 4.7 us)

commit v6 on v2

--- a/solution.py
+++ b/solution.py
@@ -39,31 +39,25 @@
     return [lax.rem(place_ref[axis] + sign * step + chips, chips) for step in ring]
 
 
-def project_kernel(split, place_ref, own_ref, other_ref, cos_ref, sin_ref, *refs):
+def project_kernel(place_ref, own_ref, other_ref, cos_ref, sin_ref, *refs):
     a_refs, b_refs = refs[: len(X_RING)], refs[len(X_RING) : len(X_RING) + len(Z_RING)]
     own_out, other_out, query_out, weight = refs[len(X_RING) + len(Z_RING) :]
-    core = place_ref[2]
     rows, depth = own_ref.shape
     width = weight.shape[1]
-    half = depth // (2 * Z_CHIPS * X_CHIPS)
-    extra = a_refs[0].shape[0] // len(Z_RING) - 2 * half
-
-    def place(piece, at, chip, columns):
-        for part, whose in ((0, core), (1, 1 - core)):
-            to = pl.multiple_of((2 * chip + whose) * half, 16)
-            weight[pl.ds(to, half), columns] = piece[pl.ds(at + part * half, half), :]
-
-    for a_ref, x in zip(a_refs, around(place_ref, 1, X_CHIPS, X_RING)):
+    devices, split = query_out.shape[0], query_out.shape[2]
+    span, features = depth // devices, b_refs[0].shape[0]
+
+    for ref, x in zip(a_refs, around(place_ref, 1, X_CHIPS, X_RING)):
         for z in range(Z_CHIPS):
-            chip = z * X_CHIPS + x
-            at = z * (2 * half + extra)
-            place(a_ref, at, chip, pl.ds(0, split))
-            tiles = a_ref[pl.ds(at + 2 * half, extra), :].astype(jnp.float32)
-            query_out[chip, pl.ds(pl.multiple_of(core * 8, 8), 8), :] = tiles[:8]
-            query_out[chip, pl.ds(pl.multiple_of(8 - core * 8, 8), 8), :] = tiles[8:16]
-    for b_ref, z in zip(b_refs, around(place_ref, 0, Z_CHIPS, Z_RING)):
-        for x in range(X_CHIPS):
-            place(b_ref, x * 2 * half, z * X_CHIPS + x, pl.ds(split, width - split))
+            for core in (0, 1):
+                device = (z * X_CHIPS + x) * 2 + core
+                to = pl.ds(pl.multiple_of(device * span, 16), span)
+                piece = ref[2 * z + core]
+                weight[to, pl.ds(0, split)] = piece[:span]
+                query_out[device] = piece[span:].astype(jnp.float32)
+    for ref, z in zip(b_refs, around(place_ref, 0, Z_CHIPS, Z_RING)):
+        to = pl.ds(pl.multiple_of(z * features, 16), features)
+        weight[to, pl.ds(split, width - split)] = ref[...]
 
     chunk = 1024 if depth % 1024 == 0 else depth
     for part, (rows_ref, out) in enumerate(((own_ref, own_out), (other_ref, other_out))):
@@ -83,17 +77,18 @@
 
 def project(place, own, other, cosine, sine, a_blocks, b_blocks):
     rows, depth = own.shape
-    split = a_blocks[0].shape[1]
+    split = a_blocks[0].shape[2]
     width = split + b_blocks[0].shape[1]
+    lines = a_blocks[0].shape[1] - depth // (2 * Z_CHIPS * X_CHIPS)
     out = jax.ShapeDtypeStruct((rows, width), jnp.bfloat16)
-    tiles = jax.ShapeDtypeStruct((Z_CHIPS * X_CHIPS, 16, split), jnp.float32)
+    notes = jax.ShapeDtypeStruct((2 * Z_CHIPS * X_CHIPS, lines, split), jnp.float32)
     vmem = pl.BlockSpec(memory_space=pltpu.VMEM)
     operands = (own, other, cosine, sine, *a_blocks, *b_blocks)
     return pl.pallas_call(
-        functools.partial(project_kernel, split),
+        project_kernel,
         in_specs=[pl.BlockSpec(memory_space=pltpu.SMEM)] + [vmem] * len(operands),
         out_specs=[vmem] * 3,
-        out_shape=[out, out, tiles],
+        out_shape=[out, out, notes],
         scratch_shapes=[pltpu.VMEM((depth, width), jnp.bfloat16)],
         compiler_params=pltpu.CompilerParams(vmem_limit_bytes=40 * MIB),
         cost_estimate=pl.CostEstimate(
@@ -106,22 +101,16 @@
 
 def attend_kernel(place_ref, mine_ref, theirs_ref, query_ref, keys_ref, out_ref, tiles):
     has_keys = place_ref[2] == 0
-    chips = query_ref.shape[0]
+    count = query_ref.shape[0]
     heads = mine_ref.shape[1] // HEAD_DIM
     key_conv = keys_ref[0:1, :]
 
     def rows_of(part):
-        lanes = pl.ds(part % 2 * HEAD_DIM, HEAD_DIM)
-        return jnp.concatenate([query_ref[:, core * 8 + part // 2, lanes] for core in (0, 1)])
+        return query_ref[:, part // 2, pl.ds(part % 2 * HEAD_DIM, HEAD_DIM)]
 
     allowed = rows_of(heads)[:, 0:1] == key_conv
-    lane = lax.broadcasted_iota(jnp.int32, (2 * chips, HEAD_DIM), 1)
+    lane = lax.broadcasted_iota(jnp.int32, (count, HEAD_DIM), 1)
     stats = jnp.zeros(lane.shape, jnp.float32)
-
-    def put(row, value):
-        for core in (0, 1):
-            tiles[:, core, row, :] = value[core * chips : (core + 1) * chips]
-
     for head in range(heads):
         lanes = pl.ds(head * HEAD_DIM, HEAD_DIM)
         mine, theirs = mine_ref[:, lanes], theirs_ref[:, lanes]
@@ -137,7 +126,7 @@
         top = jnp.max(scores, axis=-1, keepdims=True)
         weight = jnp.where(allowed, jnp.exp(scores - top), 0.0).astype(jnp.bfloat16)
         total = jnp.sum(weight.astype(jnp.float32), axis=-1, keepdims=True)
-        put(head, jnp.dot(weight, values, preferred_element_type=jnp.float32))
+        tiles[:, head, :] = jnp.dot(weight, values, preferred_element_type=jnp.float32)
         at = head
         for value, parts in ((top, TOP_PARTS), (total, SUM_PARTS)):
             for _ in range(parts):
@@ -145,14 +134,14 @@
                 stats = jnp.where(lane == at, rounded, stats)
                 value = value - rounded
                 at += 8
-    put(heads, stats)
+    tiles[:, heads, :] = stats
     for row in range(heads + 1, 8):
-        put(row, jnp.zeros_like(stats))
+        tiles[:, row, :] = jnp.zeros_like(stats)
     out_ref[...] = tiles[...].astype(jnp.bfloat16)
 
 
 def attend(place, mine, theirs, queries, key_conv):
-    shape = (queries.shape[0], 2, 8, HEAD_DIM)
+    shape = (queries.shape[0], 8, HEAD_DIM)
     vmem = pl.BlockSpec(memory_space=pltpu.VMEM)
     return pl.pallas_call(
         attend_kernel,
@@ -210,21 +199,8 @@
     return lax.ppermute(value, GROUP, pairs)
 
 
-def ring(value, chips, dz, dx):
-    behind, ahead, found = value, value, [value]
-    for _ in range(chips // 2 - 1):
-        behind, ahead = send(behind, dz, dx), send(ahead, -dz, -dx)
-        found += [behind, ahead]
-    return found + [send(behind, dz, dx)]
-
-
 def exchange(value, axis):
     return lax.all_to_all(value, axis, 0, 0, tiled=True)
-
-
-def collect(piece, axis, chips):
-    copies = jnp.broadcast_to(piece, (chips,) + piece.shape)
-    return exchange(copies, axis).reshape(chips * piece.shape[0], piece.shape[1])
 
 
 def per_device(
@@ -239,28 +215,38 @@
     first_core = core == 0
 
     split = 2 * HEAD_DIM
-    keep = jnp.where(first_core, kv_weight[:, 0], kv_weight[:, 1])
-    give = jnp.where(first_core, kv_weight[:, 1], kv_weight[:, 0])
-    numbers = jnp.broadcast_to(row_conv, (HEAD_DIM,)), jnp.pad(block_per_slot, (0, split - slot_dev))
-    conv_part, block_part = (part.astype(jnp.bfloat16)[None] for part in numbers)
-    wide = jnp.concatenate([queries, conv_part], axis=1)
-    rows = [wide[:, at : at + split] for at in range(0, wide.shape[1], split)] + [block_part]
-    notes = jnp.pad(jnp.concatenate(rows), ((0, 8 - len(rows)), (0, 0)))
-    sent = jnp.concatenate([give, jnp.pad(notes, ((0, 8), (0, local_width - split)))])
-    got = swap_cores(sent)
-    part_rows = keep.shape[0]
-    got_notes = got[part_rows : part_rows + 8, :split]
-    piece_a = jnp.concatenate([keep[:, :split], got[:part_rows, :split], notes, got_notes])
-    piece_b = jnp.concatenate([keep[:, split:], got[:part_rows, split:]])
-    block_b = collect(piece_b, "x", X_CHIPS)
-    block_a = collect(piece_a, "z", Z_CHIPS)
-    saved, block_b = lax.optimization_barrier((saved, block_b))
-    b_blocks = ring(block_b, Z_CHIPS, 1, 0)
-    a_blocks = ring(block_a, X_CHIPS, 0, 1)
+    def copies(pieces, chips):
+        pieces = jnp.broadcast_to(jnp.stack(pieces), (chips, 2) + pieces[0].shape)
+        return pieces.reshape(-1, *pieces.shape[2:])
+
+    part_rows = kv_weight.shape[0]
+    block_b = exchange(copies([kv_weight[:, k, split:] for k in (0, 1)], X_CHIPS), ("x", "core"))
+    block_b = block_b.reshape(-1, local_width - split)
+    numbers = jnp.concatenate([row_conv, block_per_slot]).astype(jnp.bfloat16)
+    numbers = jnp.broadcast_to(numbers[:, None], (1 + slot_dev, split))
+    wide = jnp.concatenate([queries, numbers[:1, :HEAD_DIM]], axis=1)
+    lines = [wide[:, at : at + split] for at in range(0, wide.shape[1], split)]
+    notes = jnp.concatenate([*lines, numbers[1:]])
+    notes = jnp.pad(notes, ((0, 8 - notes.shape[0]), (0, 0)))
+    pieces_a = [jnp.concatenate([kv_weight[:, k, :split], notes]) for k in (0, 1)]
+    copies_a = copies(pieces_a, Z_CHIPS)
+    pieces_a = exchange(copies_a, ("z", "core"))
+    saved, block_b, _ = lax.optimization_barrier((saved, block_b, copies_a))
+    a_behind, a_ahead = send(pieces_a, 0, 1), send(pieces_a, 0, -1)
+    behind1, ahead1 = send(block_b, 1, 0), send(block_b, -1, 0)
+    ahead1, a_behind = lax.optimization_barrier((ahead1, a_behind))
+    behind2, ahead2 = send(behind1, 1, 0), send(ahead1, -1, 0)
+    ahead2, a_ahead = lax.optimization_barrier((ahead2, a_ahead))
+    behind3, ahead3 = send(behind2, 1, 0), send(ahead2, -1, 0)
+    a_blocks = (pieces_a, a_behind, a_ahead, send(a_behind, 0, 1))
+    b_blocks = (block_b, behind1, ahead1, behind2, ahead2, behind3, ahead3, send(behind3, 1, 0))
 
     normed = normalize(saved, norm_gain).reshape(slot_dev * block_rows, model_width)
     other_normed = swap_cores(normed)
-    other_blocks = got_notes[len(rows) - 1, :slot_dev]
+    beside = 2 * lax.axis_index("z") + 1 - core
+    other_blocks = lax.dynamic_index_in_dim(pieces_a, beside, keepdims=False)
+    first_line = part_rows + len(lines)
+    other_blocks = other_blocks[first_line : first_line + slot_dev, 0]
     blocks = jnp.concatenate([block_per_slot, other_blocks.astype(jnp.int32)])
     conv = blocks // blocks_conv
     positions = (blocks % blocks_conv * block_rows)[:, None] + jnp.arange(
@@ -280,11 +266,11 @@
     key_conv = jnp.broadcast_to(key_conv.astype(jnp.float32), (8, own_rows))
     place = jnp.stack([lax.axis_index("z"), lax.axis_index("x"), core]).astype(jnp.int32)
 
-    mine, for_other, tiles = project(
+    mine, give, tiles = project(
         place, normed, other_normed, cosine, sine, a_blocks, b_blocks
     )
-    theirs = swap_cores(for_other)
-    parts = attend(place, mine, theirs, tiles, key_conv).reshape(groups, 8, HEAD_DIM)
+    theirs = swap_cores(give)
+    parts = attend(place, mine, theirs, tiles, key_conv)
     merged = merge(exchange(parts, GROUP), queries, new_kv[0])
     attended = exchange(merged, GROUP)[:, :heads].reshape(groups, local_width)
     decoded = jnp.dot(attended, out_weight, preferred_element_type=jnp.float32)

time: 167 us -> 167 us (level)
  waiting for transfers between devices: 51 us -> 57.2 us
  blocking collectives: 18.6 us -> 14.9 us
    all_to_all x4, waiting for transfers between devices: 22.8 us -> 34.1 us  [exchange(): return lax.all_to_all(value, axis, 0, 0, tiled=True)]
    ppermute x3 -> x2, starting transfers between devices: 15.2 us -> 4.72 us  [swap_cores(): return lax.ppermute(value, 'core', [(0, 1), (1, 0)])]
    all_to_all x4, starting transfers between devices: 20 us -> 28.5 us  [exchange(): return lax.all_to_all(value, axis, 0, 0, tiled=True)]
    ppermute x10, waiting for transfers between devices: 26.2 us -> 22 us  [send(): return lax.ppermute(value, GROUP, pairs)]
    all_to_all x1, blocking collectives: 18.6 us -> 14.9 us  [exchange(): return lax.all_to_all(value, axis, 0, 0, tiled=True)]
  transfers between devices with their start and end apart: 17 -> 16, of which waited for: 10 -> 8; matrix products, arithmetic and copies ran while one was open for 5% -> 5% of each run, Pallas kernels for 0% -> 0%
where the time goes in v6:
time: 167 us; the launch traced here: 166 us
  starting transfers between devices  66.7 us (40%)
  waiting for transfers between devices  57.2 us (34%)
  blocking collectives  14.9 us (9%)
  Pallas kernels  10.5 us (6%)
  other arithmetic  7.51 us (4%)
  local copies, waits for them, and re-layouts  6.23 us (4%)
  between operations  1.71 us (1%)
    all_to_all x4, waiting for transfers between devices, exchange(): return lax.all_to_all(value, axis, 0, 0, tiled=True)  34.1 us
    ppermute x10, starting transfers between devices, send(): return lax.ppermute(value, GROUP, pairs)  33.5 us
    all_to_all x4, starting transfers between devices, exchange(): return lax.all_to_all(value, axis, 0, 0, tiled=True)  28.5 us
    ppermute x10, waiting for transfers between devices, send(): return lax.ppermute(value, GROUP, pairs)  22 us
    all_to_all x1, blocking collectives, exchange(): return lax.all_to_all(value, axis, 0, 0, tiled=True)  14.9 us
    pallas_call x1, Pallas kernels, project(): pl.pallas_call(project_kernel, in_specs=[pl.BlockSpec(memory_space=pltpu....  7.4 us
    ppermute x2, starting transfers between devices, swap_cores(): return lax.ppermute(value, 'core', [(0, 1), (1, 0)])  4.72 us
  transfers between devices with their start and end apart: 16, of which 8 were waited for; matrix products, arithmetic and copies ran while one was open for 5% of the time, Pallas kernels for 0%

profile of v6, /device:TPU:1, one launch (start us, length us, event | category | flops | bytes accessed | tf_op | source)
XLA Modules:
  0.0 165.6 jit_solution(861435080637002156)
XLA Ops:
  2.8 11.0 %all-to-all-start = ((bf16[8,80,384]{2,1,0:T(8,128)(2,1)}), bf16[8,80,384]{2,1,0:T(8,128)(2,1)}, u32[]{:S(2)}, u32[]{:S(2)}) async-start(bf16[8,80,384]{2,1,0:T(8,128)(2,1)} %bitcast.5), calls=%async_computation | async-start | bytes 983040 | tf_op jit(solution)/shard_map/all_to_all | solution.py:203
  14.9 8.2 %all-to-all-done = bf16[8,80,384]{2,1,0:T(8,128)(2,1)} async-done(((bf16[8,80,384]{2,1,0:T(8,128)(2,1)}), bf16[8,80,384]{2,1,0:T(8,128)(2,1)}, u32[]{:S(2)}, u32[]{:S(2)}) %all-to-all-start) | async-done | bytes 491552 | tf_op jit(solution)/shard_map/all_to_all | solution.py:203
  24.0 6.1 %all-to-all-start.1 = ((bf16[16,88,256]{2,1,0:T(8,128)(2,1)}), bf16[16,88,256]{2,1,0:T(8,128)(2,1)S(1)}, u32[]{:S(2)}, u32[]{:S(2)}) async-start(bf16[16,88,256]{2,1,0:T(8,128)(2,1)} %bitcast.40), calls=%async_computation.1 | async-start | bytes 1441792 | tf_op jit(solution)/shard_map/all_to_all | solution.py:203
  32.6 2.0 %collective-permute-start = (bf16[256,5120]{1,0:T(8,128)(2,1)S(1)}, bf16[256,5120]{1,0:T(8,128)(2,1)}, u32[]{:S(2)}, u32[]{:S(2)}) collective-permute-start(bf16[256,5120]{1,0:T(8,128)(2,1)S(1)} %bitcast.37), channel_id=1, source_target_pairs={{0,8},{8,0},{1,9},{9,1},{2,10},{10,2},{3,11},{11,3},{4,12},{12,4},... | collective-permute-start | bytes 7864328 | tf_op jit(solution)/shard_map/ppermute | solution.py:34
  34.6 4.8 %collective-permute-start.6 = (bf16[640,384]{1,0:T(8,128)(2,1)}, bf16[640,384]{1,0:T(8,128)(2,1)}, u32[]{:S(2)}, u32[]{:S(2)}) collective-permute-start(bf16[640,384]{1,0:T(8,128)(2,1)} %bitcast.6.refs_4_), channel_id=1, source_target_pairs={{0,64},{8,456},{16,80},{24,472},{32,96},{40,488},{48,112},{56,504}... | collective-permute-start | bytes 1474568 | tf_op jit(solution)/shard_map/ppermute | solution.py:199
  39.4 12.0 %all-to-all-done.1.refs_0_ = bf16[16,88,256]{2,1,0:T(8,128)(2,1)S(1)} async-done(((bf16[16,88,256]{2,1,0:T(8,128)(2,1)}), bf16[16,88,256]{2,1,0:T(8,128)(2,1)S(1)}, u32[]{:S(2)}, u32[]{:S(2)}) %all-to-all-start.1) | async-done | bytes 720928 | tf_op jit(solution)/shard_map/all_to_all | solution.py:203
  51.4 2.8 %collective-permute-start.2 = (bf16[16,88,256]{2,1,0:T(8,128)(2,1)S(1)}, bf16[16,88,256]{2,1,0:T(8,128)(2,1)}, u32[]{:S(2)}, u32[]{:S(2)}) collective-permute-start(bf16[16,88,256]{2,1,0:T(8,128)(2,1)S(1)} %all-to-all-done.1.refs_0_), channel_id=1, source_target_pairs={{0,16},{8,56},{16,32},{24,8},{32,48},{40,24},{48,0},{56,40},{64,80... | collective-permute-start | bytes 2162696 | tf_op jit(solution)/shard_map/ppermute | solution.py:199
  54.2 1.9 %collective-permute-start.1 = (bf16[640,384]{1,0:T(8,128)(2,1)}, bf16[640,384]{1,0:T(8,128)(2,1)}, u32[]{:S(2)}, u32[]{:S(2)}) collective-permute-start(bf16[640,384]{1,0:T(8,128)(2,1)} %bitcast.6.refs_4_), channel_id=1, source_target_pairs={{0,448},{8,72},{16,464},{24,88},{32,480},{40,104},{48,496},{56,120... | collective-permute-start | bytes 1474568 | tf_op jit(solution)/shard_map/ppermute | solution.py:199
  56.2 4.6 %collective-permute-start.7 = (bf16[640,384]{1,0:T(8,128)(2,1)}, bf16[640,384]{1,0:T(8,128)(2,1)}, u32[]{:S(2)}, u32[]{:S(2)}) collective-permute-start(bf16[640,384]{1,0:T(8,128)(2,1)} %collective-permute-done.6.refs_5_), channel_id=1, source_target_pairs={{0,64},{8,456},{16,80},{24,472},{32,96},{40,488},{48,112},{56,504}... | collective-permute-start | bytes 1474568 | tf_op jit(solution)/shard_map/ppermute | solution.py:199
  60.9 2.5 %collective-permute-start.4 = (bf16[16,88,256]{2,1,0:T(8,128)(2,1)S(1)}, bf16[16,88,256]{2,1,0:T(8,128)(2,1)S(1)}, u32[]{:S(2)}, u32[]{:S(2)}) collective-permute-start(bf16[16,88,256]{2,1,0:T(8,128)(2,1)S(1)} %all-to-all-done.1.refs_0_), channel_id=1, source_target_pairs={{0,48},{8,24},{16,0},{24,40},{32,16},{40,56},{48,32},{56,8},{64,11... | collective-permute-start | bytes 2162696 | tf_op jit(solution)/shard_map/ppermute | solution.py:199
  63.6 4.6 %collective-permute-done.7.refs_7_ = bf16[640,384]{1,0:T(8,128)(2,1)} collective-permute-done((bf16[640,384]{1,0:T(8,128)(2,1)}, bf16[640,384]{1,0:T(8,128)(2,1)}, u32[]{:S(2)}, u32[]{:S(2)}) %collective-permute-start.7) | collective-permute-done | bytes 491552 | tf_op jit(solution)/shard_map/ppermute | solution.py:199
  68.1 4.1 %collective-permute-start.8 = (bf16[640,384]{1,0:T(8,128)(2,1)}, bf16[640,384]{1,0:T(8,128)(2,1)S(1)}, u32[]{:S(2)}, u32[]{:S(2)}) collective-permute-start(bf16[640,384]{1,0:T(8,128)(2,1)} %collective-permute-done.7.refs_7_), channel_id=1, source_target_pairs={{0,64},{8,456},{16,80},{24,472},{32,96},{40,488},{48,112},{56,504}... | collective-permute-start | bytes 1474568 | tf_op jit(solution)/shard_map/ppermute | solution.py:199
  74.2 4.5 %collective-permute-start.5 = (bf16[16,88,256]{2,1,0:T(8,128)(2,1)}, bf16[16,88,256]{2,1,0:T(8,128)(2,1)S(1)}, u32[]{:S(2)}, u32[]{:S(2)}) collective-permute-start(bf16[16,88,256]{2,1,0:T(8,128)(2,1)} %collective-permute-done.2.refs_1_), channel_id=1, source_target_pairs={{0,16},{8,56},{16,32},{24,8},{32,48},{40,24},{48,0},{56,40},{64,80... | collective-permute-start | bytes 2162696 | tf_op jit(solution)/shard_map/ppermute | solution.py:199
  78.9 4.6 %collective-permute-start.10 = (bf16[640,384]{1,0:T(8,128)(2,1)S(1)}, bf16[640,384]{1,0:T(8,128)(2,1)S(1)}, u32[]{:S(2)}, u32[]{:S(2)}) collective-permute-start(bf16[640,384]{1,0:T(8,128)(2,1)S(1)} %collective-permute-done.8.refs_9_), channel_id=1, source_target_pairs={{0,64},{8,456},{16,80},{24,472},{32,96},{40,488},{48,112},{56,504}... | collective-permute-start | bytes 1474568 | tf_op jit(solution)/shard_map/ppermute | solution.py:199
  83.5 4.8 %collective-permute-done.3.refs_8_ = bf16[640,384]{1,0:T(8,128)(2,1)S(1)} collective-permute-done((bf16[640,384]{1,0:T(8,128)(2,1)}, bf16[640,384]{1,0:T(8,128)(2,1)S(1)}, u32[]{:S(2)}, u32[]{:S(2)}) %collective-permute-start.3) | collective-permute-done | bytes 491552 | tf_op jit(solution)/shard_map/ppermute | solution.py:199
  91.6 12.7 %collective-permute-done.9.refs_10_ = bf16[640,384]{1,0:T(8,128)(2,1)S(1)} collective-permute-done((bf16[640,384]{1,0:T(8,128)(2,1)S(1)}, bf16[640,384]{1,0:T(8,128)(2,1)S(1)}, u32[]{:S(2)}, u32[]{:S(2)}) %collective-permute-start.9) | collective-permute-done | bytes 491552 | tf_op jit(solution)/shard_map/ppermute | solution.py:199
  104.2 7.4 %shard_map.104 = (bf16[256,640]{1,0:T(8,128)(2,1)S(1)}, bf16[256,640]{1,0:T(8,128)(2,1)S(1)}, f32[64,8,256]{2,1,0:T(8,128)S(1)}) custom-call(s32[3]{0:T(128)S(1)} %pad_add_fusion.place_ref, bf16[256,5120]{1,0:T(8,128)(2,1)S(1)} %bitcast.38, bf16[256,5120]{1,0:T(8,128)(2,1)} %collective-permute-done.other_ref, f32[512,128]{1,0:T(8,128)S(1)} %get-tuple-element.37.cos_ref, ...), custom_call_target="tpu_custom_call" | custom-call | flops 3355443200 | bytes 11796480 | tf_op jit(solution)/shard_map/pallas_call | solution.py:87
  111.7 2.7 %collective-permute-start.11 = (bf16[256,640]{1,0:T(8,128)(2,1)S(1)}, bf16[256,640]{1,0:T(8,128)(2,1)S(1)}, u32[]{:S(2)}, u32[]{:S(2)}) collective-permute-start(bf16[256,640]{1,0:T(8,128)(2,1)S(1)} %get-tuple-element.18), channel_id=1, source_target_pairs={{0,8},{8,0},{1,9},{9,1},{2,10},{10,2},{3,11},{11,3},{4,12},{12,4},... | collective-permute-start | bytes 983048 | tf_op jit(solution)/shard_map/ppermute | solution.py:34
  118.2 14.9 %all_to_all.25.parts_ref = bf16[64,8,128]{2,1,0:T(8,128)(2,1)S(1)} all-to-all(bf16[64,8,128]{2,1,0:T(8,128)(2,1)S(1)} %shard_map.105), channel_id=1, replica_groups=mesh['z'=8,'x'=4,'core'=2,'tp'=8] {'z','x','core'}, dimensions={0} | all-to-all | bytes 262144 | tf_op jit(solution)/shard_map/all_to_all | solution.py:203
  134.4 4.6 %all-to-all-start.3 = ((bf16[64,8,128]{2,1,0:T(8,128)(2,1)}), bf16[64,8,128]{2,1,0:T(8,128)(2,1)S(1)}, u32[]{:S(2)}, u32[]{:S(2)}) async-start(bf16[64,8,128]{2,1,0:T(8,128)(2,1)} %shard_map.106), calls=%async_computation.3 | async-start | bytes 262144 | tf_op jit(solution)/shard_map/all_to_all | solution.py:203
  141.1 9.3 %all-to-all-done.3 = bf16[64,8,128]{2,1,0:T(8,128)(2,1)S(1)} async-done(((bf16[64,8,128]{2,1,0:T(8,128)(2,1)}), bf16[64,8,128]{2,1,0:T(8,128)(2,1)S(1)}, u32[]{:S(2)}, u32[]{:S(2)}) %all-to-all-start.3) | async-done | bytes 131104 | tf_op jit(solution)/shard_map/all_to_all | solution.py:203
  151.3 6.8 %all-to-all-start.4 = ((f32[8,8,80]{2,1,0:T(8,128)}), f32[8,8,80]{2,1,0:T(8,128)S(1)}, u32[]{:S(2)}, u32[]{:S(2)}) async-start(f32[8,8,80]{2,1,0:T(8,128)} %fusion.5), calls=%async_computation.4 | async-start | bytes 65536 | tf_op jit(solution)/shard_map/all_to_all | solution.py:203
  158.1 2.3 %pad_maximum_fusion = bf16[2,128,2,640]{3,2,1,0:T(2,128)(2,1)} fusion(bf16[2,128,1,640]{3,2,1,0:T(2,128)(2,1)S(1)} %copy.32, bf16[2,128,1,640]{3,2,1,0:T(2,128)(2,1)S(1)} %copy.31), kind=kLoop, calls=%fused_computation.5 | loop fusion | flops 1310720 | bytes 1310720 | tf_op jit(solution)/shard_map/stack | solution.py:283
  160.4 4.6 %all-to-all-done.4 = f32[8,8,80]{2,1,0:T(8,128)S(1)} async-done(((f32[8,8,80]{2,1,0:T(8,128)}), f32[8,8,80]{2,1,0:T(8,128)S(1)}, u32[]{:S(2)}, u32[]{:S(2)}) %all-to-all-start.4) | async-done | bytes 20512 | tf_op jit(solution)/shard_map/all_to_all | solution.py:203
  (70 shorter events, 20.2 us)
Async XLA Ops:
  0.6 149.8 %copy-start = (bf16[640,80]{0,1:T(8,128)(2,1)S(1)}, bf16[640,80]{0,1:T(8,128)(2,1)}, u32[]{:S(2)}) copy-start(bf16[640,80]{0,1:T(8,128)(2,1)} %param.14) | copy-start | bytes 307204
  0.6 13.2 %copy-start.6 = (bf16[80,2,640]{2,1,0:T(2,128)(2,1)S(1)}, bf16[80,2,640]{2,1,0:T(2,128)(2,1)}, u32[]{:S(2)}) copy-start(bf16[80,2,640]{2,1,0:T(2,128)(2,1)} %param.13) | copy-start | bytes 614404
  0.7 14.0 %copy-start.8 = (s32[2]{0:T(128)S(1)}, s32[2]{0:T(128)}, u32[]{:S(2)}) copy-start(s32[2]{0:T(128)} %param.10) | copy-start | bytes 28
  0.7 14.0 %copy-start.7 = (bf16[5120]{0:T(1024)(128)(2,1)S(1)}, bf16[5120]{0:T(1024)(128)(2,1)}, u32[]{:S(2)}) copy-start(bf16[5120]{0:T(1024)(128)(2,1)} %param.12) | copy-start | bytes 30724
  0.7 14.0 %copy-start.2 = (bf16[1,640]{1,0:T(2,128)(2,1)S(1)}, bf16[1,640]{1,0:T(2,128)(2,1)}, u32[]{:S(2)}) copy-start(bf16[1,640]{1,0:T(2,128)(2,1)} %query_ref.1) | copy-start | bytes 3844
  2.0 28.2 %copy-start.4 = (bf16[2,128,5120]{2,1,0:T(8,128)(2,1)S(1)}, bf16[2,128,5120]{2,1,0:T(8,128)(2,1)}, u32[]{:S(2)}) copy-start(bf16[2,128,5120]{2,1,0:T(8,128)(2,1)} %param.9) | copy-start | bytes 7864324
  2.8 20.3 %all-to-all-start = ((bf16[8,80,384]{2,1,0:T(8,128)(2,1)}), bf16[8,80,384]{2,1,0:T(8,128)(2,1)}, u32[]{:S(2)}, u32[]{:S(2)}) async-start(bf16[8,80,384]{2,1,0:T(8,128)(2,1)} %bitcast.5), calls=%async_computation | async-start | bytes 983040 | tf_op jit(solution)/shard_map/all_to_all | solution.py:203
  24.0 27.4 %all-to-all-start.1 = ((bf16[16,88,256]{2,1,0:T(8,128)(2,1)}), bf16[16,88,256]{2,1,0:T(8,128)(2,1)S(1)}, u32[]{:S(2)}, u32[]{:S(2)}) async-start(bf16[16,88,256]{2,1,0:T(8,128)(2,1)} %bitcast.40), calls=%async_computation.1 | async-start | bytes 1441792 | tf_op jit(solution)/shard_map/all_to_all | solution.py:203
  31.8 46.9 %copy-start.9 = (s32[4]{0:T(128)S(1)}, s32[4]{0:T(128)}, u32[]{:S(2)}) copy-start(s32[4]{0:T(128)} %param.11) | copy-start | bytes 52
  32.6 59.0 %collective-permute-start = (bf16[256,5120]{1,0:T(8,128)(2,1)S(1)}, bf16[256,5120]{1,0:T(8,128)(2,1)}, u32[]{:S(2)}, u32[]{:S(2)}) collective-permute-start(bf16[256,5120]{1,0:T(8,128)(2,1)S(1)} %bitcast.37), channel_id=1, source_target_pairs={{0,8},{8,0},{1,9},{9,1},{2,10},{10,2},{3,11},{11,3},{4,12},{12,4},... | collective-permute-start | bytes 7864328 | tf_op jit(solution)/shard_map/ppermute | solution.py:34
  34.6 21.5 %collective-permute-start.6 = (bf16[640,384]{1,0:T(8,128)(2,1)}, bf16[640,384]{1,0:T(8,128)(2,1)}, u32[]{:S(2)}, u32[]{:S(2)}) collective-permute-start(bf16[640,384]{1,0:T(8,128)(2,1)} %bitcast.6.refs_4_), channel_id=1, source_target_pairs={{0,64},{8,456},{16,80},{24,472},{32,96},{40,488},{48,112},{56,504}... | collective-permute-start | bytes 1474568 | tf_op jit(solution)/shard_map/ppermute | solution.py:199
  51.4 20.8 %collective-permute-start.2 = (bf16[16,88,256]{2,1,0:T(8,128)(2,1)S(1)}, bf16[16,88,256]{2,1,0:T(8,128)(2,1)}, u32[]{:S(2)}, u32[]{:S(2)}) collective-permute-start(bf16[16,88,256]{2,1,0:T(8,128)(2,1)S(1)} %all-to-all-done.1.refs_0_), channel_id=1, source_target_pairs={{0,16},{8,56},{16,32},{24,8},{32,48},{40,24},{48,0},{56,40},{64,80... | collective-permute-start | bytes 2162696 | tf_op jit(solution)/shard_map/ppermute | solution.py:199
  54.2 18.0 %collective-permute-start.1 = (bf16[640,384]{1,0:T(8,128)(2,1)}, bf16[640,384]{1,0:T(8,128)(2,1)}, u32[]{:S(2)}, u32[]{:S(2)}) collective-permute-start(bf16[640,384]{1,0:T(8,128)(2,1)} %bitcast.6.refs_4_), channel_id=1, source_target_pairs={{0,448},{8,72},{16,464},{24,88},{32,480},{40,104},{48,496},{56,120... | collective-permute-start | bytes 1474568 | tf_op jit(solution)/shard_map/ppermute | solution.py:199
  56.2 12.0 %collective-permute-start.7 = (bf16[640,384]{1,0:T(8,128)(2,1)}, bf16[640,384]{1,0:T(8,128)(2,1)}, u32[]{:S(2)}, u32[]{:S(2)}) collective-permute-start(bf16[640,384]{1,0:T(8,128)(2,1)} %collective-permute-done.6.refs_5_), channel_id=1, source_target_pairs={{0,64},{8,456},{16,80},{24,472},{32,96},{40,488},{48,112},{56,504}... | collective-permute-start | bytes 1474568 | tf_op jit(solution)/shard_map/ppermute | solution.py:199
  60.9 22.6 %collective-permute-start.4 = (bf16[16,88,256]{2,1,0:T(8,128)(2,1)S(1)}, bf16[16,88,256]{2,1,0:T(8,128)(2,1)S(1)}, u32[]{:S(2)}, u32[]{:S(2)}) collective-permute-start(bf16[16,88,256]{2,1,0:T(8,128)(2,1)S(1)} %all-to-all-done.1.refs_0_), channel_id=1, source_target_pairs={{0,48},{8,24},{16,0},{24,40},{32,16},{40,56},{48,32},{56,8},{64,11... | collective-permute-start | bytes 2162696 | tf_op jit(solution)/shard_map/ppermute | solution.py:199
  68.1 10.8 %collective-permute-start.8 = (bf16[640,384]{1,0:T(8,128)(2,1)}, bf16[640,384]{1,0:T(8,128)(2,1)S(1)}, u32[]{:S(2)}, u32[]{:S(2)}) collective-permute-start(bf16[640,384]{1,0:T(8,128)(2,1)} %collective-permute-done.7.refs_7_), channel_id=1, source_target_pairs={{0,64},{8,456},{16,80},{24,472},{32,96},{40,488},{48,112},{56,504}... | collective-permute-start | bytes 1474568 | tf_op jit(solution)/shard_map/ppermute | solution.py:199
  72.2 16.1 %collective-permute-start.3 = (bf16[640,384]{1,0:T(8,128)(2,1)}, bf16[640,384]{1,0:T(8,128)(2,1)S(1)}, u32[]{:S(2)}, u32[]{:S(2)}) collective-permute-start(bf16[640,384]{1,0:T(8,128)(2,1)} %collective-permute-done.1.refs_6_), channel_id=1, source_target_pairs={{0,448},{8,72},{16,464},{24,88},{32,480},{40,104},{48,496},{56,120... | collective-permute-start | bytes 1474568 | tf_op jit(solution)/shard_map/ppermute | solution.py:199
  74.2 17.4 %collective-permute-start.5 = (bf16[16,88,256]{2,1,0:T(8,128)(2,1)}, bf16[16,88,256]{2,1,0:T(8,128)(2,1)S(1)}, u32[]{:S(2)}, u32[]{:S(2)}) collective-permute-start(bf16[16,88,256]{2,1,0:T(8,128)(2,1)} %collective-permute-done.2.refs_1_), channel_id=1, source_target_pairs={{0,16},{8,56},{16,32},{24,8},{32,48},{40,24},{48,0},{56,40},{64,80... | collective-permute-start | bytes 2162696 | tf_op jit(solution)/shard_map/ppermute | solution.py:199
  78.9 12.7 %collective-permute-start.10 = (bf16[640,384]{1,0:T(8,128)(2,1)S(1)}, bf16[640,384]{1,0:T(8,128)(2,1)S(1)}, u32[]{:S(2)}, u32[]{:S(2)}) collective-permute-start(bf16[640,384]{1,0:T(8,128)(2,1)S(1)} %collective-permute-done.8.refs_9_), channel_id=1, source_target_pairs={{0,64},{8,456},{16,80},{24,472},{32,96},{40,488},{48,112},{56,504}... | collective-permute-start | bytes 1474568 | tf_op jit(solution)/shard_map/ppermute | solution.py:199
  88.3 16.0 %collective-permute-start.9 = (bf16[640,384]{1,0:T(8,128)(2,1)S(1)}, bf16[640,384]{1,0:T(8,128)(2,1)S(1)}, u32[]{:S(2)}, u32[]{:S(2)}) collective-permute-start(bf16[640,384]{1,0:T(8,128)(2,1)S(1)} %collective-permute-done.3.refs_8_), channel_id=1, source_target_pairs={{0,448},{8,72},{16,464},{24,88},{32,480},{40,104},{48,496},{56,120... | collective-permute-start | bytes 1474568 | tf_op jit(solution)/shard_map/ppermute | solution.py:199
  104.2 28.9 %copy-start.3 = (bf16[1,2,640]{2,1,0:T(2,128)(2,1)S(1)}, bf16[1,2,640]{2,1,0:T(2,128)(2,1)}, u32[]{:S(2)}) copy-start(bf16[1,2,640]{2,1,0:T(2,128)(2,1)} %param.16) | copy-start | bytes 7684
  111.7 4.0 %collective-permute-start.11 = (bf16[256,640]{1,0:T(8,128)(2,1)S(1)}, bf16[256,640]{1,0:T(8,128)(2,1)S(1)}, u32[]{:S(2)}, u32[]{:S(2)}) collective-permute-start(bf16[256,640]{1,0:T(8,128)(2,1)S(1)} %get-tuple-element.18), channel_id=1, source_target_pairs={{0,8},{8,0},{1,9},{9,1},{2,10},{10,2},{3,11},{11,3},{4,12},{12,4},... | collective-permute-start | bytes 983048 | tf_op jit(solution)/shard_map/ppermute | solution.py:34
  134.4 16.0 %all-to-all-start.3 = ((bf16[64,8,128]{2,1,0:T(8,128)(2,1)}), bf16[64,8,128]{2,1,0:T(8,128)(2,1)S(1)}, u32[]{:S(2)}, u32[]{:S(2)}) async-start(bf16[64,8,128]{2,1,0:T(8,128)(2,1)} %shard_map.106), calls=%async_computation.3 | async-start | bytes 262144 | tf_op jit(solution)/shard_map/all_to_all | solution.py:203
  151.3 13.8 %all-to-all-start.4 = ((f32[8,8,80]{2,1,0:T(8,128)}), f32[8,8,80]{2,1,0:T(8,128)S(1)}, u32[]{:S(2)}, u32[]{:S(2)}) async-start(f32[8,8,80]{2,1,0:T(8,128)} %fusion.5), calls=%async_computation.4 | async-start | bytes 65536 | tf_op jit(solution)/shard_map/all_to_all | solution.py:203
  (2 other events, 2.5 us)

commit v7 on v6

--- a/solution.py
+++ b/solution.py
@@ -234,9 +234,7 @@
     saved, block_b, _ = lax.optimization_barrier((saved, block_b, copies_a))
     a_behind, a_ahead = send(pieces_a, 0, 1), send(pieces_a, 0, -1)
     behind1, ahead1 = send(block_b, 1, 0), send(block_b, -1, 0)
-    ahead1, a_behind = lax.optimization_barrier((ahead1, a_behind))
     behind2, ahead2 = send(behind1, 1, 0), send(ahead1, -1, 0)
-    ahead2, a_ahead = lax.optimization_barrier((ahead2, a_ahead))
     behind3, ahead3 = send(behind2, 1, 0), send(ahead2, -1, 0)
     a_blocks = (pieces_a, a_behind, a_ahead, send(a_behind, 0, 1))
     b_blocks = (block_b, behind1, ahead1, behind2, ahead2, behind3, ahead3, send(behind3, 1, 0))

time: 167 us -> 170 us (1.018)
  blocking collectives: 14.9 us -> 19.1 us
  waiting for transfers between devices: 57.2 us -> 54.3 us
  starting transfers between devices: 66.7 us -> 69.4 us
    all_to_all x4, waiting for transfers between devices: 34.1 us -> 22.1 us  [exchange(): return lax.all_to_all(value, axis, 0, 0, tiled=True)]
    ppermute x10, waiting for transfers between devices: 22 us -> 31.1 us  [send(): return lax.ppermute(value, GROUP, pairs)]
    all_to_all x1, blocking collectives: 14.9 us -> 19.1 us  [exchange(): return lax.all_to_all(value, axis, 0, 0, tiled=True)]
    ppermute x2, starting transfers between devices: 4.72 us -> 7.32 us  [swap_cores(): return lax.ppermute(value, 'core', [(0, 1), (1, 0)])]
where the time goes in v7:
time: 170 us
  starting transfers between devices  69.4 us (41%)
  waiting for transfers between devices  54.3 us (32%)
  blocking collectives  19.1 us (11%)
  Pallas kernels  10.5 us (6%)
  other arithmetic  7.51 us (4%)
  local copies, waits for them, and re-layouts  6.23 us (4%)
    ppermute x10, starting transfers between devices, send(): return lax.ppermute(value, GROUP, pairs)  33.6 us
    ppermute x10, waiting for transfers between devices, send(): return lax.ppermute(value, GROUP, pairs)  31.1 us
    all_to_all x4, starting transfers between devices, exchange(): return lax.all_to_all(value, axis, 0, 0, tiled=True)  28.5 us
    all_to_all x4, waiting for transfers between devices, exchange(): return lax.all_to_all(value, axis, 0, 0, tiled=True)  22.1 us
    all_to_all x1, blocking collectives, exchange(): return lax.all_to_all(value, axis, 0, 0, tiled=True)  19.1 us
    pallas_call x1, Pallas kernels, project(): pl.pallas_call(project_kernel, in_specs=[pl.BlockSpec(memory_space=pltpu....  7.36 us
    ppermute x2, starting transfers between devices, swap_cores(): return lax.ppermute(value, 'core', [(0, 1), (1, 0)])  7.32 us
  transfers between devices with their start and end apart: 16, of which 8 were waited for; matrix products, arithmetic and copies ran while one was open for 5% of the time, Pallas kernels for 0%

profile of v7, /device:TPU:1, one launch (start us, length us, event | category | flops | bytes accessed | tf_op | source)
XLA Modules:
  0.0 169.5 jit_solution(2790677648655907067)
XLA Ops:
  2.8 11.0 %all-to-all-start = ((bf16[8,80,384]{2,1,0:T(8,128)(2,1)}), bf16[8,80,384]{2,1,0:T(8,128)(2,1)}, u32[]{:S(2)}, u32[]{:S(2)}) async-start(bf16[8,80,384]{2,1,0:T(8,128)(2,1)} %bitcast.5), calls=%async_computation | async-start | bytes 983040 | tf_op jit(solution)/shard_map/all_to_all | solution.py:203
  14.9 8.2 %all-to-all-done = bf16[8,80,384]{2,1,0:T(8,128)(2,1)} async-done(((bf16[8,80,384]{2,1,0:T(8,128)(2,1)}), bf16[8,80,384]{2,1,0:T(8,128)(2,1)}, u32[]{:S(2)}, u32[]{:S(2)}) %all-to-all-start) | async-done | bytes 491552 | tf_op jit(solution)/shard_map/all_to_all | solution.py:203
  24.0 6.1 %all-to-all-start.1 = ((bf16[16,88,256]{2,1,0:T(8,128)(2,1)}), bf16[16,88,256]{2,1,0:T(8,128)(2,1)S(1)}, u32[]{:S(2)}, u32[]{:S(2)}) async-start(bf16[16,88,256]{2,1,0:T(8,128)(2,1)} %bitcast.40), calls=%async_computation.1 | async-start | bytes 1441792 | tf_op jit(solution)/shard_map/all_to_all | solution.py:203
  32.6 2.0 %collective-permute-start = (bf16[256,5120]{1,0:T(8,128)(2,1)S(1)}, bf16[256,5120]{1,0:T(8,128)(2,1)}, u32[]{:S(2)}, u32[]{:S(2)}) collective-permute-start(bf16[256,5120]{1,0:T(8,128)(2,1)S(1)} %bitcast.37), channel_id=1, source_target_pairs={{0,8},{8,0},{1,9},{9,1},{2,10},{10,2},{3,11},{11,3},{4,12},{12,4},... | collective-permute-start | bytes 7864328 | tf_op jit(solution)/shard_map/ppermute | solution.py:34
  34.6 4.8 %collective-permute-start.4 = (bf16[640,384]{1,0:T(8,128)(2,1)}, bf16[640,384]{1,0:T(8,128)(2,1)}, u32[]{:S(2)}, u32[]{:S(2)}) collective-permute-start(bf16[640,384]{1,0:T(8,128)(2,1)} %bitcast.6.refs_4_), channel_id=1, source_target_pairs={{0,64},{8,456},{16,80},{24,472},{32,96},{40,488},{48,112},{56,504}... | collective-permute-start | bytes 1474568 | tf_op jit(solution)/shard_map/ppermute | solution.py:199
  41.4 17.2 %collective-permute-done.4.refs_5_ = bf16[640,384]{1,0:T(8,128)(2,1)} collective-permute-done((bf16[640,384]{1,0:T(8,128)(2,1)}, bf16[640,384]{1,0:T(8,128)(2,1)}, u32[]{:S(2)}, u32[]{:S(2)}) %collective-permute-start.4) | collective-permute-done | bytes 491552 | tf_op jit(solution)/shard_map/ppermute | solution.py:199
  58.6 3.4 %collective-permute-start.6 = (bf16[640,384]{1,0:T(8,128)(2,1)}, bf16[640,384]{1,0:T(8,128)(2,1)}, u32[]{:S(2)}, u32[]{:S(2)}) collective-permute-start(bf16[640,384]{1,0:T(8,128)(2,1)} %collective-permute-done.4.refs_5_), channel_id=1, source_target_pairs={{0,64},{8,456},{16,80},{24,472},{32,96},{40,488},{48,112},{56,504}... | collective-permute-start | bytes 1474568 | tf_op jit(solution)/shard_map/ppermute | solution.py:199
  64.1 2.8 %collective-permute-start.1 = (bf16[16,88,256]{2,1,0:T(8,128)(2,1)S(1)}, bf16[16,88,256]{2,1,0:T(8,128)(2,1)S(1)}, u32[]{:S(2)}, u32[]{:S(2)}) collective-permute-start(bf16[16,88,256]{2,1,0:T(8,128)(2,1)S(1)} %all-to-all-done.1.refs_0_), channel_id=1, source_target_pairs={{0,16},{8,56},{16,32},{24,8},{32,48},{40,24},{48,0},{56,40},{64,80... | collective-permute-start | bytes 2162696 | tf_op jit(solution)/shard_map/ppermute | solution.py:199
  66.9 2.5 %collective-permute-start.2 = (bf16[16,88,256]{2,1,0:T(8,128)(2,1)S(1)}, bf16[16,88,256]{2,1,0:T(8,128)(2,1)S(1)}, u32[]{:S(2)}, u32[]{:S(2)}) collective-permute-start(bf16[16,88,256]{2,1,0:T(8,128)(2,1)S(1)} %all-to-all-done.1.refs_0_), channel_id=1, source_target_pairs={{0,48},{8,24},{16,0},{24,40},{32,16},{40,56},{48,32},{56,8},{64,11... | collective-permute-start | bytes 2162696 | tf_op jit(solution)/shard_map/ppermute | solution.py:199
  69.6 4.6 %collective-permute-start.8 = (bf16[640,384]{1,0:T(8,128)(2,1)}, bf16[640,384]{1,0:T(8,128)(2,1)S(1)}, u32[]{:S(2)}, u32[]{:S(2)}) collective-permute-start(bf16[640,384]{1,0:T(8,128)(2,1)} %collective-permute-done.6.refs_7_), channel_id=1, source_target_pairs={{0,64},{8,456},{16,80},{24,472},{32,96},{40,488},{48,112},{56,504}... | collective-permute-start | bytes 1474568 | tf_op jit(solution)/shard_map/ppermute | solution.py:199
  74.3 3.1 %collective-permute-done.1.refs_1_ = bf16[16,88,256]{2,1,0:T(8,128)(2,1)S(1)} collective-permute-done((bf16[16,88,256]{2,1,0:T(8,128)(2,1)S(1)}, bf16[16,88,256]{2,1,0:T(8,128)(2,1)S(1)}, u32[]{:S(2)}, u32[]{:S(2)}) %collective-permute-start.1) | collective-permute-done | bytes 720928 | tf_op jit(solution)/shard_map/ppermute | solution.py:199
  77.4 2.7 %collective-permute-start.3 = (bf16[16,88,256]{2,1,0:T(8,128)(2,1)S(1)}, bf16[16,88,256]{2,1,0:T(8,128)(2,1)S(1)}, u32[]{:S(2)}, u32[]{:S(2)}) collective-permute-start(bf16[16,88,256]{2,1,0:T(8,128)(2,1)S(1)} %collective-permute-done.1.refs_1_), channel_id=1, source_target_pairs={{0,16},{8,56},{16,32},{24,8},{32,48},{40,24},{48,0},{56,40},{64,80... | collective-permute-start | bytes 2162696 | tf_op jit(solution)/shard_map/ppermute | solution.py:199
  80.3 5.5 %collective-permute-start.9 = (bf16[640,384]{1,0:T(8,128)(2,1)}, bf16[640,384]{1,0:T(8,128)(2,1)S(1)}, u32[]{:S(2)}, u32[]{:S(2)}) collective-permute-start(bf16[640,384]{1,0:T(8,128)(2,1)} %collective-permute-done.7.refs_8_), channel_id=1, source_target_pairs={{0,448},{8,72},{16,464},{24,88},{32,480},{40,104},{48,496},{56,120... | collective-permute-start | bytes 1474568 | tf_op jit(solution)/shard_map/ppermute | solution.py:199
  85.8 3.5 %collective-permute-start.10 = (bf16[640,384]{1,0:T(8,128)(2,1)S(1)}, bf16[640,384]{1,0:T(8,128)(2,1)S(1)}, u32[]{:S(2)}, u32[]{:S(2)}) collective-permute-start(bf16[640,384]{1,0:T(8,128)(2,1)S(1)} %collective-permute-done.8.refs_9_), channel_id=1, source_target_pairs={{0,64},{8,456},{16,80},{24,472},{32,96},{40,488},{48,112},{56,504}... | collective-permute-start | bytes 1474568 | tf_op jit(solution)/shard_map/ppermute | solution.py:199
  90.6 3.2 %collective-permute-done.9.refs_10_ = bf16[640,384]{1,0:T(8,128)(2,1)S(1)} collective-permute-done((bf16[640,384]{1,0:T(8,128)(2,1)}, bf16[640,384]{1,0:T(8,128)(2,1)S(1)}, u32[]{:S(2)}, u32[]{:S(2)}) %collective-permute-start.9) | collective-permute-done | bytes 491552 | tf_op jit(solution)/shard_map/ppermute | solution.py:199
  93.8 7.6 %collective-permute-done.10.refs_11_ = bf16[640,384]{1,0:T(8,128)(2,1)S(1)} collective-permute-done((bf16[640,384]{1,0:T(8,128)(2,1)S(1)}, bf16[640,384]{1,0:T(8,128)(2,1)S(1)}, u32[]{:S(2)}, u32[]{:S(2)}) %collective-permute-start.10) | collective-permute-done | bytes 491552 | tf_op jit(solution)/shard_map/ppermute | solution.py:199
  101.4 7.4 %shard_map.104 = (bf16[256,640]{1,0:T(8,128)(2,1)S(1)}, bf16[256,640]{1,0:T(8,128)(2,1)S(1)}, f32[64,8,256]{2,1,0:T(8,128)S(1)}) custom-call(s32[3]{0:T(128)S(1)} %pad_add_fusion.place_ref, bf16[256,5120]{1,0:T(8,128)(2,1)S(1)} %bitcast.38, bf16[256,5120]{1,0:T(8,128)(2,1)} %collective-permute-done.other_ref, f32[512,128]{1,0:T(8,128)S(1)} %get-tuple-element.29.cos_ref, ...), custom_call_target="tpu_custom_call" | custom-call | flops 3355443200 | bytes 11796480 | tf_op jit(solution)/shard_map/pallas_call | solution.py:87
  108.8 5.3 %collective-permute-start.11 = (bf16[256,640]{1,0:T(8,128)(2,1)S(1)}, bf16[256,640]{1,0:T(8,128)(2,1)S(1)}, u32[]{:S(2)}, u32[]{:S(2)}) collective-permute-start(bf16[256,640]{1,0:T(8,128)(2,1)S(1)} %get-tuple-element.10), channel_id=1, source_target_pairs={{0,8},{8,0},{1,9},{9,1},{2,10},{10,2},{3,11},{11,3},{4,12},{12,4},... | collective-permute-start | bytes 983048 | tf_op jit(solution)/shard_map/ppermute | solution.py:34
  118.0 19.1 %all_to_all.25.parts_ref = bf16[64,8,128]{2,1,0:T(8,128)(2,1)S(1)} all-to-all(bf16[64,8,128]{2,1,0:T(8,128)(2,1)S(1)} %shard_map.105), channel_id=1, replica_groups=mesh['z'=8,'x'=4,'core'=2,'tp'=8] {'z','x','core'}, dimensions={0} | all-to-all | bytes 262144 | tf_op jit(solution)/shard_map/all_to_all | solution.py:203
  138.3 4.6 %all-to-all-start.3 = ((bf16[64,8,128]{2,1,0:T(8,128)(2,1)}), bf16[64,8,128]{2,1,0:T(8,128)(2,1)S(1)}, u32[]{:S(2)}, u32[]{:S(2)}) async-start(bf16[64,8,128]{2,1,0:T(8,128)(2,1)} %shard_map.106), calls=%async_computation.3 | async-start | bytes 262144 | tf_op jit(solution)/shard_map/all_to_all | solution.py:203
  145.0 9.3 %all-to-all-done.3 = bf16[64,8,128]{2,1,0:T(8,128)(2,1)S(1)} async-done(((bf16[64,8,128]{2,1,0:T(8,128)(2,1)}), bf16[64,8,128]{2,1,0:T(8,128)(2,1)S(1)}, u32[]{:S(2)}, u32[]{:S(2)}) %all-to-all-start.3) | async-done | bytes 131104 | tf_op jit(solution)/shard_map/all_to_all | solution.py:203
  155.2 6.8 %all-to-all-start.4 = ((f32[8,8,80]{2,1,0:T(8,128)}), f32[8,8,80]{2,1,0:T(8,128)S(1)}, u32[]{:S(2)}, u32[]{:S(2)}) async-start(f32[8,8,80]{2,1,0:T(8,128)} %fusion.5), calls=%async_computation.4 | async-start | bytes 65536 | tf_op jit(solution)/shard_map/all_to_all | solution.py:203
  162.0 2.3 %pad_maximum_fusion = bf16[2,128,2,640]{3,2,1,0:T(2,128)(2,1)} fusion(bf16[2,128,1,640]{3,2,1,0:T(2,128)(2,1)S(1)} %copy.32, bf16[2,128,1,640]{3,2,1,0:T(2,128)(2,1)S(1)} %copy.31), kind=kLoop, calls=%fused_computation.5 | loop fusion | flops 1310720 | bytes 1310720 | tf_op jit(solution)/shard_map/stack | solution.py:281
  164.3 4.6 %all-to-all-done.4 = f32[8,8,80]{2,1,0:T(8,128)S(1)} async-done(((f32[8,8,80]{2,1,0:T(8,128)}), f32[8,8,80]{2,1,0:T(8,128)S(1)}, u32[]{:S(2)}, u32[]{:S(2)}) %all-to-all-start.4) | async-done | bytes 20512 | tf_op jit(solution)/shard_map/all_to_all | solution.py:203
  (70 shorter events, 20.3 us)
Async XLA Ops:
  0.6 153.8 %copy-start = (bf16[640,80]{0,1:T(8,128)(2,1)S(1)}, bf16[640,80]{0,1:T(8,128)(2,1)}, u32[]{:S(2)}) copy-start(bf16[640,80]{0,1:T(8,128)(2,1)} %param.14) | copy-start | bytes 307204
  0.6 13.2 %copy-start.6 = (bf16[80,2,640]{2,1,0:T(2,128)(2,1)S(1)}, bf16[80,2,640]{2,1,0:T(2,128)(2,1)}, u32[]{:S(2)}) copy-start(bf16[80,2,640]{2,1,0:T(2,128)(2,1)} %param.13) | copy-start | bytes 614404
  0.7 14.0 %copy-start.8 = (s32[2]{0:T(128)S(1)}, s32[2]{0:T(128)}, u32[]{:S(2)}) copy-start(s32[2]{0:T(128)} %param.10) | copy-start | bytes 28
  0.7 14.0 %copy-start.7 = (bf16[5120]{0:T(1024)(128)(2,1)S(1)}, bf16[5120]{0:T(1024)(128)(2,1)}, u32[]{:S(2)}) copy-start(bf16[5120]{0:T(1024)(128)(2,1)} %param.12) | copy-start | bytes 30724
  0.7 14.0 %copy-start.2 = (bf16[1,640]{1,0:T(2,128)(2,1)S(1)}, bf16[1,640]{1,0:T(2,128)(2,1)}, u32[]{:S(2)}) copy-start(bf16[1,640]{1,0:T(2,128)(2,1)} %query_ref.1) | copy-start | bytes 3844
  2.0 28.2 %copy-start.4 = (bf16[2,128,5120]{2,1,0:T(8,128)(2,1)S(1)}, bf16[2,128,5120]{2,1,0:T(8,128)(2,1)}, u32[]{:S(2)}) copy-start(bf16[2,128,5120]{2,1,0:T(8,128)(2,1)} %param.9) | copy-start | bytes 7864324
  2.8 20.3 %all-to-all-start = ((bf16[8,80,384]{2,1,0:T(8,128)(2,1)}), bf16[8,80,384]{2,1,0:T(8,128)(2,1)}, u32[]{:S(2)}, u32[]{:S(2)}) async-start(bf16[8,80,384]{2,1,0:T(8,128)(2,1)} %bitcast.5), calls=%async_computation | async-start | bytes 983040 | tf_op jit(solution)/shard_map/all_to_all | solution.py:203
  24.0 40.0 %all-to-all-start.1 = ((bf16[16,88,256]{2,1,0:T(8,128)(2,1)}), bf16[16,88,256]{2,1,0:T(8,128)(2,1)S(1)}, u32[]{:S(2)}, u32[]{:S(2)}) async-start(bf16[16,88,256]{2,1,0:T(8,128)(2,1)} %bitcast.40), calls=%async_computation.1 | async-start | bytes 1441792 | tf_op jit(solution)/shard_map/all_to_all | solution.py:203
  31.8 48.3 %copy-start.9 = (s32[4]{0:T(128)S(1)}, s32[4]{0:T(128)}, u32[]{:S(2)}) copy-start(s32[4]{0:T(128)} %param.11) | copy-start | bytes 52
  32.6 68.8 %collective-permute-start = (bf16[256,5120]{1,0:T(8,128)(2,1)S(1)}, bf16[256,5120]{1,0:T(8,128)(2,1)}, u32[]{:S(2)}, u32[]{:S(2)}) collective-permute-start(bf16[256,5120]{1,0:T(8,128)(2,1)S(1)} %bitcast.37), channel_id=1, source_target_pairs={{0,8},{8,0},{1,9},{9,1},{2,10},{10,2},{3,11},{11,3},{4,12},{12,4},... | collective-permute-start | bytes 7864328 | tf_op jit(solution)/shard_map/ppermute | solution.py:34
  34.6 23.9 %collective-permute-start.4 = (bf16[640,384]{1,0:T(8,128)(2,1)}, bf16[640,384]{1,0:T(8,128)(2,1)}, u32[]{:S(2)}, u32[]{:S(2)}) collective-permute-start(bf16[640,384]{1,0:T(8,128)(2,1)} %bitcast.6.refs_4_), channel_id=1, source_target_pairs={{0,64},{8,456},{16,80},{24,472},{32,96},{40,488},{48,112},{56,504}... | collective-permute-start | bytes 1474568 | tf_op jit(solution)/shard_map/ppermute | solution.py:199
  39.4 22.7 %collective-permute-start.5 = (bf16[640,384]{1,0:T(8,128)(2,1)}, bf16[640,384]{1,0:T(8,128)(2,1)}, u32[]{:S(2)}, u32[]{:S(2)}) collective-permute-start(bf16[640,384]{1,0:T(8,128)(2,1)} %bitcast.6.refs_4_), channel_id=1, source_target_pairs={{0,448},{8,72},{16,464},{24,88},{32,480},{40,104},{48,496},{56,120... | collective-permute-start | bytes 1474568 | tf_op jit(solution)/shard_map/ppermute | solution.py:199
  58.6 11.0 %collective-permute-start.6 = (bf16[640,384]{1,0:T(8,128)(2,1)}, bf16[640,384]{1,0:T(8,128)(2,1)}, u32[]{:S(2)}, u32[]{:S(2)}) collective-permute-start(bf16[640,384]{1,0:T(8,128)(2,1)} %collective-permute-done.4.refs_5_), channel_id=1, source_target_pairs={{0,64},{8,456},{16,80},{24,472},{32,96},{40,488},{48,112},{56,504}... | collective-permute-start | bytes 1474568 | tf_op jit(solution)/shard_map/ppermute | solution.py:199
  62.1 18.2 %collective-permute-start.7 = (bf16[640,384]{1,0:T(8,128)(2,1)}, bf16[640,384]{1,0:T(8,128)(2,1)}, u32[]{:S(2)}, u32[]{:S(2)}) collective-permute-start(bf16[640,384]{1,0:T(8,128)(2,1)} %collective-permute-done.5.refs_6_), channel_id=1, source_target_pairs={{0,448},{8,72},{16,464},{24,88},{32,480},{40,104},{48,496},{56,120... | collective-permute-start | bytes 1474568 | tf_op jit(solution)/shard_map/ppermute | solution.py:199
  64.1 13.3 %collective-permute-start.1 = (bf16[16,88,256]{2,1,0:T(8,128)(2,1)S(1)}, bf16[16,88,256]{2,1,0:T(8,128)(2,1)S(1)}, u32[]{:S(2)}, u32[]{:S(2)}) collective-permute-start(bf16[16,88,256]{2,1,0:T(8,128)(2,1)S(1)} %all-to-all-done.1.refs_0_), channel_id=1, source_target_pairs={{0,16},{8,56},{16,32},{24,8},{32,48},{40,24},{48,0},{56,40},{64,80... | collective-permute-start | bytes 2162696 | tf_op jit(solution)/shard_map/ppermute | solution.py:199
  66.9 26.9 %collective-permute-start.2 = (bf16[16,88,256]{2,1,0:T(8,128)(2,1)S(1)}, bf16[16,88,256]{2,1,0:T(8,128)(2,1)S(1)}, u32[]{:S(2)}, u32[]{:S(2)}) collective-permute-start(bf16[16,88,256]{2,1,0:T(8,128)(2,1)S(1)} %all-to-all-done.1.refs_0_), channel_id=1, source_target_pairs={{0,48},{8,24},{16,0},{24,40},{32,16},{40,56},{48,32},{56,8},{64,11... | collective-permute-start | bytes 2162696 | tf_op jit(solution)/shard_map/ppermute | solution.py:199
  69.6 16.2 %collective-permute-start.8 = (bf16[640,384]{1,0:T(8,128)(2,1)}, bf16[640,384]{1,0:T(8,128)(2,1)S(1)}, u32[]{:S(2)}, u32[]{:S(2)}) collective-permute-start(bf16[640,384]{1,0:T(8,128)(2,1)} %collective-permute-done.6.refs_7_), channel_id=1, source_target_pairs={{0,64},{8,456},{16,80},{24,472},{32,96},{40,488},{48,112},{56,504}... | collective-permute-start | bytes 1474568 | tf_op jit(solution)/shard_map/ppermute | solution.py:199
  77.4 24.0 %collective-permute-start.3 = (bf16[16,88,256]{2,1,0:T(8,128)(2,1)S(1)}, bf16[16,88,256]{2,1,0:T(8,128)(2,1)S(1)}, u32[]{:S(2)}, u32[]{:S(2)}) collective-permute-start(bf16[16,88,256]{2,1,0:T(8,128)(2,1)S(1)} %collective-permute-done.1.refs_1_), channel_id=1, source_target_pairs={{0,16},{8,56},{16,32},{24,8},{32,48},{40,24},{48,0},{56,40},{64,80... | collective-permute-start | bytes 2162696 | tf_op jit(solution)/shard_map/ppermute | solution.py:199
  80.3 13.5 %collective-permute-start.9 = (bf16[640,384]{1,0:T(8,128)(2,1)}, bf16[640,384]{1,0:T(8,128)(2,1)S(1)}, u32[]{:S(2)}, u32[]{:S(2)}) collective-permute-start(bf16[640,384]{1,0:T(8,128)(2,1)} %collective-permute-done.7.refs_8_), channel_id=1, source_target_pairs={{0,448},{8,72},{16,464},{24,88},{32,480},{40,104},{48,496},{56,120... | collective-permute-start | bytes 1474568 | tf_op jit(solution)/shard_map/ppermute | solution.py:199
  85.8 15.6 %collective-permute-start.10 = (bf16[640,384]{1,0:T(8,128)(2,1)S(1)}, bf16[640,384]{1,0:T(8,128)(2,1)S(1)}, u32[]{:S(2)}, u32[]{:S(2)}) collective-permute-start(bf16[640,384]{1,0:T(8,128)(2,1)S(1)} %collective-permute-done.8.refs_9_), channel_id=1, source_target_pairs={{0,64},{8,456},{16,80},{24,472},{32,96},{40,488},{48,112},{56,504}... | collective-permute-start | bytes 1474568 | tf_op jit(solution)/shard_map/ppermute | solution.py:199
  101.4 35.7 %copy-start.3 = (bf16[1,2,640]{2,1,0:T(2,128)(2,1)S(1)}, bf16[1,2,640]{2,1,0:T(2,128)(2,1)}, u32[]{:S(2)}) copy-start(bf16[1,2,640]{2,1,0:T(2,128)(2,1)} %param.16) | copy-start | bytes 7684
  108.8 6.5 %collective-permute-start.11 = (bf16[256,640]{1,0:T(8,128)(2,1)S(1)}, bf16[256,640]{1,0:T(8,128)(2,1)S(1)}, u32[]{:S(2)}, u32[]{:S(2)}) collective-permute-start(bf16[256,640]{1,0:T(8,128)(2,1)S(1)} %get-tuple-element.10), channel_id=1, source_target_pairs={{0,8},{8,0},{1,9},{9,1},{2,10},{10,2},{3,11},{11,3},{4,12},{12,4},... | collective-permute-start | bytes 983048 | tf_op jit(solution)/shard_map/ppermute | solution.py:34
  138.3 16.0 %all-to-all-start.3 = ((bf16[64,8,128]{2,1,0:T(8,128)(2,1)}), bf16[64,8,128]{2,1,0:T(8,128)(2,1)S(1)}, u32[]{:S(2)}, u32[]{:S(2)}) async-start(bf16[64,8,128]{2,1,0:T(8,128)(2,1)} %shard_map.106), calls=%async_computation.3 | async-start | bytes 262144 | tf_op jit(solution)/shard_map/all_to_all | solution.py:203
  155.2 13.8 %all-to-all-start.4 = ((f32[8,8,80]{2,1,0:T(8,128)}), f32[8,8,80]{2,1,0:T(8,128)S(1)}, u32[]{:S(2)}, u32[]{:S(2)}) async-start(f32[8,8,80]{2,1,0:T(8,128)} %fusion.5), calls=%async_computation.4 | async-start | bytes 65536 | tf_op jit(solution)/shard_map/all_to_all | solution.py:203
  (2 other events, 2.5 us)

commit v8 on v6

--- a/solution.py
+++ b/solution.py
@@ -234,6 +234,7 @@
     saved, block_b, _ = lax.optimization_barrier((saved, block_b, copies_a))
     a_behind, a_ahead = send(pieces_a, 0, 1), send(pieces_a, 0, -1)
     behind1, ahead1 = send(block_b, 1, 0), send(block_b, -1, 0)
+    behind1, ahead1 = lax.optimization_barrier((behind1, ahead1))
     ahead1, a_behind = lax.optimization_barrier((ahead1, a_behind))
     behind2, ahead2 = send(behind1, 1, 0), send(ahead1, -1, 0)
     ahead2, a_ahead = lax.optimization_barrier((ahead2, a_ahead))

time: 167 us -> 168 us (level)
  waiting for transfers between devices: 57.2 us -> 62 us
  starting transfers between devices: 66.7 us -> 63.6 us
    ppermute x10, waiting for transfers between devices: 22 us -> 28.7 us  [send(): return lax.ppermute(value, GROUP, pairs)]
    ppermute x10, starting transfers between devices: 33.5 us -> 30.4 us  [send(): return lax.ppermute(value, GROUP, pairs)]
    all_to_all x4, waiting for transfers between devices: 34.1 us -> 32.2 us  [exchange(): return lax.all_to_all(value, axis, 0, 0, tiled=True)]
  transfers between devices with their start and end apart: 16 -> 16, of which waited for: 8 -> 11; matrix products, arithmetic and copies ran while one was open for 5% -> 5% of each run, Pallas kernels for 0% -> 0%
where the time goes in v8:
time: 168 us; the launch traced here: 167 us
  starting transfers between devices  63.6 us (38%)
  waiting for transfers between devices  62 us (37%)
  blocking collectives  14.9 us (9%)
  Pallas kernels  10.5 us (6%)
  other arithmetic  7.51 us (4%)
  local copies, waits for them, and re-layouts  6.23 us (4%)
  between operations  1.7 us (1%)
    all_to_all x4, waiting for transfers between devices, exchange(): return lax.all_to_all(value, axis, 0, 0, tiled=True)  32.2 us
    ppermute x10, starting transfers between devices, send(): return lax.ppermute(value, GROUP, pairs)  30.4 us
    ppermute x10, waiting for transfers between devices, send(): return lax.ppermute(value, GROUP, pairs)  28.7 us
    all_to_all x4, starting transfers between devices, exchange(): return lax.all_to_all(value, axis, 0, 0, tiled=True)  28.5 us
    all_to_all x1, blocking collectives, exchange(): return lax.all_to_all(value, axis, 0, 0, tiled=True)  14.9 us
    pallas_call x1, Pallas kernels, project(): pl.pallas_call(project_kernel, in_specs=[pl.BlockSpec(memory_space=pltpu....  7.4 us
    ppermute x2, starting transfers between devices, swap_cores(): return lax.ppermute(value, 'core', [(0, 1), (1, 0)])  4.62 us
  transfers between devices with their start and end apart: 16, of which 11 were waited for; matrix products, arithmetic and copies ran while one was open for 5% of the time, Pallas kernels for 0%

profile of v8, /device:TPU:1, one launch (start us, length us, event | category | flops | bytes accessed | tf_op | source)
XLA Modules:
  0.0 167.2 jit_solution(12136933533486670798)
XLA Ops:
  2.8 11.0 %all-to-all-start = ((bf16[8,80,384]{2,1,0:T(8,128)(2,1)}), bf16[8,80,384]{2,1,0:T(8,128)(2,1)}, u32[]{:S(2)}, u32[]{:S(2)}) async-start(bf16[8,80,384]{2,1,0:T(8,128)(2,1)} %bitcast.5), calls=%async_computation | async-start | bytes 983040 | tf_op jit(solution)/shard_map/all_to_all | solution.py:203
  14.9 8.2 %all-to-all-done = bf16[8,80,384]{2,1,0:T(8,128)(2,1)} async-done(((bf16[8,80,384]{2,1,0:T(8,128)(2,1)}), bf16[8,80,384]{2,1,0:T(8,128)(2,1)}, u32[]{:S(2)}, u32[]{:S(2)}) %all-to-all-start) | async-done | bytes 491552 | tf_op jit(solution)/shard_map/all_to_all | solution.py:203
  24.0 6.1 %all-to-all-start.1 = ((bf16[16,88,256]{2,1,0:T(8,128)(2,1)}), bf16[16,88,256]{2,1,0:T(8,128)(2,1)S(1)}, u32[]{:S(2)}, u32[]{:S(2)}) async-start(bf16[16,88,256]{2,1,0:T(8,128)(2,1)} %bitcast.40), calls=%async_computation.1 | async-start | bytes 1441792 | tf_op jit(solution)/shard_map/all_to_all | solution.py:203
  32.6 2.0 %collective-permute-start = (bf16[256,5120]{1,0:T(8,128)(2,1)S(1)}, bf16[256,5120]{1,0:T(8,128)(2,1)}, u32[]{:S(2)}, u32[]{:S(2)}) collective-permute-start(bf16[256,5120]{1,0:T(8,128)(2,1)S(1)} %bitcast.37), channel_id=1, source_target_pairs={{0,8},{8,0},{1,9},{9,1},{2,10},{10,2},{3,11},{11,3},{4,12},{12,4},... | collective-permute-start | bytes 7864328 | tf_op jit(solution)/shard_map/ppermute | solution.py:34
  34.6 4.8 %collective-permute-start.1 = (bf16[640,384]{1,0:T(8,128)(2,1)}, bf16[640,384]{1,0:T(8,128)(2,1)}, u32[]{:S(2)}, u32[]{:S(2)}) collective-permute-start(bf16[640,384]{1,0:T(8,128)(2,1)} %bitcast.6.refs_4_), channel_id=1, source_target_pairs={{0,64},{8,456},{16,80},{24,472},{32,96},{40,488},{48,112},{56,504}... | collective-permute-start | bytes 1474568 | tf_op jit(solution)/shard_map/ppermute | solution.py:199
  41.4 10.1 %all-to-all-done.1.refs_0_ = bf16[16,88,256]{2,1,0:T(8,128)(2,1)S(1)} async-done(((bf16[16,88,256]{2,1,0:T(8,128)(2,1)}), bf16[16,88,256]{2,1,0:T(8,128)(2,1)S(1)}, u32[]{:S(2)}, u32[]{:S(2)}) %all-to-all-start.1) | async-done | bytes 720928 | tf_op jit(solution)/shard_map/all_to_all | solution.py:203
  51.4 2.8 %collective-permute-start.3 = (bf16[16,88,256]{2,1,0:T(8,128)(2,1)S(1)}, bf16[16,88,256]{2,1,0:T(8,128)(2,1)}, u32[]{:S(2)}, u32[]{:S(2)}) collective-permute-start(bf16[16,88,256]{2,1,0:T(8,128)(2,1)S(1)} %all-to-all-done.1.refs_0_), channel_id=1, source_target_pairs={{0,16},{8,56},{16,32},{24,8},{32,48},{40,24},{48,0},{56,40},{64,80... | collective-permute-start | bytes 2162696 | tf_op jit(solution)/shard_map/ppermute | solution.py:199
  54.2 4.4 %collective-permute-done.1.refs_5_ = bf16[640,384]{1,0:T(8,128)(2,1)} collective-permute-done((bf16[640,384]{1,0:T(8,128)(2,1)}, bf16[640,384]{1,0:T(8,128)(2,1)}, u32[]{:S(2)}, u32[]{:S(2)}) %collective-permute-start.1) | collective-permute-done | bytes 491552 | tf_op jit(solution)/shard_map/ppermute | solution.py:199
  59.8 3.1 %collective-permute-start.7 = (bf16[640,384]{1,0:T(8,128)(2,1)}, bf16[640,384]{1,0:T(8,128)(2,1)}, u32[]{:S(2)}, u32[]{:S(2)}) collective-permute-start(bf16[640,384]{1,0:T(8,128)(2,1)} %collective-permute-done.1.refs_5_), channel_id=1, source_target_pairs={{0,64},{8,456},{16,80},{24,472},{32,96},{40,488},{48,112},{56,504}... | collective-permute-start | bytes 1474568 | tf_op jit(solution)/shard_map/ppermute | solution.py:199
  63.0 2.2 %collective-permute-start.5 = (bf16[16,88,256]{2,1,0:T(8,128)(2,1)S(1)}, bf16[16,88,256]{2,1,0:T(8,128)(2,1)S(1)}, u32[]{:S(2)}, u32[]{:S(2)}) collective-permute-start(bf16[16,88,256]{2,1,0:T(8,128)(2,1)S(1)} %all-to-all-done.1.refs_0_), channel_id=1, source_target_pairs={{0,48},{8,24},{16,0},{24,40},{32,16},{40,56},{48,32},{56,8},{64,11... | collective-permute-start | bytes 2162696 | tf_op jit(solution)/shard_map/ppermute | solution.py:199
  65.4 4.6 %collective-permute-done.7.refs_7_ = bf16[640,384]{1,0:T(8,128)(2,1)} collective-permute-done((bf16[640,384]{1,0:T(8,128)(2,1)}, bf16[640,384]{1,0:T(8,128)(2,1)}, u32[]{:S(2)}, u32[]{:S(2)}) %collective-permute-start.7) | collective-permute-done | bytes 491552 | tf_op jit(solution)/shard_map/ppermute | solution.py:199
  69.9 4.0 %collective-permute-start.8 = (bf16[640,384]{1,0:T(8,128)(2,1)}, bf16[640,384]{1,0:T(8,128)(2,1)S(1)}, u32[]{:S(2)}, u32[]{:S(2)}) collective-permute-start(bf16[640,384]{1,0:T(8,128)(2,1)} %collective-permute-done.7.refs_7_), channel_id=1, source_target_pairs={{0,64},{8,456},{16,80},{24,472},{32,96},{40,488},{48,112},{56,504}... | collective-permute-start | bytes 1474568 | tf_op jit(solution)/shard_map/ppermute | solution.py:199
  76.0 3.0 %collective-permute-start.6 = (bf16[16,88,256]{2,1,0:T(8,128)(2,1)}, bf16[16,88,256]{2,1,0:T(8,128)(2,1)S(1)}, u32[]{:S(2)}, u32[]{:S(2)}) collective-permute-start(bf16[16,88,256]{2,1,0:T(8,128)(2,1)} %collective-permute-done.3.refs_1_), channel_id=1, source_target_pairs={{0,16},{8,56},{16,32},{24,8},{32,48},{40,24},{48,0},{56,40},{64,80... | collective-permute-start | bytes 2162696 | tf_op jit(solution)/shard_map/ppermute | solution.py:199
  80.0 4.9 %collective-permute-start.10 = (bf16[640,384]{1,0:T(8,128)(2,1)S(1)}, bf16[640,384]{1,0:T(8,128)(2,1)S(1)}, u32[]{:S(2)}, u32[]{:S(2)}) collective-permute-start(bf16[640,384]{1,0:T(8,128)(2,1)S(1)} %collective-permute-done.8.refs_9_), channel_id=1, source_target_pairs={{0,64},{8,456},{16,80},{24,472},{32,96},{40,488},{48,112},{56,504}... | collective-permute-start | bytes 1474568 | tf_op jit(solution)/shard_map/ppermute | solution.py:199
  84.9 5.0 %collective-permute-done.4.refs_8_ = bf16[640,384]{1,0:T(8,128)(2,1)S(1)} collective-permute-done((bf16[640,384]{1,0:T(8,128)(2,1)}, bf16[640,384]{1,0:T(8,128)(2,1)S(1)}, u32[]{:S(2)}, u32[]{:S(2)}) %collective-permute-start.4) | collective-permute-done | bytes 491552 | tf_op jit(solution)/shard_map/ppermute | solution.py:199
  93.2 12.8 %collective-permute-done.9.refs_10_ = bf16[640,384]{1,0:T(8,128)(2,1)S(1)} collective-permute-done((bf16[640,384]{1,0:T(8,128)(2,1)S(1)}, bf16[640,384]{1,0:T(8,128)(2,1)S(1)}, u32[]{:S(2)}, u32[]{:S(2)}) %collective-permute-start.9) | collective-permute-done | bytes 491552 | tf_op jit(solution)/shard_map/ppermute | solution.py:199
  105.9 7.4 %shard_map.104 = (bf16[256,640]{1,0:T(8,128)(2,1)S(1)}, bf16[256,640]{1,0:T(8,128)(2,1)S(1)}, f32[64,8,256]{2,1,0:T(8,128)S(1)}) custom-call(s32[3]{0:T(128)S(1)} %pad_add_fusion.place_ref, bf16[256,5120]{1,0:T(8,128)(2,1)S(1)} %bitcast.38, bf16[256,5120]{1,0:T(8,128)(2,1)} %collective-permute-done.other_ref, f32[512,128]{1,0:T(8,128)S(1)} %get-tuple-element.41.cos_ref, ...), custom_call_target="tpu_custom_call" | custom-call | flops 3355443200 | bytes 11796480 | tf_op jit(solution)/shard_map/pallas_call | solution.py:87
  113.3 2.6 %collective-permute-start.11 = (bf16[256,640]{1,0:T(8,128)(2,1)S(1)}, bf16[256,640]{1,0:T(8,128)(2,1)S(1)}, u32[]{:S(2)}, u32[]{:S(2)}) collective-permute-start(bf16[256,640]{1,0:T(8,128)(2,1)S(1)} %get-tuple-element.22), channel_id=1, source_target_pairs={{0,8},{8,0},{1,9},{9,1},{2,10},{10,2},{3,11},{11,3},{4,12},{12,4},... | collective-permute-start | bytes 983048 | tf_op jit(solution)/shard_map/ppermute | solution.py:34
  119.8 14.9 %all_to_all.25.parts_ref = bf16[64,8,128]{2,1,0:T(8,128)(2,1)S(1)} all-to-all(bf16[64,8,128]{2,1,0:T(8,128)(2,1)S(1)} %shard_map.105), channel_id=1, replica_groups=mesh['z'=8,'x'=4,'core'=2,'tp'=8] {'z','x','core'}, dimensions={0} | all-to-all | bytes 262144 | tf_op jit(solution)/shard_map/all_to_all | solution.py:203
  135.9 4.6 %all-to-all-start.3 = ((bf16[64,8,128]{2,1,0:T(8,128)(2,1)}), bf16[64,8,128]{2,1,0:T(8,128)(2,1)S(1)}, u32[]{:S(2)}, u32[]{:S(2)}) async-start(bf16[64,8,128]{2,1,0:T(8,128)(2,1)} %shard_map.106), calls=%async_computation.3 | async-start | bytes 262144 | tf_op jit(solution)/shard_map/all_to_all | solution.py:203
  142.7 9.3 %all-to-all-done.3 = bf16[64,8,128]{2,1,0:T(8,128)(2,1)S(1)} async-done(((bf16[64,8,128]{2,1,0:T(8,128)(2,1)}), bf16[64,8,128]{2,1,0:T(8,128)(2,1)S(1)}, u32[]{:S(2)}, u32[]{:S(2)}) %all-to-all-start.3) | async-done | bytes 131104 | tf_op jit(solution)/shard_map/all_to_all | solution.py:203
  152.8 6.8 %all-to-all-start.4 = ((f32[8,8,80]{2,1,0:T(8,128)}), f32[8,8,80]{2,1,0:T(8,128)S(1)}, u32[]{:S(2)}, u32[]{:S(2)}) async-start(f32[8,8,80]{2,1,0:T(8,128)} %fusion.5), calls=%async_computation.4 | async-start | bytes 65536 | tf_op jit(solution)/shard_map/all_to_all | solution.py:203
  159.6 2.3 %pad_maximum_fusion = bf16[2,128,2,640]{3,2,1,0:T(2,128)(2,1)} fusion(bf16[2,128,1,640]{3,2,1,0:T(2,128)(2,1)S(1)} %copy.32, bf16[2,128,1,640]{3,2,1,0:T(2,128)(2,1)S(1)} %copy.31), kind=kLoop, calls=%fused_computation.5 | loop fusion | flops 1310720 | bytes 1310720 | tf_op jit(solution)/shard_map/stack | solution.py:284
  161.9 4.6 %all-to-all-done.4 = f32[8,8,80]{2,1,0:T(8,128)S(1)} async-done(((f32[8,8,80]{2,1,0:T(8,128)}), f32[8,8,80]{2,1,0:T(8,128)S(1)}, u32[]{:S(2)}, u32[]{:S(2)}) %all-to-all-start.4) | async-done | bytes 20512 | tf_op jit(solution)/shard_map/all_to_all | solution.py:203
  (70 shorter events, 24.2 us)
Async XLA Ops:
  0.6 151.4 %copy-start = (bf16[640,80]{0,1:T(8,128)(2,1)S(1)}, bf16[640,80]{0,1:T(8,128)(2,1)}, u32[]{:S(2)}) copy-start(bf16[640,80]{0,1:T(8,128)(2,1)} %param.14) | copy-start | bytes 307204
  0.6 13.2 %copy-start.6 = (bf16[80,2,640]{2,1,0:T(2,128)(2,1)S(1)}, bf16[80,2,640]{2,1,0:T(2,128)(2,1)}, u32[]{:S(2)}) copy-start(bf16[80,2,640]{2,1,0:T(2,128)(2,1)} %param.13) | copy-start | bytes 614404
  0.7 14.0 %copy-start.8 = (s32[2]{0:T(128)S(1)}, s32[2]{0:T(128)}, u32[]{:S(2)}) copy-start(s32[2]{0:T(128)} %param.10) | copy-start | bytes 28
  0.7 14.0 %copy-start.7 = (bf16[5120]{0:T(1024)(128)(2,1)S(1)}, bf16[5120]{0:T(1024)(128)(2,1)}, u32[]{:S(2)}) copy-start(bf16[5120]{0:T(1024)(128)(2,1)} %param.12) | copy-start | bytes 30724
  0.7 14.0 %copy-start.2 = (bf16[1,640]{1,0:T(2,128)(2,1)S(1)}, bf16[1,640]{1,0:T(2,128)(2,1)}, u32[]{:S(2)}) copy-start(bf16[1,640]{1,0:T(2,128)(2,1)} %query_ref.1) | copy-start | bytes 3844
  2.0 28.2 %copy-start.4 = (bf16[2,128,5120]{2,1,0:T(8,128)(2,1)S(1)}, bf16[2,128,5120]{2,1,0:T(8,128)(2,1)}, u32[]{:S(2)}) copy-start(bf16[2,128,5120]{2,1,0:T(8,128)(2,1)} %param.9) | copy-start | bytes 7864324
  2.8 20.3 %all-to-all-start = ((bf16[8,80,384]{2,1,0:T(8,128)(2,1)}), bf16[8,80,384]{2,1,0:T(8,128)(2,1)}, u32[]{:S(2)}, u32[]{:S(2)}) async-start(bf16[8,80,384]{2,1,0:T(8,128)(2,1)} %bitcast.5), calls=%async_computation | async-start | bytes 983040 | tf_op jit(solution)/shard_map/all_to_all | solution.py:203
  24.0 27.4 %all-to-all-start.1 = ((bf16[16,88,256]{2,1,0:T(8,128)(2,1)}), bf16[16,88,256]{2,1,0:T(8,128)(2,1)S(1)}, u32[]{:S(2)}, u32[]{:S(2)}) async-start(bf16[16,88,256]{2,1,0:T(8,128)(2,1)} %bitcast.40), calls=%async_computation.1 | async-start | bytes 1441792 | tf_op jit(solution)/shard_map/all_to_all | solution.py:203
  31.8 47.1 %copy-start.9 = (s32[4]{0:T(128)S(1)}, s32[4]{0:T(128)}, u32[]{:S(2)}) copy-start(s32[4]{0:T(128)} %param.11) | copy-start | bytes 52
  32.6 60.6 %collective-permute-start = (bf16[256,5120]{1,0:T(8,128)(2,1)S(1)}, bf16[256,5120]{1,0:T(8,128)(2,1)}, u32[]{:S(2)}, u32[]{:S(2)}) collective-permute-start(bf16[256,5120]{1,0:T(8,128)(2,1)S(1)} %bitcast.37), channel_id=1, source_target_pairs={{0,8},{8,0},{1,9},{9,1},{2,10},{10,2},{3,11},{11,3},{4,12},{12,4},... | collective-permute-start | bytes 7864328 | tf_op jit(solution)/shard_map/ppermute | solution.py:34
  34.6 23.9 %collective-permute-start.1 = (bf16[640,384]{1,0:T(8,128)(2,1)}, bf16[640,384]{1,0:T(8,128)(2,1)}, u32[]{:S(2)}, u32[]{:S(2)}) collective-permute-start(bf16[640,384]{1,0:T(8,128)(2,1)} %bitcast.6.refs_4_), channel_id=1, source_target_pairs={{0,64},{8,456},{16,80},{24,472},{32,96},{40,488},{48,112},{56,504}... | collective-permute-start | bytes 1474568 | tf_op jit(solution)/shard_map/ppermute | solution.py:199
  39.4 20.3 %collective-permute-start.2 = (bf16[640,384]{1,0:T(8,128)(2,1)}, bf16[640,384]{1,0:T(8,128)(2,1)}, u32[]{:S(2)}, u32[]{:S(2)}) collective-permute-start(bf16[640,384]{1,0:T(8,128)(2,1)} %bitcast.6.refs_4_), channel_id=1, source_target_pairs={{0,448},{8,72},{16,464},{24,88},{32,480},{40,104},{48,496},{56,120... | collective-permute-start | bytes 1474568 | tf_op jit(solution)/shard_map/ppermute | solution.py:199
  51.4 22.5 %collective-permute-start.3 = (bf16[16,88,256]{2,1,0:T(8,128)(2,1)S(1)}, bf16[16,88,256]{2,1,0:T(8,128)(2,1)}, u32[]{:S(2)}, u32[]{:S(2)}) collective-permute-start(bf16[16,88,256]{2,1,0:T(8,128)(2,1)S(1)} %all-to-all-done.1.refs_0_), channel_id=1, source_target_pairs={{0,16},{8,56},{16,32},{24,8},{32,48},{40,24},{48,0},{56,40},{64,80... | collective-permute-start | bytes 2162696 | tf_op jit(solution)/shard_map/ppermute | solution.py:199
  59.8 10.2 %collective-permute-start.7 = (bf16[640,384]{1,0:T(8,128)(2,1)}, bf16[640,384]{1,0:T(8,128)(2,1)}, u32[]{:S(2)}, u32[]{:S(2)}) collective-permute-start(bf16[640,384]{1,0:T(8,128)(2,1)} %collective-permute-done.1.refs_5_), channel_id=1, source_target_pairs={{0,64},{8,456},{16,80},{24,472},{32,96},{40,488},{48,112},{56,504}... | collective-permute-start | bytes 1474568 | tf_op jit(solution)/shard_map/ppermute | solution.py:199
  63.0 22.0 %collective-permute-start.5 = (bf16[16,88,256]{2,1,0:T(8,128)(2,1)S(1)}, bf16[16,88,256]{2,1,0:T(8,128)(2,1)S(1)}, u32[]{:S(2)}, u32[]{:S(2)}) collective-permute-start(bf16[16,88,256]{2,1,0:T(8,128)(2,1)S(1)} %all-to-all-done.1.refs_0_), channel_id=1, source_target_pairs={{0,48},{8,24},{16,0},{24,40},{32,16},{40,56},{48,32},{56,8},{64,11... | collective-permute-start | bytes 2162696 | tf_op jit(solution)/shard_map/ppermute | solution.py:199
  69.9 10.1 %collective-permute-start.8 = (bf16[640,384]{1,0:T(8,128)(2,1)}, bf16[640,384]{1,0:T(8,128)(2,1)S(1)}, u32[]{:S(2)}, u32[]{:S(2)}) collective-permute-start(bf16[640,384]{1,0:T(8,128)(2,1)} %collective-permute-done.7.refs_7_), channel_id=1, source_target_pairs={{0,64},{8,456},{16,80},{24,472},{32,96},{40,488},{48,112},{56,504}... | collective-permute-start | bytes 1474568 | tf_op jit(solution)/shard_map/ppermute | solution.py:199
  74.0 15.9 %collective-permute-start.4 = (bf16[640,384]{1,0:T(8,128)(2,1)}, bf16[640,384]{1,0:T(8,128)(2,1)S(1)}, u32[]{:S(2)}, u32[]{:S(2)}) collective-permute-start(bf16[640,384]{1,0:T(8,128)(2,1)} %collective-permute-done.2.refs_6_), channel_id=1, source_target_pairs={{0,448},{8,72},{16,464},{24,88},{32,480},{40,104},{48,496},{56,120... | collective-permute-start | bytes 1474568 | tf_op jit(solution)/shard_map/ppermute | solution.py:199
  76.0 17.2 %collective-permute-start.6 = (bf16[16,88,256]{2,1,0:T(8,128)(2,1)}, bf16[16,88,256]{2,1,0:T(8,128)(2,1)S(1)}, u32[]{:S(2)}, u32[]{:S(2)}) collective-permute-start(bf16[16,88,256]{2,1,0:T(8,128)(2,1)} %collective-permute-done.3.refs_1_), channel_id=1, source_target_pairs={{0,16},{8,56},{16,32},{24,8},{32,48},{40,24},{48,0},{56,40},{64,80... | collective-permute-start | bytes 2162696 | tf_op jit(solution)/shard_map/ppermute | solution.py:199
  80.0 13.1 %collective-permute-start.10 = (bf16[640,384]{1,0:T(8,128)(2,1)S(1)}, bf16[640,384]{1,0:T(8,128)(2,1)S(1)}, u32[]{:S(2)}, u32[]{:S(2)}) collective-permute-start(bf16[640,384]{1,0:T(8,128)(2,1)S(1)} %collective-permute-done.8.refs_9_), channel_id=1, source_target_pairs={{0,64},{8,456},{16,80},{24,472},{32,96},{40,488},{48,112},{56,504}... | collective-permute-start | bytes 1474568 | tf_op jit(solution)/shard_map/ppermute | solution.py:199
  89.9 16.0 %collective-permute-start.9 = (bf16[640,384]{1,0:T(8,128)(2,1)S(1)}, bf16[640,384]{1,0:T(8,128)(2,1)S(1)}, u32[]{:S(2)}, u32[]{:S(2)}) collective-permute-start(bf16[640,384]{1,0:T(8,128)(2,1)S(1)} %collective-permute-done.4.refs_8_), channel_id=1, source_target_pairs={{0,448},{8,72},{16,464},{24,88},{32,480},{40,104},{48,496},{56,120... | collective-permute-start | bytes 1474568 | tf_op jit(solution)/shard_map/ppermute | solution.py:199
  105.9 28.8 %copy-start.3 = (bf16[1,2,640]{2,1,0:T(2,128)(2,1)S(1)}, bf16[1,2,640]{2,1,0:T(2,128)(2,1)}, u32[]{:S(2)}) copy-start(bf16[1,2,640]{2,1,0:T(2,128)(2,1)} %param.16) | copy-start | bytes 7684
  113.3 3.9 %collective-permute-start.11 = (bf16[256,640]{1,0:T(8,128)(2,1)S(1)}, bf16[256,640]{1,0:T(8,128)(2,1)S(1)}, u32[]{:S(2)}, u32[]{:S(2)}) collective-permute-start(bf16[256,640]{1,0:T(8,128)(2,1)S(1)} %get-tuple-element.22), channel_id=1, source_target_pairs={{0,8},{8,0},{1,9},{9,1},{2,10},{10,2},{3,11},{11,3},{4,12},{12,4},... | collective-permute-start | bytes 983048 | tf_op jit(solution)/shard_map/ppermute | solution.py:34
  135.9 16.0 %all-to-all-start.3 = ((bf16[64,8,128]{2,1,0:T(8,128)(2,1)}), bf16[64,8,128]{2,1,0:T(8,128)(2,1)S(1)}, u32[]{:S(2)}, u32[]{:S(2)}) async-start(bf16[64,8,128]{2,1,0:T(8,128)(2,1)} %shard_map.106), calls=%async_computation.3 | async-start | bytes 262144 | tf_op jit(solution)/shard_map/all_to_all | solution.py:203
  152.8 13.8 %all-to-all-start.4 = ((f32[8,8,80]{2,1,0:T(8,128)}), f32[8,8,80]{2,1,0:T(8,128)S(1)}, u32[]{:S(2)}, u32[]{:S(2)}) async-start(f32[8,8,80]{2,1,0:T(8,128)} %fusion.5), calls=%async_computation.4 | async-start | bytes 65536 | tf_op jit(solution)/shard_map/all_to_all | solution.py:203
  (2 other events, 2.5 us)

commit v9 on v7

--- a/solution.py
+++ b/solution.py
@@ -236,7 +236,8 @@
     behind1, ahead1 = send(block_b, 1, 0), send(block_b, -1, 0)
     behind2, ahead2 = send(behind1, 1, 0), send(ahead1, -1, 0)
     behind3, ahead3 = send(behind2, 1, 0), send(ahead2, -1, 0)
-    a_blocks = (pieces_a, a_behind, a_ahead, send(a_behind, 0, 1))
+    behind3, a_last = lax.optimization_barrier((behind3, send(a_behind, 0, 1)))
+    a_blocks = (pieces_a, a_behind, a_ahead, a_last)
     b_blocks = (block_b, behind1, ahead1, behind2, ahead2, behind3, ahead3, send(behind3, 1, 0))
 
     normed = normalize(saved, norm_gain).reshape(slot_dev * block_rows, model_width)

time: 170 us -> 170 us (level)
  starting transfers between devices: 69.4 us -> 66.8 us
    all_to_all x4, waiting for transfers between devices: 22.1 us -> 34.1 us  [exchange(): return lax.all_to_all(value, axis, 0, 0, tiled=True)]
    ppermute x10, waiting for transfers between devices: 31.1 us -> 20.2 us  [send(): return lax.ppermute(value, GROUP, pairs)]
  transfers between devices with their start and end apart: 16 -> 16, of which waited for: 8 -> 9; matrix products, arithmetic and copies ran while one was open for 5% -> 5% of each run, Pallas kernels for 0% -> 0%
where the time goes in v9:
time: 170 us; the launch traced here: 169 us
  starting transfers between devices  66.8 us (39%)
  waiting for transfers between devices  55.5 us (33%)
  blocking collectives  20.5 us (12%)
  Pallas kernels  10.5 us (6%)
  other arithmetic  7.51 us (4%)
  local copies, waits for them, and re-layouts  6.23 us (4%)
    all_to_all x4, waiting for transfers between devices, exchange(): return lax.all_to_all(value, axis, 0, 0, tiled=True)  34.1 us
    ppermute x10, starting transfers between devices, send(): return lax.ppermute(value, GROUP, pairs)  32.4 us
    all_to_all x4, starting transfers between devices, exchange(): return lax.all_to_all(value, axis, 0, 0, tiled=True)  28.5 us
    all_to_all x1, blocking collectives, exchange(): return lax.all_to_all(value, axis, 0, 0, tiled=True)  20.5 us
    ppermute x10, waiting for transfers between devices, send(): return lax.ppermute(value, GROUP, pairs)  20.2 us
    pallas_call x1, Pallas kernels, project(): pl.pallas_call(project_kernel, in_specs=[pl.BlockSpec(memory_space=pltpu....  7.4 us
    ppermute x2, starting transfers between devices, swap_cores(): return lax.ppermute(value, 'core', [(0, 1), (1, 0)])  5.83 us
  transfers between devices with their start and end apart: 16, of which 9 were waited for; matrix products, arithmetic and copies ran while one was open for 5% of the time, Pallas kernels for 0%

profile of v9, /device:TPU:1, one launch (start us, length us, event | category | flops | bytes accessed | tf_op | source)
XLA Modules:
  0.0 169.4 jit_solution(7618992695401407939)
XLA Ops:
  2.8 11.0 %all-to-all-start = ((bf16[8,80,384]{2,1,0:T(8,128)(2,1)}), bf16[8,80,384]{2,1,0:T(8,128)(2,1)}, u32[]{:S(2)}, u32[]{:S(2)}) async-start(bf16[8,80,384]{2,1,0:T(8,128)(2,1)} %bitcast.5), calls=%async_computation | async-start | bytes 983040 | tf_op jit(solution)/shard_map/all_to_all | solution.py:203
  14.9 8.2 %all-to-all-done = bf16[8,80,384]{2,1,0:T(8,128)(2,1)} async-done(((bf16[8,80,384]{2,1,0:T(8,128)(2,1)}), bf16[8,80,384]{2,1,0:T(8,128)(2,1)}, u32[]{:S(2)}, u32[]{:S(2)}) %all-to-all-start) | async-done | bytes 491552 | tf_op jit(solution)/shard_map/all_to_all | solution.py:203
  24.0 6.1 %all-to-all-start.1 = ((bf16[16,88,256]{2,1,0:T(8,128)(2,1)}), bf16[16,88,256]{2,1,0:T(8,128)(2,1)S(1)}, u32[]{:S(2)}, u32[]{:S(2)}) async-start(bf16[16,88,256]{2,1,0:T(8,128)(2,1)} %bitcast.40), calls=%async_computation.1 | async-start | bytes 1441792 | tf_op jit(solution)/shard_map/all_to_all | solution.py:203
  32.6 2.0 %collective-permute-start = (bf16[256,5120]{1,0:T(8,128)(2,1)S(1)}, bf16[256,5120]{1,0:T(8,128)(2,1)}, u32[]{:S(2)}, u32[]{:S(2)}) collective-permute-start(bf16[256,5120]{1,0:T(8,128)(2,1)S(1)} %bitcast.37), channel_id=1, source_target_pairs={{0,8},{8,0},{1,9},{9,1},{2,10},{10,2},{3,11},{11,3},{4,12},{12,4},... | collective-permute-start | bytes 7864328 | tf_op jit(solution)/shard_map/ppermute | solution.py:34
  34.6 4.8 %collective-permute-start.3 = (bf16[640,384]{1,0:T(8,128)(2,1)}, bf16[640,384]{1,0:T(8,128)(2,1)}, u32[]{:S(2)}, u32[]{:S(2)}) collective-permute-start(bf16[640,384]{1,0:T(8,128)(2,1)} %bitcast.6.refs_4_), channel_id=1, source_target_pairs={{0,64},{8,456},{16,80},{24,472},{32,96},{40,488},{48,112},{56,504}... | collective-permute-start | bytes 1474568 | tf_op jit(solution)/shard_map/ppermute | solution.py:199
  39.4 12.0 %all-to-all-done.1.refs_0_ = bf16[16,88,256]{2,1,0:T(8,128)(2,1)S(1)} async-done(((bf16[16,88,256]{2,1,0:T(8,128)(2,1)}), bf16[16,88,256]{2,1,0:T(8,128)(2,1)S(1)}, u32[]{:S(2)}, u32[]{:S(2)}) %all-to-all-start.1) | async-done | bytes 720928 | tf_op jit(solution)/shard_map/all_to_all | solution.py:203
  51.4 2.8 %collective-permute-start.1 = (bf16[16,88,256]{2,1,0:T(8,128)(2,1)S(1)}, bf16[16,88,256]{2,1,0:T(8,128)(2,1)}, u32[]{:S(2)}, u32[]{:S(2)}) collective-permute-start(bf16[16,88,256]{2,1,0:T(8,128)(2,1)S(1)} %all-to-all-done.1.refs_0_), channel_id=1, source_target_pairs={{0,16},{8,56},{16,32},{24,8},{32,48},{40,24},{48,0},{56,40},{64,80... | collective-permute-start | bytes 2162696 | tf_op jit(solution)/shard_map/ppermute | solution.py:199
  54.2 1.9 %collective-permute-start.7 = (bf16[640,384]{1,0:T(8,128)(2,1)}, bf16[640,384]{1,0:T(8,128)(2,1)}, u32[]{:S(2)}, u32[]{:S(2)}) collective-permute-start(bf16[640,384]{1,0:T(8,128)(2,1)} %bitcast.6.refs_4_), channel_id=1, source_target_pairs={{0,448},{8,72},{16,464},{24,88},{32,480},{40,104},{48,496},{56,120... | collective-permute-start | bytes 1474568 | tf_op jit(solution)/shard_map/ppermute | solution.py:199
  56.2 4.6 %collective-permute-start.4 = (bf16[640,384]{1,0:T(8,128)(2,1)}, bf16[640,384]{1,0:T(8,128)(2,1)}, u32[]{:S(2)}, u32[]{:S(2)}) collective-permute-start(bf16[640,384]{1,0:T(8,128)(2,1)} %collective-permute-done.3.refs_5_), channel_id=1, source_target_pairs={{0,64},{8,456},{16,80},{24,472},{32,96},{40,488},{48,112},{56,504}... | collective-permute-start | bytes 1474568 | tf_op jit(solution)/shard_map/ppermute | solution.py:199
  60.9 8.1 %collective-permute-done.7.refs_6_ = bf16[640,384]{1,0:T(8,128)(2,1)} collective-permute-done((bf16[640,384]{1,0:T(8,128)(2,1)}, bf16[640,384]{1,0:T(8,128)(2,1)}, u32[]{:S(2)}, u32[]{:S(2)}) %collective-permute-start.7) | collective-permute-done | bytes 491552 | tf_op jit(solution)/shard_map/ppermute | solution.py:199
  72.9 3.4 %collective-permute-start.2 = (bf16[16,88,256]{2,1,0:T(8,128)(2,1)S(1)}, bf16[16,88,256]{2,1,0:T(8,128)(2,1)S(1)}, u32[]{:S(2)}, u32[]{:S(2)}) collective-permute-start(bf16[16,88,256]{2,1,0:T(8,128)(2,1)S(1)} %all-to-all-done.1.refs_0_), channel_id=1, source_target_pairs={{0,48},{8,24},{16,0},{24,40},{32,16},{40,56},{48,32},{56,8},{64,11... | collective-permute-start | bytes 2162696 | tf_op jit(solution)/shard_map/ppermute | solution.py:199
  76.4 4.6 %collective-permute-start.5 = (bf16[640,384]{1,0:T(8,128)(2,1)}, bf16[640,384]{1,0:T(8,128)(2,1)S(1)}, u32[]{:S(2)}, u32[]{:S(2)}) collective-permute-start(bf16[640,384]{1,0:T(8,128)(2,1)} %collective-permute-done.4.refs_7_), channel_id=1, source_target_pairs={{0,64},{8,456},{16,80},{24,472},{32,96},{40,488},{48,112},{56,504}... | collective-permute-start | bytes 1474568 | tf_op jit(solution)/shard_map/ppermute | solution.py:199
  83.2 5.4 %collective-permute-done.5.refs_9_ = bf16[640,384]{1,0:T(8,128)(2,1)S(1)} collective-permute-done((bf16[640,384]{1,0:T(8,128)(2,1)}, bf16[640,384]{1,0:T(8,128)(2,1)S(1)}, u32[]{:S(2)}, u32[]{:S(2)}) %collective-permute-start.5) | collective-permute-done | bytes 491552 | tf_op jit(solution)/shard_map/ppermute | solution.py:199
  88.6 2.4 %collective-permute-done.6.refs_3_ = bf16[16,88,256]{2,1,0:T(8,128)(2,1)S(1)} collective-permute-done((bf16[16,88,256]{2,1,0:T(8,128)(2,1)}, bf16[16,88,256]{2,1,0:T(8,128)(2,1)S(1)}, u32[]{:S(2)}, u32[]{:S(2)}) %collective-permute-start.6) | collective-permute-done | bytes 720928 | tf_op jit(solution)/shard_map/ppermute | solution.py:199
  90.9 4.7 %collective-permute-start.10 = (bf16[640,384]{1,0:T(8,128)(2,1)S(1)}, bf16[640,384]{1,0:T(8,128)(2,1)S(1)}, u32[]{:S(2)}, u32[]{:S(2)}) collective-permute-start(bf16[640,384]{1,0:T(8,128)(2,1)S(1)} %collective-permute-done.5.refs_9_), channel_id=1, source_target_pairs={{0,64},{8,456},{16,80},{24,472},{32,96},{40,488},{48,112},{56,504}... | collective-permute-start | bytes 1474568 | tf_op jit(solution)/shard_map/ppermute | solution.py:199
  97.0 4.4 %collective-permute-done.10.refs_11_ = bf16[640,384]{1,0:T(8,128)(2,1)S(1)} collective-permute-done((bf16[640,384]{1,0:T(8,128)(2,1)S(1)}, bf16[640,384]{1,0:T(8,128)(2,1)S(1)}, u32[]{:S(2)}, u32[]{:S(2)}) %collective-permute-start.10) | collective-permute-done | bytes 491552 | tf_op jit(solution)/shard_map/ppermute | solution.py:199
  101.4 7.4 %shard_map.104 = (bf16[256,640]{1,0:T(8,128)(2,1)S(1)}, bf16[256,640]{1,0:T(8,128)(2,1)S(1)}, f32[64,8,256]{2,1,0:T(8,128)S(1)}) custom-call(s32[3]{0:T(128)S(1)} %pad_add_fusion.place_ref, bf16[256,5120]{1,0:T(8,128)(2,1)S(1)} %bitcast.38, bf16[256,5120]{1,0:T(8,128)(2,1)} %collective-permute-done.other_ref, f32[512,128]{1,0:T(8,128)S(1)} %get-tuple-element.33.cos_ref, ...), custom_call_target="tpu_custom_call" | custom-call | flops 3355443200 | bytes 11796480 | tf_op jit(solution)/shard_map/pallas_call | solution.py:87
  108.8 3.8 %collective-permute-start.11 = (bf16[256,640]{1,0:T(8,128)(2,1)S(1)}, bf16[256,640]{1,0:T(8,128)(2,1)S(1)}, u32[]{:S(2)}, u32[]{:S(2)}) collective-permute-start(bf16[256,640]{1,0:T(8,128)(2,1)S(1)} %get-tuple-element.14), channel_id=1, source_target_pairs={{0,8},{8,0},{1,9},{9,1},{2,10},{10,2},{3,11},{11,3},{4,12},{12,4},... | collective-permute-start | bytes 983048 | tf_op jit(solution)/shard_map/ppermute | solution.py:34
  116.5 20.5 %all_to_all.25.parts_ref = bf16[64,8,128]{2,1,0:T(8,128)(2,1)S(1)} all-to-all(bf16[64,8,128]{2,1,0:T(8,128)(2,1)S(1)} %shard_map.105), channel_id=1, replica_groups=mesh['z'=8,'x'=4,'core'=2,'tp'=8] {'z','x','core'}, dimensions={0} | all-to-all | bytes 262144 | tf_op jit(solution)/shard_map/all_to_all | solution.py:203
  138.2 4.6 %all-to-all-start.3 = ((bf16[64,8,128]{2,1,0:T(8,128)(2,1)}), bf16[64,8,128]{2,1,0:T(8,128)(2,1)S(1)}, u32[]{:S(2)}, u32[]{:S(2)}) async-start(bf16[64,8,128]{2,1,0:T(8,128)(2,1)} %shard_map.106), calls=%async_computation.3 | async-start | bytes 262144 | tf_op jit(solution)/shard_map/all_to_all | solution.py:203
  144.9 9.3 %all-to-all-done.3 = bf16[64,8,128]{2,1,0:T(8,128)(2,1)S(1)} async-done(((bf16[64,8,128]{2,1,0:T(8,128)(2,1)}), bf16[64,8,128]{2,1,0:T(8,128)(2,1)S(1)}, u32[]{:S(2)}, u32[]{:S(2)}) %all-to-all-start.3) | async-done | bytes 131104 | tf_op jit(solution)/shard_map/all_to_all | solution.py:203
  155.0 6.8 %all-to-all-start.4 = ((f32[8,8,80]{2,1,0:T(8,128)}), f32[8,8,80]{2,1,0:T(8,128)S(1)}, u32[]{:S(2)}, u32[]{:S(2)}) async-start(f32[8,8,80]{2,1,0:T(8,128)} %fusion.5), calls=%async_computation.4 | async-start | bytes 65536 | tf_op jit(solution)/shard_map/all_to_all | solution.py:203
  161.8 2.3 %pad_maximum_fusion = bf16[2,128,2,640]{3,2,1,0:T(2,128)(2,1)} fusion(bf16[2,128,1,640]{3,2,1,0:T(2,128)(2,1)S(1)} %copy.32, bf16[2,128,1,640]{3,2,1,0:T(2,128)(2,1)S(1)} %copy.31), kind=kLoop, calls=%fused_computation.5 | loop fusion | flops 1310720 | bytes 1310720 | tf_op jit(solution)/shard_map/stack | solution.py:282
  164.2 4.6 %all-to-all-done.4 = f32[8,8,80]{2,1,0:T(8,128)S(1)} async-done(((f32[8,8,80]{2,1,0:T(8,128)}), f32[8,8,80]{2,1,0:T(8,128)S(1)}, u32[]{:S(2)}, u32[]{:S(2)}) %all-to-all-start.4) | async-done | bytes 20512 | tf_op jit(solution)/shard_map/all_to_all | solution.py:203
  (70 shorter events, 22.2 us)
Async XLA Ops:
  0.6 153.6 %copy-start = (bf16[640,80]{0,1:T(8,128)(2,1)S(1)}, bf16[640,80]{0,1:T(8,128)(2,1)}, u32[]{:S(2)}) copy-start(bf16[640,80]{0,1:T(8,128)(2,1)} %param.14) | copy-start | bytes 307204
  0.6 13.2 %copy-start.6 = (bf16[80,2,640]{2,1,0:T(2,128)(2,1)S(1)}, bf16[80,2,640]{2,1,0:T(2,128)(2,1)}, u32[]{:S(2)}) copy-start(bf16[80,2,640]{2,1,0:T(2,128)(2,1)} %param.13) | copy-start | bytes 614404
  0.7 14.0 %copy-start.8 = (s32[2]{0:T(128)S(1)}, s32[2]{0:T(128)}, u32[]{:S(2)}) copy-start(s32[2]{0:T(128)} %param.10) | copy-start | bytes 28
  0.7 14.0 %copy-start.7 = (bf16[5120]{0:T(1024)(128)(2,1)S(1)}, bf16[5120]{0:T(1024)(128)(2,1)}, u32[]{:S(2)}) copy-start(bf16[5120]{0:T(1024)(128)(2,1)} %param.12) | copy-start | bytes 30724
  0.7 14.0 %copy-start.2 = (bf16[1,640]{1,0:T(2,128)(2,1)S(1)}, bf16[1,640]{1,0:T(2,128)(2,1)}, u32[]{:S(2)}) copy-start(bf16[1,640]{1,0:T(2,128)(2,1)} %query_ref.1) | copy-start | bytes 3844
  2.0 28.2 %copy-start.4 = (bf16[2,128,5120]{2,1,0:T(8,128)(2,1)S(1)}, bf16[2,128,5120]{2,1,0:T(8,128)(2,1)}, u32[]{:S(2)}) copy-start(bf16[2,128,5120]{2,1,0:T(8,128)(2,1)} %param.9) | copy-start | bytes 7864324
  2.8 20.3 %all-to-all-start = ((bf16[8,80,384]{2,1,0:T(8,128)(2,1)}), bf16[8,80,384]{2,1,0:T(8,128)(2,1)}, u32[]{:S(2)}, u32[]{:S(2)}) async-start(bf16[8,80,384]{2,1,0:T(8,128)(2,1)} %bitcast.5), calls=%async_computation | async-start | bytes 983040 | tf_op jit(solution)/shard_map/all_to_all | solution.py:203
  24.0 27.4 %all-to-all-start.1 = ((bf16[16,88,256]{2,1,0:T(8,128)(2,1)}), bf16[16,88,256]{2,1,0:T(8,128)(2,1)S(1)}, u32[]{:S(2)}, u32[]{:S(2)}) async-start(bf16[16,88,256]{2,1,0:T(8,128)(2,1)} %bitcast.40), calls=%async_computation.1 | async-start | bytes 1441792 | tf_op jit(solution)/shard_map/all_to_all | solution.py:203
  31.8 49.2 %copy-start.9 = (s32[4]{0:T(128)S(1)}, s32[4]{0:T(128)}, u32[]{:S(2)}) copy-start(s32[4]{0:T(128)} %param.11) | copy-start | bytes 52
  32.6 64.4 %collective-permute-start = (bf16[256,5120]{1,0:T(8,128)(2,1)S(1)}, bf16[256,5120]{1,0:T(8,128)(2,1)}, u32[]{:S(2)}, u32[]{:S(2)}) collective-permute-start(bf16[256,5120]{1,0:T(8,128)(2,1)S(1)} %bitcast.37), channel_id=1, source_target_pairs={{0,8},{8,0},{1,9},{9,1},{2,10},{10,2},{3,11},{11,3},{4,12},{12,4},... | collective-permute-start | bytes 7864328 | tf_op jit(solution)/shard_map/ppermute | solution.py:34
  34.6 21.5 %collective-permute-start.3 = (bf16[640,384]{1,0:T(8,128)(2,1)}, bf16[640,384]{1,0:T(8,128)(2,1)}, u32[]{:S(2)}, u32[]{:S(2)}) collective-permute-start(bf16[640,384]{1,0:T(8,128)(2,1)} %bitcast.6.refs_4_), channel_id=1, source_target_pairs={{0,64},{8,456},{16,80},{24,472},{32,96},{40,488},{48,112},{56,504}... | collective-permute-start | bytes 1474568 | tf_op jit(solution)/shard_map/ppermute | solution.py:199
  51.4 19.4 %collective-permute-start.1 = (bf16[16,88,256]{2,1,0:T(8,128)(2,1)S(1)}, bf16[16,88,256]{2,1,0:T(8,128)(2,1)}, u32[]{:S(2)}, u32[]{:S(2)}) collective-permute-start(bf16[16,88,256]{2,1,0:T(8,128)(2,1)S(1)} %all-to-all-done.1.refs_0_), channel_id=1, source_target_pairs={{0,16},{8,56},{16,32},{24,8},{32,48},{40,24},{48,0},{56,40},{64,80... | collective-permute-start | bytes 2162696 | tf_op jit(solution)/shard_map/ppermute | solution.py:199
  54.2 14.7 %collective-permute-start.7 = (bf16[640,384]{1,0:T(8,128)(2,1)}, bf16[640,384]{1,0:T(8,128)(2,1)}, u32[]{:S(2)}, u32[]{:S(2)}) collective-permute-start(bf16[640,384]{1,0:T(8,128)(2,1)} %bitcast.6.refs_4_), channel_id=1, source_target_pairs={{0,448},{8,72},{16,464},{24,88},{32,480},{40,104},{48,496},{56,120... | collective-permute-start | bytes 1474568 | tf_op jit(solution)/shard_map/ppermute | solution.py:199
  56.2 20.2 %collective-permute-start.4 = (bf16[640,384]{1,0:T(8,128)(2,1)}, bf16[640,384]{1,0:T(8,128)(2,1)}, u32[]{:S(2)}, u32[]{:S(2)}) collective-permute-start(bf16[640,384]{1,0:T(8,128)(2,1)} %collective-permute-done.3.refs_5_), channel_id=1, source_target_pairs={{0,64},{8,456},{16,80},{24,472},{32,96},{40,488},{48,112},{56,504}... | collective-permute-start | bytes 1474568 | tf_op jit(solution)/shard_map/ppermute | solution.py:199
  68.9 12.3 %collective-permute-start.8 = (bf16[640,384]{1,0:T(8,128)(2,1)}, bf16[640,384]{1,0:T(8,128)(2,1)S(1)}, u32[]{:S(2)}, u32[]{:S(2)}) collective-permute-start(bf16[640,384]{1,0:T(8,128)(2,1)} %collective-permute-done.7.refs_6_), channel_id=1, source_target_pairs={{0,448},{8,72},{16,464},{24,88},{32,480},{40,104},{48,496},{56,120... | collective-permute-start | bytes 1474568 | tf_op jit(solution)/shard_map/ppermute | solution.py:199
  70.9 20.1 %collective-permute-start.6 = (bf16[16,88,256]{2,1,0:T(8,128)(2,1)}, bf16[16,88,256]{2,1,0:T(8,128)(2,1)S(1)}, u32[]{:S(2)}, u32[]{:S(2)}) collective-permute-start(bf16[16,88,256]{2,1,0:T(8,128)(2,1)} %collective-permute-done.1.refs_1_), channel_id=1, source_target_pairs={{0,16},{8,56},{16,32},{24,8},{32,48},{40,24},{48,0},{56,40},{64,80... | collective-permute-start | bytes 2162696 | tf_op jit(solution)/shard_map/ppermute | solution.py:199
  72.9 24.1 %collective-permute-start.2 = (bf16[16,88,256]{2,1,0:T(8,128)(2,1)S(1)}, bf16[16,88,256]{2,1,0:T(8,128)(2,1)S(1)}, u32[]{:S(2)}, u32[]{:S(2)}) collective-permute-start(bf16[16,88,256]{2,1,0:T(8,128)(2,1)S(1)} %all-to-all-done.1.refs_0_), channel_id=1, source_target_pairs={{0,48},{8,24},{16,0},{24,40},{32,16},{40,56},{48,32},{56,8},{64,11... | collective-permute-start | bytes 2162696 | tf_op jit(solution)/shard_map/ppermute | solution.py:199
  76.4 12.2 %collective-permute-start.5 = (bf16[640,384]{1,0:T(8,128)(2,1)}, bf16[640,384]{1,0:T(8,128)(2,1)S(1)}, u32[]{:S(2)}, u32[]{:S(2)}) collective-permute-start(bf16[640,384]{1,0:T(8,128)(2,1)} %collective-permute-done.4.refs_7_), channel_id=1, source_target_pairs={{0,64},{8,456},{16,80},{24,472},{32,96},{40,488},{48,112},{56,504}... | collective-permute-start | bytes 1474568 | tf_op jit(solution)/shard_map/ppermute | solution.py:199
  81.2 15.7 %collective-permute-start.9 = (bf16[640,384]{1,0:T(8,128)(2,1)S(1)}, bf16[640,384]{1,0:T(8,128)(2,1)S(1)}, u32[]{:S(2)}, u32[]{:S(2)}) collective-permute-start(bf16[640,384]{1,0:T(8,128)(2,1)S(1)} %collective-permute-done.8.refs_8_), channel_id=1, source_target_pairs={{0,448},{8,72},{16,464},{24,88},{32,480},{40,104},{48,496},{56,120... | collective-permute-start | bytes 1474568 | tf_op jit(solution)/shard_map/ppermute | solution.py:199
  90.9 10.4 %collective-permute-start.10 = (bf16[640,384]{1,0:T(8,128)(2,1)S(1)}, bf16[640,384]{1,0:T(8,128)(2,1)S(1)}, u32[]{:S(2)}, u32[]{:S(2)}) collective-permute-start(bf16[640,384]{1,0:T(8,128)(2,1)S(1)} %collective-permute-done.5.refs_9_), channel_id=1, source_target_pairs={{0,64},{8,456},{16,80},{24,472},{32,96},{40,488},{48,112},{56,504}... | collective-permute-start | bytes 1474568 | tf_op jit(solution)/shard_map/ppermute | solution.py:199
  101.4 35.6 %copy-start.3 = (bf16[1,2,640]{2,1,0:T(2,128)(2,1)S(1)}, bf16[1,2,640]{2,1,0:T(2,128)(2,1)}, u32[]{:S(2)}) copy-start(bf16[1,2,640]{2,1,0:T(2,128)(2,1)} %param.16) | copy-start | bytes 7684
  108.8 5.1 %collective-permute-start.11 = (bf16[256,640]{1,0:T(8,128)(2,1)S(1)}, bf16[256,640]{1,0:T(8,128)(2,1)S(1)}, u32[]{:S(2)}, u32[]{:S(2)}) collective-permute-start(bf16[256,640]{1,0:T(8,128)(2,1)S(1)} %get-tuple-element.14), channel_id=1, source_target_pairs={{0,8},{8,0},{1,9},{9,1},{2,10},{10,2},{3,11},{11,3},{4,12},{12,4},... | collective-permute-start | bytes 983048 | tf_op jit(solution)/shard_map/ppermute | solution.py:34
  138.2 16.0 %all-to-all-start.3 = ((bf16[64,8,128]{2,1,0:T(8,128)(2,1)}), bf16[64,8,128]{2,1,0:T(8,128)(2,1)S(1)}, u32[]{:S(2)}, u32[]{:S(2)}) async-start(bf16[64,8,128]{2,1,0:T(8,128)(2,1)} %shard_map.106), calls=%async_computation.3 | async-start | bytes 262144 | tf_op jit(solution)/shard_map/all_to_all | solution.py:203
  155.0 13.8 %all-to-all-start.4 = ((f32[8,8,80]{2,1,0:T(8,128)}), f32[8,8,80]{2,1,0:T(8,128)S(1)}, u32[]{:S(2)}, u32[]{:S(2)}) async-start(f32[8,8,80]{2,1,0:T(8,128)} %fusion.5), calls=%async_computation.4 | async-start | bytes 65536 | tf_op jit(solution)/shard_map/all_to_all | solution.py:203
  (2 other events, 2.5 us)

commit v10 on v6

--- a/solution.py
+++ b/solution.py
@@ -60,14 +60,14 @@
         weight[to, pl.ds(split, width - split)] = ref[...]
 
     chunk = 1024 if depth % 1024 == 0 else depth
-    for part, (rows_ref, out) in enumerate(((own_ref, own_out), (other_ref, other_out))):
+    both = jnp.zeros((2 * rows, width), jnp.float32)
+    for k in range(depth // chunk):
+        lanes = pl.ds(k * chunk, chunk)
+        stacked = jnp.concatenate([own_ref[:, lanes], other_ref[:, lanes]])
+        both += jnp.dot(stacked, weight[lanes, :], preferred_element_type=jnp.float32)
+    for part, out in enumerate((own_out, other_out)):
         span = pl.ds(part * rows, rows)
-        total = jnp.zeros((rows, width), jnp.float32)
-        for k in range(depth // chunk):
-            lanes = pl.ds(k * chunk, chunk)
-            total += jnp.dot(
-                rows_ref[:, lanes], weight[lanes, :], preferred_element_type=jnp.float32
-            )
+        total = both[part * rows : (part + 1) * rows]
         cosine, sine = cos_ref[span, :], sin_ref[span, :]
         for head in range(width // HEAD_DIM):
             value = total[:, head * HEAD_DIM : (head + 1) * HEAD_DIM]

time: 167 us -> 167 us (level)
  no operation moved by 1% of the time
where the time goes in v10:
time: 167 us; the launch traced here: 166 us
  starting transfers between devices  66.7 us (40%)
  waiting for transfers between devices  57.2 us (34%)
  blocking collectives  14.9 us (9%)
  Pallas kernels  10.5 us (6%)
  other arithmetic  7.51 us (4%)
  local copies, waits for them, and re-layouts  6.23 us (4%)
  between operations  1.71 us (1%)
    all_to_all x4, waiting for transfers between devices, exchange(): return lax.all_to_all(value, axis, 0, 0, tiled=True)  34.1 us
    ppermute x10, starting transfers between devices, send(): return lax.ppermute(value, GROUP, pairs)  33.5 us
    all_to_all x4, starting transfers between devices, exchange(): return lax.all_to_all(value, axis, 0, 0, tiled=True)  28.5 us
    ppermute x10, waiting for transfers between devices, send(): return lax.ppermute(value, GROUP, pairs)  22 us
    all_to_all x1, blocking collectives, exchange(): return lax.all_to_all(value, axis, 0, 0, tiled=True)  14.9 us
    pallas_call x1, Pallas kernels, project(): pl.pallas_call(project_kernel, in_specs=[pl.BlockSpec(memory_space=pltpu....  7.43 us
    ppermute x2, starting transfers between devices, swap_cores(): return lax.ppermute(value, 'core', [(0, 1), (1, 0)])  4.72 us
  transfers between devices with their start and end apart: 16, of which 8 were waited for; matrix products, arithmetic and copies ran while one was open for 5% of the time, Pallas kernels for 0%

profile of v10, /device:TPU:1, one launch (start us, length us, event | category | flops | bytes accessed | tf_op | source)
XLA Modules:
  0.0 165.7 jit_solution(6934461825009314695)
XLA Ops:
  2.8 11.0 %all-to-all-start = ((bf16[8,80,384]{2,1,0:T(8,128)(2,1)}), bf16[8,80,384]{2,1,0:T(8,128)(2,1)}, u32[]{:S(2)}, u32[]{:S(2)}) async-start(bf16[8,80,384]{2,1,0:T(8,128)(2,1)} %bitcast.5), calls=%async_computation | async-start | bytes 983040 | tf_op jit(solution)/shard_map/all_to_all | solution.py:203
  14.9 8.2 %all-to-all-done = bf16[8,80,384]{2,1,0:T(8,128)(2,1)} async-done(((bf16[8,80,384]{2,1,0:T(8,128)(2,1)}), bf16[8,80,384]{2,1,0:T(8,128)(2,1)}, u32[]{:S(2)}, u32[]{:S(2)}) %all-to-all-start) | async-done | bytes 491552 | tf_op jit(solution)/shard_map/all_to_all | solution.py:203
  24.0 6.1 %all-to-all-start.1 = ((bf16[16,88,256]{2,1,0:T(8,128)(2,1)}), bf16[16,88,256]{2,1,0:T(8,128)(2,1)S(1)}, u32[]{:S(2)}, u32[]{:S(2)}) async-start(bf16[16,88,256]{2,1,0:T(8,128)(2,1)} %bitcast.40), calls=%async_computation.1 | async-start | bytes 1441792 | tf_op jit(solution)/shard_map/all_to_all | solution.py:203
  32.6 2.0 %collective-permute-start = (bf16[256,5120]{1,0:T(8,128)(2,1)S(1)}, bf16[256,5120]{1,0:T(8,128)(2,1)}, u32[]{:S(2)}, u32[]{:S(2)}) collective-permute-start(bf16[256,5120]{1,0:T(8,128)(2,1)S(1)} %bitcast.37), channel_id=1, source_target_pairs={{0,8},{8,0},{1,9},{9,1},{2,10},{10,2},{3,11},{11,3},{4,12},{12,4},... | collective-permute-start | bytes 7864328 | tf_op jit(solution)/shard_map/ppermute | solution.py:34
  34.6 4.8 %collective-permute-start.6 = (bf16[640,384]{1,0:T(8,128)(2,1)}, bf16[640,384]{1,0:T(8,128)(2,1)}, u32[]{:S(2)}, u32[]{:S(2)}) collective-permute-start(bf16[640,384]{1,0:T(8,128)(2,1)} %bitcast.6.refs_4_), channel_id=1, source_target_pairs={{0,64},{8,456},{16,80},{24,472},{32,96},{40,488},{48,112},{56,504}... | collective-permute-start | bytes 1474568 | tf_op jit(solution)/shard_map/ppermute | solution.py:199
  39.4 12.0 %all-to-all-done.1.refs_0_ = bf16[16,88,256]{2,1,0:T(8,128)(2,1)S(1)} async-done(((bf16[16,88,256]{2,1,0:T(8,128)(2,1)}), bf16[16,88,256]{2,1,0:T(8,128)(2,1)S(1)}, u32[]{:S(2)}, u32[]{:S(2)}) %all-to-all-start.1) | async-done | bytes 720928 | tf_op jit(solution)/shard_map/all_to_all | solution.py:203
  51.4 2.8 %collective-permute-start.2 = (bf16[16,88,256]{2,1,0:T(8,128)(2,1)S(1)}, bf16[16,88,256]{2,1,0:T(8,128)(2,1)}, u32[]{:S(2)}, u32[]{:S(2)}) collective-permute-start(bf16[16,88,256]{2,1,0:T(8,128)(2,1)S(1)} %all-to-all-done.1.refs_0_), channel_id=1, source_target_pairs={{0,16},{8,56},{16,32},{24,8},{32,48},{40,24},{48,0},{56,40},{64,80... | collective-permute-start | bytes 2162696 | tf_op jit(solution)/shard_map/ppermute | solution.py:199
  54.2 1.9 %collective-permute-start.1 = (bf16[640,384]{1,0:T(8,128)(2,1)}, bf16[640,384]{1,0:T(8,128)(2,1)}, u32[]{:S(2)}, u32[]{:S(2)}) collective-permute-start(bf16[640,384]{1,0:T(8,128)(2,1)} %bitcast.6.refs_4_), channel_id=1, source_target_pairs={{0,448},{8,72},{16,464},{24,88},{32,480},{40,104},{48,496},{56,120... | collective-permute-start | bytes 1474568 | tf_op jit(solution)/shard_map/ppermute | solution.py:199
  56.2 4.6 %collective-permute-start.7 = (bf16[640,384]{1,0:T(8,128)(2,1)}, bf16[640,384]{1,0:T(8,128)(2,1)}, u32[]{:S(2)}, u32[]{:S(2)}) collective-permute-start(bf16[640,384]{1,0:T(8,128)(2,1)} %collective-permute-done.6.refs_5_), channel_id=1, source_target_pairs={{0,64},{8,456},{16,80},{24,472},{32,96},{40,488},{48,112},{56,504}... | collective-permute-start | bytes 1474568 | tf_op jit(solution)/shard_map/ppermute | solution.py:199
  60.9 2.5 %collective-permute-start.4 = (bf16[16,88,256]{2,1,0:T(8,128)(2,1)S(1)}, bf16[16,88,256]{2,1,0:T(8,128)(2,1)S(1)}, u32[]{:S(2)}, u32[]{:S(2)}) collective-permute-start(bf16[16,88,256]{2,1,0:T(8,128)(2,1)S(1)} %all-to-all-done.1.refs_0_), channel_id=1, source_target_pairs={{0,48},{8,24},{16,0},{24,40},{32,16},{40,56},{48,32},{56,8},{64,11... | collective-permute-start | bytes 2162696 | tf_op jit(solution)/shard_map/ppermute | solution.py:199
  63.6 4.6 %collective-permute-done.7.refs_7_ = bf16[640,384]{1,0:T(8,128)(2,1)} collective-permute-done((bf16[640,384]{1,0:T(8,128)(2,1)}, bf16[640,384]{1,0:T(8,128)(2,1)}, u32[]{:S(2)}, u32[]{:S(2)}) %collective-permute-start.7) | collective-permute-done | bytes 491552 | tf_op jit(solution)/shard_map/ppermute | solution.py:199
  68.1 4.1 %collective-permute-start.8 = (bf16[640,384]{1,0:T(8,128)(2,1)}, bf16[640,384]{1,0:T(8,128)(2,1)S(1)}, u32[]{:S(2)}, u32[]{:S(2)}) collective-permute-start(bf16[640,384]{1,0:T(8,128)(2,1)} %collective-permute-done.7.refs_7_), channel_id=1, source_target_pairs={{0,64},{8,456},{16,80},{24,472},{32,96},{40,488},{48,112},{56,504}... | collective-permute-start | bytes 1474568 | tf_op jit(solution)/shard_map/ppermute | solution.py:199
  74.2 4.5 %collective-permute-start.5 = (bf16[16,88,256]{2,1,0:T(8,128)(2,1)}, bf16[16,88,256]{2,1,0:T(8,128)(2,1)S(1)}, u32[]{:S(2)}, u32[]{:S(2)}) collective-permute-start(bf16[16,88,256]{2,1,0:T(8,128)(2,1)} %collective-permute-done.2.refs_1_), channel_id=1, source_target_pairs={{0,16},{8,56},{16,32},{24,8},{32,48},{40,24},{48,0},{56,40},{64,80... | collective-permute-start | bytes 2162696 | tf_op jit(solution)/shard_map/ppermute | solution.py:199
  78.9 4.6 %collective-permute-start.10 = (bf16[640,384]{1,0:T(8,128)(2,1)S(1)}, bf16[640,384]{1,0:T(8,128)(2,1)S(1)}, u32[]{:S(2)}, u32[]{:S(2)}) collective-permute-start(bf16[640,384]{1,0:T(8,128)(2,1)S(1)} %collective-permute-done.8.refs_9_), channel_id=1, source_target_pairs={{0,64},{8,456},{16,80},{24,472},{32,96},{40,488},{48,112},{56,504}... | collective-permute-start | bytes 1474568 | tf_op jit(solution)/shard_map/ppermute | solution.py:199
  83.5 4.8 %collective-permute-done.3.refs_8_ = bf16[640,384]{1,0:T(8,128)(2,1)S(1)} collective-permute-done((bf16[640,384]{1,0:T(8,128)(2,1)}, bf16[640,384]{1,0:T(8,128)(2,1)S(1)}, u32[]{:S(2)}, u32[]{:S(2)}) %collective-permute-start.3) | collective-permute-done | bytes 491552 | tf_op jit(solution)/shard_map/ppermute | solution.py:199
  91.6 12.7 %collective-permute-done.9.refs_10_ = bf16[640,384]{1,0:T(8,128)(2,1)S(1)} collective-permute-done((bf16[640,384]{1,0:T(8,128)(2,1)S(1)}, bf16[640,384]{1,0:T(8,128)(2,1)S(1)}, u32[]{:S(2)}, u32[]{:S(2)}) %collective-permute-start.9) | collective-permute-done | bytes 491552 | tf_op jit(solution)/shard_map/ppermute | solution.py:199
  104.2 7.4 %shard_map.104 = (bf16[256,640]{1,0:T(8,128)(2,1)S(1)}, bf16[256,640]{1,0:T(8,128)(2,1)S(1)}, f32[64,8,256]{2,1,0:T(8,128)S(1)}) custom-call(s32[3]{0:T(128)S(1)} %pad_add_fusion.place_ref, bf16[256,5120]{1,0:T(8,128)(2,1)S(1)} %bitcast.38, bf16[256,5120]{1,0:T(8,128)(2,1)} %collective-permute-done.other_ref, f32[512,128]{1,0:T(8,128)S(1)} %get-tuple-element.37.cos_ref, ...), custom_call_target="tpu_custom_call" | custom-call | flops 3355443200 | bytes 11796480 | tf_op jit(solution)/shard_map/pallas_call | solution.py:87
  111.7 2.7 %collective-permute-start.11 = (bf16[256,640]{1,0:T(8,128)(2,1)S(1)}, bf16[256,640]{1,0:T(8,128)(2,1)S(1)}, u32[]{:S(2)}, u32[]{:S(2)}) collective-permute-start(bf16[256,640]{1,0:T(8,128)(2,1)S(1)} %get-tuple-element.18), channel_id=1, source_target_pairs={{0,8},{8,0},{1,9},{9,1},{2,10},{10,2},{3,11},{11,3},{4,12},{12,4},... | collective-permute-start | bytes 983048 | tf_op jit(solution)/shard_map/ppermute | solution.py:34
  118.3 14.9 %all_to_all.25.parts_ref = bf16[64,8,128]{2,1,0:T(8,128)(2,1)S(1)} all-to-all(bf16[64,8,128]{2,1,0:T(8,128)(2,1)S(1)} %shard_map.105), channel_id=1, replica_groups=mesh['z'=8,'x'=4,'core'=2,'tp'=8] {'z','x','core'}, dimensions={0} | all-to-all | bytes 262144 | tf_op jit(solution)/shard_map/all_to_all | solution.py:203
  134.4 4.6 %all-to-all-start.3 = ((bf16[64,8,128]{2,1,0:T(8,128)(2,1)}), bf16[64,8,128]{2,1,0:T(8,128)(2,1)S(1)}, u32[]{:S(2)}, u32[]{:S(2)}) async-start(bf16[64,8,128]{2,1,0:T(8,128)(2,1)} %shard_map.106), calls=%async_computation.3 | async-start | bytes 262144 | tf_op jit(solution)/shard_map/all_to_all | solution.py:203
  141.1 9.3 %all-to-all-done.3 = bf16[64,8,128]{2,1,0:T(8,128)(2,1)S(1)} async-done(((bf16[64,8,128]{2,1,0:T(8,128)(2,1)}), bf16[64,8,128]{2,1,0:T(8,128)(2,1)S(1)}, u32[]{:S(2)}, u32[]{:S(2)}) %all-to-all-start.3) | async-done | bytes 131104 | tf_op jit(solution)/shard_map/all_to_all | solution.py:203
  151.3 6.8 %all-to-all-start.4 = ((f32[8,8,80]{2,1,0:T(8,128)}), f32[8,8,80]{2,1,0:T(8,128)S(1)}, u32[]{:S(2)}, u32[]{:S(2)}) async-start(f32[8,8,80]{2,1,0:T(8,128)} %fusion.5), calls=%async_computation.4 | async-start | bytes 65536 | tf_op jit(solution)/shard_map/all_to_all | solution.py:203
  158.1 2.3 %pad_maximum_fusion = bf16[2,128,2,640]{3,2,1,0:T(2,128)(2,1)} fusion(bf16[2,128,1,640]{3,2,1,0:T(2,128)(2,1)S(1)} %copy.32, bf16[2,128,1,640]{3,2,1,0:T(2,128)(2,1)S(1)} %copy.31), kind=kLoop, calls=%fused_computation.5 | loop fusion | flops 1310720 | bytes 1310720 | tf_op jit(solution)/shard_map/stack | solution.py:283
  160.4 4.6 %all-to-all-done.4 = f32[8,8,80]{2,1,0:T(8,128)S(1)} async-done(((f32[8,8,80]{2,1,0:T(8,128)}), f32[8,8,80]{2,1,0:T(8,128)S(1)}, u32[]{:S(2)}, u32[]{:S(2)}) %all-to-all-start.4) | async-done | bytes 20512 | tf_op jit(solution)/shard_map/all_to_all | solution.py:203
  (70 shorter events, 20.2 us)
Async XLA Ops:
  0.6 149.9 %copy-start = (bf16[640,80]{0,1:T(8,128)(2,1)S(1)}, bf16[640,80]{0,1:T(8,128)(2,1)}, u32[]{:S(2)}) copy-start(bf16[640,80]{0,1:T(8,128)(2,1)} %param.14) | copy-start | bytes 307204
  0.6 13.2 %copy-start.6 = (bf16[80,2,640]{2,1,0:T(2,128)(2,1)S(1)}, bf16[80,2,640]{2,1,0:T(2,128)(2,1)}, u32[]{:S(2)}) copy-start(bf16[80,2,640]{2,1,0:T(2,128)(2,1)} %param.13) | copy-start | bytes 614404
  0.7 14.0 %copy-start.8 = (s32[2]{0:T(128)S(1)}, s32[2]{0:T(128)}, u32[]{:S(2)}) copy-start(s32[2]{0:T(128)} %param.10) | copy-start | bytes 28
  0.7 14.0 %copy-start.7 = (bf16[5120]{0:T(1024)(128)(2,1)S(1)}, bf16[5120]{0:T(1024)(128)(2,1)}, u32[]{:S(2)}) copy-start(bf16[5120]{0:T(1024)(128)(2,1)} %param.12) | copy-start | bytes 30724
  0.7 14.0 %copy-start.2 = (bf16[1,640]{1,0:T(2,128)(2,1)S(1)}, bf16[1,640]{1,0:T(2,128)(2,1)}, u32[]{:S(2)}) copy-start(bf16[1,640]{1,0:T(2,128)(2,1)} %query_ref.1) | copy-start | bytes 3844
  2.0 28.2 %copy-start.4 = (bf16[2,128,5120]{2,1,0:T(8,128)(2,1)S(1)}, bf16[2,128,5120]{2,1,0:T(8,128)(2,1)}, u32[]{:S(2)}) copy-start(bf16[2,128,5120]{2,1,0:T(8,128)(2,1)} %param.9) | copy-start | bytes 7864324
  2.8 20.3 %all-to-all-start = ((bf16[8,80,384]{2,1,0:T(8,128)(2,1)}), bf16[8,80,384]{2,1,0:T(8,128)(2,1)}, u32[]{:S(2)}, u32[]{:S(2)}) async-start(bf16[8,80,384]{2,1,0:T(8,128)(2,1)} %bitcast.5), calls=%async_computation | async-start | bytes 983040 | tf_op jit(solution)/shard_map/all_to_all | solution.py:203
  24.0 27.4 %all-to-all-start.1 = ((bf16[16,88,256]{2,1,0:T(8,128)(2,1)}), bf16[16,88,256]{2,1,0:T(8,128)(2,1)S(1)}, u32[]{:S(2)}, u32[]{:S(2)}) async-start(bf16[16,88,256]{2,1,0:T(8,128)(2,1)} %bitcast.40), calls=%async_computation.1 | async-start | bytes 1441792 | tf_op jit(solution)/shard_map/all_to_all | solution.py:203
  31.8 46.9 %copy-start.9 = (s32[4]{0:T(128)S(1)}, s32[4]{0:T(128)}, u32[]{:S(2)}) copy-start(s32[4]{0:T(128)} %param.11) | copy-start | bytes 52
  32.6 59.0 %collective-permute-start = (bf16[256,5120]{1,0:T(8,128)(2,1)S(1)}, bf16[256,5120]{1,0:T(8,128)(2,1)}, u32[]{:S(2)}, u32[]{:S(2)}) collective-permute-start(bf16[256,5120]{1,0:T(8,128)(2,1)S(1)} %bitcast.37), channel_id=1, source_target_pairs={{0,8},{8,0},{1,9},{9,1},{2,10},{10,2},{3,11},{11,3},{4,12},{12,4},... | collective-permute-start | bytes 7864328 | tf_op jit(solution)/shard_map/ppermute | solution.py:34
  34.6 21.5 %collective-permute-start.6 = (bf16[640,384]{1,0:T(8,128)(2,1)}, bf16[640,384]{1,0:T(8,128)(2,1)}, u32[]{:S(2)}, u32[]{:S(2)}) collective-permute-start(bf16[640,384]{1,0:T(8,128)(2,1)} %bitcast.6.refs_4_), channel_id=1, source_target_pairs={{0,64},{8,456},{16,80},{24,472},{32,96},{40,488},{48,112},{56,504}... | collective-permute-start | bytes 1474568 | tf_op jit(solution)/shard_map/ppermute | solution.py:199
  51.4 20.8 %collective-permute-start.2 = (bf16[16,88,256]{2,1,0:T(8,128)(2,1)S(1)}, bf16[16,88,256]{2,1,0:T(8,128)(2,1)}, u32[]{:S(2)}, u32[]{:S(2)}) collective-permute-start(bf16[16,88,256]{2,1,0:T(8,128)(2,1)S(1)} %all-to-all-done.1.refs_0_), channel_id=1, source_target_pairs={{0,16},{8,56},{16,32},{24,8},{32,48},{40,24},{48,0},{56,40},{64,80... | collective-permute-start | bytes 2162696 | tf_op jit(solution)/shard_map/ppermute | solution.py:199
  54.2 18.0 %collective-permute-start.1 = (bf16[640,384]{1,0:T(8,128)(2,1)}, bf16[640,384]{1,0:T(8,128)(2,1)}, u32[]{:S(2)}, u32[]{:S(2)}) collective-permute-start(bf16[640,384]{1,0:T(8,128)(2,1)} %bitcast.6.refs_4_), channel_id=1, source_target_pairs={{0,448},{8,72},{16,464},{24,88},{32,480},{40,104},{48,496},{56,120... | collective-permute-start | bytes 1474568 | tf_op jit(solution)/shard_map/ppermute | solution.py:199
  56.2 12.0 %collective-permute-start.7 = (bf16[640,384]{1,0:T(8,128)(2,1)}, bf16[640,384]{1,0:T(8,128)(2,1)}, u32[]{:S(2)}, u32[]{:S(2)}) collective-permute-start(bf16[640,384]{1,0:T(8,128)(2,1)} %collective-permute-done.6.refs_5_), channel_id=1, source_target_pairs={{0,64},{8,456},{16,80},{24,472},{32,96},{40,488},{48,112},{56,504}... | collective-permute-start | bytes 1474568 | tf_op jit(solution)/shard_map/ppermute | solution.py:199
  60.9 22.6 %collective-permute-start.4 = (bf16[16,88,256]{2,1,0:T(8,128)(2,1)S(1)}, bf16[16,88,256]{2,1,0:T(8,128)(2,1)S(1)}, u32[]{:S(2)}, u32[]{:S(2)}) collective-permute-start(bf16[16,88,256]{2,1,0:T(8,128)(2,1)S(1)} %all-to-all-done.1.refs_0_), channel_id=1, source_target_pairs={{0,48},{8,24},{16,0},{24,40},{32,16},{40,56},{48,32},{56,8},{64,11... | collective-permute-start | bytes 2162696 | tf_op jit(solution)/shard_map/ppermute | solution.py:199
  68.1 10.8 %collective-permute-start.8 = (bf16[640,384]{1,0:T(8,128)(2,1)}, bf16[640,384]{1,0:T(8,128)(2,1)S(1)}, u32[]{:S(2)}, u32[]{:S(2)}) collective-permute-start(bf16[640,384]{1,0:T(8,128)(2,1)} %collective-permute-done.7.refs_7_), channel_id=1, source_target_pairs={{0,64},{8,456},{16,80},{24,472},{32,96},{40,488},{48,112},{56,504}... | collective-permute-start | bytes 1474568 | tf_op jit(solution)/shard_map/ppermute | solution.py:199
  72.2 16.1 %collective-permute-start.3 = (bf16[640,384]{1,0:T(8,128)(2,1)}, bf16[640,384]{1,0:T(8,128)(2,1)S(1)}, u32[]{:S(2)}, u32[]{:S(2)}) collective-permute-start(bf16[640,384]{1,0:T(8,128)(2,1)} %collective-permute-done.1.refs_6_), channel_id=1, source_target_pairs={{0,448},{8,72},{16,464},{24,88},{32,480},{40,104},{48,496},{56,120... | collective-permute-start | bytes 1474568 | tf_op jit(solution)/shard_map/ppermute | solution.py:199
  74.2 17.4 %collective-permute-start.5 = (bf16[16,88,256]{2,1,0:T(8,128)(2,1)}, bf16[16,88,256]{2,1,0:T(8,128)(2,1)S(1)}, u32[]{:S(2)}, u32[]{:S(2)}) collective-permute-start(bf16[16,88,256]{2,1,0:T(8,128)(2,1)} %collective-permute-done.2.refs_1_), channel_id=1, source_target_pairs={{0,16},{8,56},{16,32},{24,8},{32,48},{40,24},{48,0},{56,40},{64,80... | collective-permute-start | bytes 2162696 | tf_op jit(solution)/shard_map/ppermute | solution.py:199
  78.9 12.7 %collective-permute-start.10 = (bf16[640,384]{1,0:T(8,128)(2,1)S(1)}, bf16[640,384]{1,0:T(8,128)(2,1)S(1)}, u32[]{:S(2)}, u32[]{:S(2)}) collective-permute-start(bf16[640,384]{1,0:T(8,128)(2,1)S(1)} %collective-permute-done.8.refs_9_), channel_id=1, source_target_pairs={{0,64},{8,456},{16,80},{24,472},{32,96},{40,488},{48,112},{56,504}... | collective-permute-start | bytes 1474568 | tf_op jit(solution)/shard_map/ppermute | solution.py:199
  88.3 16.0 %collective-permute-start.9 = (bf16[640,384]{1,0:T(8,128)(2,1)S(1)}, bf16[640,384]{1,0:T(8,128)(2,1)S(1)}, u32[]{:S(2)}, u32[]{:S(2)}) collective-permute-start(bf16[640,384]{1,0:T(8,128)(2,1)S(1)} %collective-permute-done.3.refs_8_), channel_id=1, source_target_pairs={{0,448},{8,72},{16,464},{24,88},{32,480},{40,104},{48,496},{56,120... | collective-permute-start | bytes 1474568 | tf_op jit(solution)/shard_map/ppermute | solution.py:199
  104.2 29.0 %copy-start.3 = (bf16[1,2,640]{2,1,0:T(2,128)(2,1)S(1)}, bf16[1,2,640]{2,1,0:T(2,128)(2,1)}, u32[]{:S(2)}) copy-start(bf16[1,2,640]{2,1,0:T(2,128)(2,1)} %param.16) | copy-start | bytes 7684
  111.7 4.0 %collective-permute-start.11 = (bf16[256,640]{1,0:T(8,128)(2,1)S(1)}, bf16[256,640]{1,0:T(8,128)(2,1)S(1)}, u32[]{:S(2)}, u32[]{:S(2)}) collective-permute-start(bf16[256,640]{1,0:T(8,128)(2,1)S(1)} %get-tuple-element.18), channel_id=1, source_target_pairs={{0,8},{8,0},{1,9},{9,1},{2,10},{10,2},{3,11},{11,3},{4,12},{12,4},... | collective-permute-start | bytes 983048 | tf_op jit(solution)/shard_map/ppermute | solution.py:34
  134.4 16.0 %all-to-all-start.3 = ((bf16[64,8,128]{2,1,0:T(8,128)(2,1)}), bf16[64,8,128]{2,1,0:T(8,128)(2,1)S(1)}, u32[]{:S(2)}, u32[]{:S(2)}) async-start(bf16[64,8,128]{2,1,0:T(8,128)(2,1)} %shard_map.106), calls=%async_computation.3 | async-start | bytes 262144 | tf_op jit(solution)/shard_map/all_to_all | solution.py:203
  151.3 13.8 %all-to-all-start.4 = ((f32[8,8,80]{2,1,0:T(8,128)}), f32[8,8,80]{2,1,0:T(8,128)S(1)}, u32[]{:S(2)}, u32[]{:S(2)}) async-start(f32[8,8,80]{2,1,0:T(8,128)} %fusion.5), calls=%async_computation.4 | async-start | bytes 65536 | tf_op jit(solution)/shard_map/all_to_all | solution.py:203
  (2 other events, 2.5 us)
